TPU v7x, 32 devices: a whole 2x2x4 slice. The times are simulated.
32 devices in a mesh: dp: 4 (over y, x), tensor: 8 (over z, core).
Axes of the slice: x: 2, y: 2, z: 4, core: 2. Of those that a mesh axis runs over, the one named last changes fastest.
Arguments:
- drafted: bfloat16 [512, 8, 4096], P('dp', None, 'tensor'), may hold values from -6 to 6
- norm_gain: float32 [4096], replicated, may hold values from 0.25 to 1.75
- w_in: bfloat16 [4096, 3, 4096], P(None, None, 'tensor'), may hold values from -0.09375 to 0.09375
- conv_taps: float32 [3, 3, 4096], P(None, None, 'tensor'), may hold values from -2 to 2
- decay: float32 [4096], P('tensor'), may hold values from 0.2 to 0.98
- w_out: bfloat16 [4096, 4096], P('tensor'), may hold values from -0.09375 to 0.09375
- queue_tails: bfloat16 [512, 2, 3, 4096], P('dp', None, None, 'tensor'), may hold values from -6 to 6
- states: float32 [512, 4096], P('dp', 'tensor'), may hold values from -6 to 6
- accepted: int32 [512], P('dp'), may hold values from 0 to 8
- owner_map: int32 [512], P('dp'), may hold values from 0 to 511, as said below
Outputs:
- mixed: bfloat16 [512, 8, 4096], P(('dp', 'tensor'))
- new_tails: bfloat16 [512, 2, 3, 4096], P('dp', None, None, 'tensor')
- new_states: float32 [512, 4096], P('dp', 'tensor')
Inputs may be any that keep to these rules, and one draw needn't show every extreme that they name: owner_map names every row once; the rows of each index of dp go 32 to each index of dp, that is to each block of 128 rows.
All inputs are finite; a program needn't handle non-finite values.
Results may differ from a plain program's by a relative error of at most 0.008.
Values may be sent and summed in bfloat16 or wider, within the bound.
No kernel may reach another device: no remote copies, remote signals or barrier semaphores. Data moves between devices by JAX's collectives and lax.ppermute only.
A program may use at most 128 MiB of HBM per device.

v0:
```python
import jax
import jax.numpy as jnp
from jax import lax
from jax.sharding import PartitionSpec as P


def per_device(
    drafted, norm_gain, w_in, conv_taps, decay, w_out, queue_tails, states, accepted, owner_map
):
    rows, steps, local = drafted.shape
    tail_len = queue_tails.shape[1]
    full = lax.all_gather(drafted, "tensor", axis=2, tiled=True)
    width = full.shape[2]
    wide_in = full.astype(jnp.float32)
    meansq = jnp.mean(wide_in * wide_in, axis=-1, keepdims=True)
    normed = (wide_in * lax.rsqrt(meansq + 1e-05) * norm_gain).astype(jnp.bfloat16)
    branches = jnp.dot(
        normed.reshape(rows * steps, width),
        w_in.reshape(width, 3 * local),
        preferred_element_type=jnp.float32,
    )
    branches = branches.astype(jnp.bfloat16).reshape(rows, steps, 3, local)
    window = jnp.concatenate([queue_tails, branches], axis=1)
    wide = window.astype(jnp.float32)
    filtered = jnp.zeros((rows, steps, 3, local), jnp.float32)
    for tap in range(conv_taps.shape[0]):
        filtered = filtered + conv_taps[tap] * wide[:, tail_len - tap : tail_len - tap + steps]
    state = states
    history = [states]
    outputs = []
    for step in range(steps):
        state = decay * state + filtered[:, step, 1] * filtered[:, step, 2]
        history.append(state)
        outputs.append(filtered[:, step, 0] * state)
    gated = jnp.stack(outputs, axis=1).astype(jnp.bfloat16)
    stacked = jnp.stack(history, axis=1)
    share = rows // lax.axis_size("tensor")
    term = lax.psum_scatter(
        jnp.dot(
            gated.reshape(share * lax.axis_size("tensor") * steps, local),
            w_out,
            preferred_element_type=jnp.float32,
        ).reshape(share * lax.axis_size("tensor"), steps * width),
        "tensor",
        scatter_dimension=0,
        tiled=True,
    )
    own = lax.dynamic_slice_in_dim(wide_in, lax.axis_index("tensor") * share, share, 0)
    mixed = (own + term.reshape(share, steps, width)).astype(jnp.bfloat16)
    order = jnp.argsort(owner_map // rows, stable=True)
    slots = owner_map % rows
    offsets = jnp.arange(tail_len, dtype=jnp.int32)[None, :]
    index = accepted[:, None] + offsets
    chosen = jnp.take_along_axis(window, index[:, :, None, None], axis=1)
    kept = jnp.take_along_axis(stacked, accepted[:, None, None], axis=1)[:, 0]
    got_tails = lax.all_to_all(chosen[order], "dp", split_axis=0, concat_axis=0, tiled=True)
    got_states, got_slots = (
        lax.all_to_all(kept[order], "dp", split_axis=0, concat_axis=0, tiled=True),
        lax.all_to_all(slots[order], "dp", split_axis=0, concat_axis=0, tiled=True),
    )
    placing = jnp.argsort(got_slots)
    return (mixed, got_tails[placing], got_states[placing])


def solution(mesh):
    return jax.shard_map(
        per_device,
        mesh=mesh,
        in_specs=(
            P("dp", None, "tensor"),
            P(),
            P(None, None, "tensor"),
            P(None, None, "tensor"),
            P("tensor"),
            P("tensor", None),
            P("dp", None, None, "tensor"),
            P("dp", "tensor"),
            P("dp"),
            P("dp"),
        ),
        out_specs=(
            P(("dp", "tensor"), None, None),
            P("dp", None, None, "tensor"),
            P("dp", "tensor"),
        ),
        check_vma=False,
    )
```

profile of v0, /device:TPU:0, one launch (start us, length us, event | category | flops | bytes accessed | tf_op | source)
XLA Modules:
  0.0 346.4 jit_solution(11455813081337332198)
XLA Ops:
  7.2 0.7 all-gather.2.cloned.1.call-update
  8.0 17.0 %copy.127 = bf16[4096,3,512]{0,2,1:T(8,128)(2,1)} copy(bf16[4096,3,512]{2,0,1:T(8,128)(2,1)} %param.12) | data formatting | bytes 25165824 | tf_op args[2]
  25.0 0.7 bitcast_dynamic-update-slice_fusion.8
  25.8 68.6 %all-gather.2.cloned.1.call-done = bf16[128,8,4096]{2,1,0:T(8,128)(2,1)} async-done(((bf16[128,8,512]{2,1,0:T(8,128)(2,1)}), bf16[128,8,4096]{2,1,0:T(8,128)(2,1)}) %all-gather.2.cloned.1.call-update) | async-done | bytes 8388624 | tf_op jit(solution)/shard_map/all_gather | solution.py:12
  94.4 5.1 %multiply_reduce_fusion = f32[128,8]{1,0:T(8,128)S(1)} fusion(bf16[128,8,4096]{2,1,0:T(8,128)(2,1)} %all-gather.2.cloned.1.call-done), kind=kLoop, calls=%fused_computation.8 | loop fusion | flops 12581888 | bytes 8392704 | tf_op jit(solution)/shard_map/reduce_sum | solution.py:15
  99.5 0.1 copy.126
  99.7 18.4 %fusion.8 = bf16[1024,1536]{1,0:T(8,128)(2,1)S(1)} fusion(bf16[4096,1536]{0,1:T(8,128)(2,1)} %bitcast.208, f32[4096]{0:T(1024)S(1)} %copy-done.9, f32[128,8]{1,0:T(8,128)S(1)} %copy.126, bf16[128,8,4096]{2,1,0:T(8,128)(2,1)} %all-gather.2.cloned.1.call-done), kind=kOutput, calls=%fused_computation.20 | convolution fusion | flops 12903251968 | bytes 24137728 | tf_op jit(solution)/shard_map/dot_general | solution.py:17
  118.1 4.7 %pad_maximum_fusion = (bf16[128,10,3,512]{3,1,2,0:T(8,128)(2,1)}, f32[128,10,3,512]{3,1,2,0:T(8,128)S(1)}) fusion(bf16[128,8,3,512]{3,1,2,0:T(8,128)(2,1)S(1)} %bitcast.210, bf16[128,2,3,512]{3,1,2,0:T(2,128)(2,1)S(1)} %copy-done.4), kind=kLoop, calls=%fused_computation.19 | loop fusion | flops 9830400 | bytes 15728640 | tf_op jit(solution)/shard_map/concatenate | solution.py:23
  122.8 1.9 fusion.6
  124.7 1.5 fusion.73
  126.2 4.8 %slice_multiply_fusion.3 = (f32[128,1,1,512]{3,1,2,0:T(1,128)S(1)}, f32[128,1,1,512]{3,1,2,0:T(1,128)S(1)}, f32[128,1,1,512]{3,1,2,0:T(1,128)S(1)}, f32[128,1,1,...) fusion(f32[128,8,3,512]{3,1,2,0:T(8,128)S(1)} %fusion.6), kind=kLoop, calls=%fused_computation.27 | loop fusion | flops 65536 | bytes 9699328 | tf_op jit(solution)/shard_map/mul | solution.py:32
  131.0 0.8 bitcast_dynamic-update-slice_fusion.7
  131.8 1.0 fusion.46
  132.8 0.8 bitcast_dynamic-update-slice_fusion.6
  133.6 1.5 fusion.48
  135.0 0.8 bitcast_dynamic-update-slice_fusion.5
  135.8 1.0 fusion.50
  136.8 0.8 bitcast_dynamic-update-slice_fusion.4
  137.6 0.8 bitcast_dynamic-update-slice_fusion.3
  138.4 0.8 bitcast_dynamic-update-slice_fusion.2
  139.2 0.8 bitcast_dynamic-update-slice_fusion.1
  140.1 8.5 %fusion.12 = f32[1024,4096]{1,0:T(8,128)} fusion(bf16[512,4096]{1,0:T(8,128)(2,1)S(1)} %copy-done.8, bf16[128,8,512]{2,0,1:T(8,128)(2,1)S(1)} %fusion.60), kind=kOutput, calls=%fused_computation.24 | convolution fusion | flops 4294967296 | bytes 22020096 | tf_op jit(solution)/shard_map/dot_general | solution.py:39
  148.6 18.2 %reshape.138 = f32[128,32768]{1,0:T(8,128)} reshape(f32[1024,4096]{1,0:T(8,128)} %fusion.12) | data formatting | bytes 33554432 | tf_op jit(solution)/shard_map/reshape | solution.py:43
  166.9 0.6 copy-done.10
  167.5 2.5 sort.34
  170.1 1.2 gather_fusion.1
  171.3 0.7 all_to_all.20
  172.0 3.6 %all-to-all-start.1 = ((s32[4,32,1]{1,2,0:T(1,128)}), s32[4,32,1]{1,2,0:T(1,128)S(1)}, u32[]{:S(2)}, u32[]{:S(2)}) async-start(s32[4,32,1]{1,2,0:T(1,128)} %bitcast.31), calls=%async_computation.2 | async-start | bytes 4096 | tf_op jit(solution)/shard_map/all_to_all | solution.py:59
  175.7 0.1 reshape.180
  175.9 0.1 copy.151
  176.1 1.3 gather_fusion.6
  177.5 1.5 gather_fusion.3
  179.0 13.0 %copy.152 = bf16[128,10,3,512]{3,2,1,0:T(4,128)(2,1)} copy(bf16[128,10,3,512]{3,1,2,0:T(8,128)(2,1)} %get-tuple-element.44) | data formatting | bytes 7864320 | tf_op jit(solution)/shard_map/concatenate | solution.py:23
  192.0 4.5 %gather_fusion.5 = bf16[256,3,512]{2,1,0:T(4,128)(2,1)S(1)} fusion(bf16[128,10,3,512]{3,2,1,0:T(4,128)(2,1)} %copy.152, s32[256]{0:T(256)S(1)} %reshape.180), kind=kCustom, calls=%fused_computation.5 | custom fusion | bytes 1574912 | tf_op jit(solution)/shard_map/jit(take_along_axis)/gather | solution.py:54
  196.5 4.2 %all-to-all-start.2 = ((f32[4,32,512]{2,1,0:T(8,128)}), f32[4,32,512]{2,1,0:T(8,128)S(1)}, u32[]{:S(2)}, u32[]{:S(2)}) async-start(f32[4,32,512]{2,1,0:T(8,128)} %bitcast.44), calls=%async_computation.3 | async-start | bytes 524288 | tf_op jit(solution)/shard_map/all_to_all | solution.py:58
  200.7 0.9 broadcast_select_fusion
  201.6 3.0 gather_fusion
  204.6 1.4 all-to-all-done.2
  206.0 3.5 %all-to-all-start = ((bf16[128,2,3,512]{3,1,2,0:T(2,128)(2,1)}), bf16[128,2,3,512]{3,1,2,0:T(2,128)(2,1)S(1)}, u32[]{:S(2)}, u32[]{:S(2)}) async-start(bf16[128,2,3,512]{3,1,2,0:T(2,128)(2,1)} %gather_fusion), calls=%async_computation.1 | async-start | bytes 1572864 | tf_op jit(solution)/shard_map/all_to_all | solution.py:56
  209.5 0.5 broadcast.179
  210.1 0.7 reduce.3
  210.8 2.5 sort.35
  213.4 11.5 %convert_element_type.20 = f32[128,8,4096]{2,1,0:T(8,128)} convert(bf16[128,8,4096]{2,1,0:T(8,128)(2,1)} %all-gather.2.cloned.1.call-done) | non-fusion elementwise | flops 4194304 | bytes 25165824 | tf_op jit(solution)/shard_map/convert_element_type | solution.py:14
  224.8 1.4 gather_fusion.4
  226.3 3.0 gather_fusion.2
  229.3 104.5 %reduce-scatter.2.cloned.1.call-done = f32[16,32768]{1,0:T(8,128)} async-done(((f32[128,32768]{1,0:T(8,128)}), f32[16,32768]{1,0:T(8,128)}) %reduce-scatter.2.cloned.1.call-update) | async-done | bytes 2097168 | tf_op jit(solution)/shard_map/reduce_scatter | solution.py:38
  333.8 2.8 copy.178
  336.6 2.9 fusion.11
  (51 shorter events, 0.8 us)
Async XLA Ops:
  7.2 87.2 %all-gather.2.cloned.1.call-start = ((), (), s32[]{:S(2)}) async-start(), calls=%async_computation.4 | async-start | bytes 9437184 | tf_op jit(solution)/shard_map/all_gather | solution.py:12
  7.9 17.1 %copy-start.6 = (f32[3,3,512]{2,1,0:T(4,128)S(1)}, f32[3,3,512]{2,1,0:T(4,128)}, u32[]{:S(2)}) copy-start(f32[3,3,512]{2,1,0:T(4,128)} %param.13) | copy-start | bytes 55300
  7.9 17.1 %copy-start.1 = (f32[128,512]{1,0:T(8,128)S(1)}, f32[128,512]{1,0:T(8,128)}, u32[]{:S(2)}) copy-start(f32[128,512]{1,0:T(8,128)} %param.17) | copy-start | bytes 786436
  7.9 325.9 %reduce-scatter.2.cloned.1.call-start = ((), (), s32[]{:S(2)}) async-start(), calls=%async_computation.5 | async-start | bytes 18874368 | tf_op jit(solution)/shard_map/reduce_scatter | solution.py:38
  25.0 74.7 %copy-start.9 = (f32[4096]{0:T(1024)S(1)}, f32[4096]{0:T(1024)}, u32[]{:S(2)}) copy-start(f32[4096]{0:T(1024)} %param.11) | copy-start | bytes 49156
  99.7 18.4 %copy-start.4 = (bf16[128,2,3,512]{3,1,2,0:T(2,128)(2,1)S(1)}, bf16[128,2,3,512]{3,1,2,0:T(2,128)(2,1)}, u32[]{:S(2)}) copy-start(bf16[128,2,3,512]{3,1,2,0:T(2,128)(2,1)} %param.16) | copy-start | bytes 2359300
  124.7 6.3 %copy-start.5 = (f32[512]{0:T(512)S(1)}, f32[512]{0:T(512)}, u32[]{:S(2)}) copy-start(f32[512]{0:T(512)} %param.14) | copy-start | bytes 6148
  131.0 6.6 %copy-start.3 = (f32[128,1,1,512]{3,1,2,0:T(1,128)S(1)}, f32[128,1,1,512]{3,1,2,0:T(1,128)}, u32[]{:S(2)}) copy-start(f32[128,1,1,512]{3,1,2,0:T(1,128)} %get-tuple-element.32) | copy-start | bytes 786436
  131.0 7.4 %copy-start.2 = (f32[128,1,1,512]{3,1,2,0:T(1,128)S(1)}, f32[128,1,1,512]{3,1,2,0:T(1,128)}, u32[]{:S(2)}) copy-start(f32[128,1,1,512]{3,1,2,0:T(1,128)} %get-tuple-element.29) | copy-start | bytes 786436
  132.8 7.4 %copy-start.8 = (bf16[512,4096]{1,0:T(8,128)(2,1)S(1)}, bf16[512,4096]{1,0:T(8,128)(2,1)}, u32[]{:S(2)}) copy-start(bf16[512,4096]{1,0:T(8,128)(2,1)} %param.15) | copy-start | bytes 12582916
  166.8 0.7 copy-start.10
  166.8 8.8 %copy-start.7 = (s32[128]{0:T(128)S(1)}, s32[128]{0:T(128)}, u32[]{:S(2)}) copy-start(s32[128]{0:T(128)} %param.18) | copy-start | bytes 1540
  166.8 9.2 %copy-start = (f32[128,9,512]{2,0,1:T(8,128)S(1)}, f32[128,9,512]{2,0,1:T(8,128)}, u32[]{:S(2)}) copy-start(f32[128,9,512]{2,0,1:T(8,128)} %get-tuple-element.7) | copy-start | bytes 7077892
  172.0 24.5 %all-to-all-start.1 = ((s32[4,32,1]{1,2,0:T(1,128)}), s32[4,32,1]{1,2,0:T(1,128)S(1)}, u32[]{:S(2)}, u32[]{:S(2)}) async-start(s32[4,32,1]{1,2,0:T(1,128)} %bitcast.31), calls=%async_computation.2 | async-start | bytes 4096 | tf_op jit(solution)/shard_map/all_to_all | solution.py:59
  196.5 9.5 %all-to-all-start.2 = ((f32[4,32,512]{2,1,0:T(8,128)}), f32[4,32,512]{2,1,0:T(8,128)S(1)}, u32[]{:S(2)}, u32[]{:S(2)}) async-start(f32[4,32,512]{2,1,0:T(8,128)} %bitcast.44), calls=%async_computation.3 | async-start | bytes 524288 | tf_op jit(solution)/shard_map/all_to_all | solution.py:58
  206.0 20.2 %all-to-all-start = ((bf16[128,2,3,512]{3,1,2,0:T(2,128)(2,1)}), bf16[128,2,3,512]{3,1,2,0:T(2,128)(2,1)S(1)}, u32[]{:S(2)}, u32[]{:S(2)}) async-start(bf16[128,2,3,512]{3,1,2,0:T(2,128)(2,1)} %gather_fusion), calls=%async_computation.1 | async-start | bytes 1572864 | tf_op jit(solution)/shard_map/all_to_all | solution.py:56
Sparse Core Ops, SparseCore 0:
  9.6 84.7 all-gather.1
  167.0 166.7 reduce-scatter.1
where the time goes:
time: 348 us; the launch traced here: 346 us
  waiting for transfers between devices  175 us (50%)
  local copies, waits for them, and re-layouts  71.6 us (21%)
  other arithmetic  46.8 us (13%)
  matrix products  26.9 us (8%)
  between operations  14.3 us (4%)
  starting transfers between devices  11.4 us (3%)
    reduce_scatter x1, waiting for transfers between devices, per_device(): lax.psum_scatter(jnp.dot(gated.reshape(share * lax.axis_size('tensor') *...  105 us
    all_gather x1, waiting for transfers between devices, per_device(): full = lax.all_gather(drafted, 'tensor', axis=2, tiled=True)  68.6 us
    unnamed x26, local copies, waits for them, and re-layouts  21.3 us
    dot_general x1, matrix products, per_device(): jnp.dot(normed.reshape(rows * steps, width), w_in.reshape(width, 3 * loca...  18.4 us
    reshape x1, local copies, waits for them, and re-layouts, per_device(): term = lax.psum_scatter(jnp.dot(gated.reshape(share * lax.axis_size('tens...  18.2 us
    concatenate x1, local copies, waits for them, and re-layouts, per_device(): window = jnp.concatenate([queue_tails, branches], axis=1)  13 us
    convert_element_type x1, other arithmetic, per_device(): wide_in = full.astype(jnp.float32)  11.5 us
    unnamed x14, other arithmetic  9.02 us
  transfers between devices with their start and end apart: 5, of which 3 were waited for; matrix products, arithmetic and copies ran while one was open for 19% of the time, Pallas kernels for 0%

commit v1 on v0

v1 whole, which is shorter than its diff:
```python
import functools
import jax
import jax.numpy as jnp
from jax import lax
from jax.experimental import pallas as pl
from jax.experimental.pallas import tpu as pltpu
from jax.sharding import PartitionSpec as P


AHEAD = 4
COST = 40


def chunk_kernel(
    nz, choices, tail_len, taps_n, steps, rows, local, width, block, share_rows,
    meta, *refs
):
    n_in = sum(choices)
    pieces = [refs[sum(choices[:k]):sum(choices[:k + 1])] for k in range(nz)]
    (w_own, w_sib, o_own, o_sib, gain, taps, decay, tails, states, accepted) = refs[n_in:n_in + 10]
    outs = refs[n_in + 10:]
    terms = outs[:nz]
    commit = outs[nz]
    xs, ns, wbuf, wob, br, gf, gs, pf, xsem, wsem, osem = outs[nz + 1:]
    is_end, core = meta[0], meta[1]
    tokens = rows * steps
    unit = share_rows * steps

    def piece_copy(slot, half, ref):
        place = meta[2 + slot] * 2 + (core if half == 0 else 1 - core)
        at = pl.multiple_of(place * local, 128)
        return pltpu.make_async_copy(ref.at[half], xs.at[:, pl.ds(at, local)], xsem.at[slot, half])

    for slot in range(nz):
        for half in range(2):
            if choices[slot] == 1:
                piece_copy(slot, half, pieces[slot][0]).start()
            else:
                @pl.when(is_end == 0)
                def _(slot=slot, half=half):
                    piece_copy(slot, half, pieces[slot][0]).start()

                @pl.when(is_end == 1)
                def _(slot=slot, half=half):
                    piece_copy(slot, half, pieces[slot][1]).start()

    half_k, half_o = width // 2, local // 2
    stream = []
    for index in range(6):
        for part in range(2):
            at = pl.ds(part * half_k, half_k)
            src = (w_own, w_sib)[index // 3].at[index % 3, at]
            stream.append(pltpu.make_async_copy(src, wbuf.at[index, at], wsem.at[2 * index + part]))
    for index in range(2):
        for part in range(2):
            src = (o_own, o_sib)[index].at[pl.ds(part * half_o, half_o)]
            dst = wob.at[pl.ds(index * local + part * half_o, half_o)]
            stream.append(pltpu.make_async_copy(src, dst, osem.at[2 * index + part]))
    for copy in stream[:AHEAD]:
        copy.start()

    def take(number):
        stream[number].wait()
        if number + AHEAD < len(stream):
            stream[number + AHEAD].start()

    for slot in range(nz):
        for half in range(2):
            piece_copy(slot, half, pieces[slot][0]).wait()

    def normalise(index, carry):
        at = pl.ds(pl.multiple_of(index * 16, 16), 16)
        wide = xs[at, :].astype(jnp.float32)
        meansq = jnp.mean(wide * wide, axis=-1, keepdims=True)
        ns[at, :] = (wide * lax.rsqrt(meansq + 1e-05) * gain[...]).astype(jnp.bfloat16)
        return carry

    lax.fori_loop(0, tokens // 16, normalise, 0, unroll=4)

    for block_index in range(2):
        for branch in range(3):
            take(6 * block_index + 2 * branch)
            take(6 * block_index + 2 * branch + 1)
            product = jnp.dot(ns[...], wbuf[block_index * 3 + branch], preferred_element_type=jnp.float32)
            product = product.astype(jnp.bfloat16).astype(jnp.float32)
            for lane in range(block // 128):
                br[branch, lane] = product[:, lane * 128:(lane + 1) * 128]
        for lane in range(0, block, 128):
            lanes = pl.ds(lane, 128)
            taken = jnp.broadcast_to(accepted[...], (rows, 128))
            window = []
            for s in range(tail_len):
                window.append([tails[block_index, s * 3 + j, :, lanes].astype(jnp.float32) for j in range(3)])
            state = states[block_index, :, lanes]
            kept = state
            rate = decay[block_index, :, lanes]
            weight = [[taps[block_index, pl.ds(tap * 3 + j, 1), lanes] for j in range(3)] for tap in range(taps_n)]
            tail = [[window[i][j] for j in range(3)] for i in range(tail_len)]
            for i in range(tail_len):
                for s in range(i + 1, tail_len):
                    for j in range(3):
                        tail[i][j] = jnp.where(taken == s - i, window[s][j], tail[i][j])
            for step in range(steps):
                window.append([br[j, lane // 128, pl.ds(step, rows, stride=steps), :] for j in range(3)])
                s = tail_len + step
                for i in range(tail_len):
                    if s - i <= steps:
                        mask = taken == s - i
                        for j in range(3):
                            tail[i][j] = jnp.where(mask, window[s][j], tail[i][j])
                mixed = []
                for j in range(3):
                    total = weight[0][j] * window[s][j]
                    for tap in range(1, taps_n):
                        total = total + weight[tap][j] * window[s - tap][j]
                    mixed.append(total)
                state = rate * state + mixed[1] * mixed[2]
                kept = jnp.where(taken == step + 1, state, kept)
                gf[lane // 128, pl.ds(step, rows, stride=steps), :] = mixed[0] * state
            for i in range(tail_len):
                for j in range(3):
                    plane = (j * tail_len + i) * block + lane
                    commit[block_index, :, plane:plane + 128] = tail[i][j].astype(jnp.bfloat16)
            high = kept.astype(jnp.bfloat16)
            plane = 3 * tail_len * block + lane
            commit[block_index, :, plane:plane + 128] = high
            low = (kept - high.astype(jnp.float32)).astype(jnp.bfloat16)
            commit[block_index, :, plane + block:plane + block + 128] = low
        for lane in range(block // 128):
            gs[block_index, :, pl.ds(lane * 128, 128)] = gf[lane].astype(jnp.bfloat16)

    for number in range(12, 16):
        take(number)
    gated = jnp.concatenate([gs[b] for b in range(2)], axis=1)
    wide_out = 512
    for at in range(0, width, wide_out):
        columns = pl.ds(at, wide_out)
        pf[...] = jnp.dot(gated, wob[:, columns], preferred_element_type=jnp.float32)
        for slot in range(nz):
            picked = pl.ds(pl.multiple_of(meta[2 + slot] * unit, 16), unit)
            value = pf[picked, :]
            if slot == 0:
                terms[slot][:, columns] = value + xs[picked, columns].astype(jnp.float32)
            else:
                terms[slot][:, columns] = value.astype(jnp.bfloat16)


def run_chunk(nz, meta, slots, w_own, w_sib, o_own, o_sib, gain, taps, decay, tails, states, accepted, steps, share_rows, taps_n, tail_len):
    choices = tuple(len(slot) for slot in slots)
    pieces = [piece for slot in slots for piece in slot]
    _, tokens, local = pieces[0].shape
    width = w_own.shape[1]
    block = local
    blocks = 2 * local // block
    rows = tokens // steps
    unit = share_rows * steps
    anywhere = pl.BlockSpec(memory_space=pl.ANY)
    vmem = pl.BlockSpec(memory_space=pltpu.VMEM)
    out_shape = [jax.ShapeDtypeStruct((unit, width), jnp.float32)]
    out_shape += [jax.ShapeDtypeStruct((unit, width), jnp.bfloat16)] * (nz - 1)
    out_shape += [
        jax.ShapeDtypeStruct((blocks, rows, (tail_len * 3 + 2) * block), jnp.bfloat16),
    ]
    return pl.pallas_call(
        functools.partial(
            chunk_kernel, nz, choices, tail_len, taps_n, steps, rows, local, width, block, share_rows
        ),
        out_shape=out_shape,
        in_specs=[pl.BlockSpec(memory_space=pltpu.SMEM)] + [anywhere] * (len(pieces) + 4) + [vmem] * 6,
        out_specs=[vmem] * len(out_shape),
        scratch_shapes=[
            pltpu.VMEM((tokens, width), jnp.bfloat16),
            pltpu.VMEM((tokens, width), jnp.bfloat16),
            pltpu.VMEM((6, width, block), jnp.bfloat16),
            pltpu.VMEM((2 * local, width), jnp.bfloat16),
            pltpu.VMEM((3, block // 128, tokens, 128), jnp.float32),
            pltpu.VMEM((block // 128, tokens, 128), jnp.float32),
            pltpu.VMEM((blocks, tokens, block), jnp.bfloat16),
            pltpu.VMEM((tokens, 512), jnp.float32),
            pltpu.SemaphoreType.DMA((nz, 2)),
            pltpu.SemaphoreType.DMA((12,)),
            pltpu.SemaphoreType.DMA((4,)),
        ],
        compiler_params=pltpu.CompilerParams(vmem_limit_bytes=58 * 1024 * 1024),
        cost_estimate=pl.CostEstimate(
            flops=COST * tokens * width * local, bytes_accessed=4 * tokens * width, transcendentals=0
        ),
    )(meta, *pieces, w_own, w_sib, o_own, o_sib, gain, taps, decay, tails, states, accepted)


def per_device(
    n_tensor, n_dp,
    drafted, norm_gain, w_in, conv_taps, decay, w_out, queue_tails, states, accepted, owner_map
):
    rows, steps, local = drafted.shape
    taps_n = conv_taps.shape[0]
    tail_len = queue_tails.shape[1]
    width = w_in.shape[0]
    nz = n_tensor // 2
    share = rows // n_tensor
    block = local
    me = lax.axis_index("tensor")
    z, core = me // 2, me % 2
    is_end = jnp.logical_or(z == 0, z == nz - 1)

    swap_pairs = [(t, t ^ 1) for t in range(n_tensor)]

    def permute(value, links, what):
        with jax.named_scope(what):
            return lax.ppermute(value, "tensor", links)

    def swap(value, what):
        return permute(value, swap_pairs, what)

    def chips(links):
        return [(2 * a + c, 2 * b + c) for a, b in links for c in (0, 1)]

    sizes = [share // 2, share - share // 2]
    parts = len(sizes)
    cuts = [slice(sum(sizes[:p]), sum(sizes[:p + 1])) for p in range(parts)]

    def mine(array):
        return lax.dynamic_index_in_dim(array, core, 1, keepdims=False)

    def other(array):
        return lax.dynamic_index_in_dim(array, 1 - core, 1, keepdims=False)

    by_core = drafted.reshape(nz, 2, share, steps, local)
    here, there = mine(by_core), other(by_core)
    arrived = swap(there, "swap_tokens")
    held = []
    for part in range(parts):
        cut, size = cuts[part], sizes[part]
        held.append(jnp.stack([
            here[:, cut].reshape(nz * size * steps, local),
            arrived[:, cut].reshape(nz * size * steps, local),
        ]))

    held, conv_taps, decay, queue_tails, states, owner_map = lax.optimization_barrier(
        (held, conv_taps, decay, queue_tails, states, owner_map)
    )
    small = jnp.concatenate([conv_taps.reshape(taps_n * 3, local), decay[None]], axis=0)
    small_sib = swap(small, "swap_taps")
    tails_core = jnp.transpose(queue_tails, (1, 2, 0, 3)).reshape(tail_len * 3, nz, 2, share, local)
    tails_here = lax.dynamic_index_in_dim(tails_core, core, 2, keepdims=False)
    tails_sib = swap(lax.dynamic_index_in_dim(tails_core, 1 - core, 2, keepdims=False), "swap_tails")
    states_core = states.reshape(nz, 2, share, local)
    states_sib = swap(other(states_core), "swap_states")
    states_here = mine(states_core)

    w_in, w_out, small_sib, tails_sib, states_sib = lax.optimization_barrier(
        (w_in, w_out, small_sib, tails_sib, states_sib)
    )
    w_own = jnp.transpose(w_in, (1, 0, 2))
    w_sib = swap(w_own, "swap_w_in")
    o_sib = swap(w_out, "swap_w_out")

    def blocked(own, sib):
        both = jnp.concatenate([own, sib], axis=-1)
        cut = both.reshape(*both.shape[:-1], 2 * local // block, block)
        return jnp.moveaxis(cut, -2, 0)

    small_all = blocked(small, small_sib)
    taps_all, decay_all = small_all[:, :-1], small_all[:, -1:]
    accepted_here = mine(accepted.reshape(nz, 2, share))

    line = nz == 4
    if line:
        order = [z, z ^ 1, jnp.where(z < 2, 2, 1), jnp.where(z < 2, 3, 0)]
        ends = chips([(0, 1), (1, 0), (2, 3), (3, 2)])
        outward = chips([(1, 0), (2, 3)])
        inward = chips([(0, 1), (3, 2)])
        between = chips([(1, 2), (2, 1)])
        middle = between + [(0, 1), (1, 0), (6, 7), (7, 6)]
        across = chips([(0, 3), (3, 0)]) + [(2, 3), (3, 2), (4, 5), (5, 4)]
        skip_in = chips([(0, 2), (3, 1)])
        skip_out = chips([(2, 0), (1, 3)])
    else:
        order = [(z - k) % nz for k in range(nz)]
        ring = chips([(k, (k + 1) % nz) for k in range(nz)])
    meta = jnp.stack([is_end.astype(jnp.int32), core] + order).astype(jnp.int32)

    def ordered(array):
        return jnp.concatenate(
            [array[:, cut].reshape(-1) for cut in cuts]
        )

    if line:
        x0, x1 = held
        e1, m1 = permute(x0, ends, "gather0_e1"), permute(x0, between, "gather0_m1")
        e1, m1, owner_map = lax.optimization_barrier((e1, m1, owner_map))
    owner_core = owner_map.reshape(nz, 2, share)
    owner = jnp.concatenate([ordered(mine(owner_core)), ordered(other(owner_core))])
    sends = rows // n_dp
    target, slot = owner // rows, owner % rows
    same = target[:, None] == target[None, :]
    index = jnp.arange(rows, dtype=jnp.int32)
    rank = jnp.sum(jnp.where(same & (index[None, :] < index[:, None]), 1, 0), axis=1)
    place = target * sends + rank
    pick = place[None, :] == index[:, None]
    slot_out = jnp.sum(jnp.where(pick, slot[None, :], 0), axis=1)
    slot_in = lax.all_to_all(slot_out.reshape(n_dp, sends), "dp", split_axis=0, concat_axis=0, tiled=True)
    put = (slot_in.reshape(rows)[None, :] == index[:, None]).astype(jnp.bfloat16)
    pick = pick.astype(jnp.bfloat16)

    gain = norm_gain[None]
    sides = []
    for cut, size in zip(cuts, sizes):
        sides.append((
            blocked(
                tails_here[:, :, cut].reshape(tail_len * 3, nz * size, local),
                tails_sib[:, :, cut].reshape(tail_len * 3, nz * size, local),
            ),
            blocked(
                states_here[:, cut].reshape(nz * size, local), states_sib[:, cut].reshape(nz * size, local)
            ),
            accepted_here[:, cut].reshape(nz * size, 1),
        ))

    barrier = lax.optimization_barrier

    def add(a, b):
        return (a.astype(jnp.float32) + b.astype(jnp.float32)).astype(jnp.bfloat16)

    def run(part, slots):
        tails_part, states_part, accepted_part = sides[part]
        return run_chunk(
            nz, meta, slots, w_own, w_sib, w_out, o_sib, gain, taps_all, decay_all,
            tails_part, states_part, accepted_part, steps, sizes[part], taps_n, tail_len,
        )

    if line:
        e2 = permute(m1, outward, "gather0_e2")
        m2 = permute(e1, between, "gather0_m2")
        m2, e2, x1, sides, taps_all, decay_all, meta, pick, put = barrier(
            (m2, e2, x1, sides, taps_all, decay_all, meta, pick, put)
        )
        e3 = permute(m2, outward, "gather0_e3")
        g1 = permute(x1, middle, "gather1_m1")
        e3, g1, x1 = barrier((e3, g1, x1))
        f1 = permute(x1, ends, "gather1_e1")
        g2, f3 = permute(x1, skip_in, "gather1_skip"), permute(x1, across, "gather1_across")
        f2 = permute(g1, outward, "gather1_e2")
        first = run(0, [(x0,), (e1,), (m1, e2), (m2, e3)])
        own0, near0, mid0, far0, commit0 = first
        near0, mid0, far0, f1, f2, f3, g2 = barrier((near0, mid0, far0, f1, f2, f3, g2))
        mid0_in = permute(mid0, inward, "sum0_mid_in")
        near0_in = permute(near0, ends, "sum0_near")
        far0_in, skip0_in = permute(far0, across, "sum0_across"), permute(far0, skip_out, "sum0_skip")
        own1, near1, mid1, far1, commit1 = run(1, [(x1,), (f1,), (g1, f2), (g2, f3)])
        far1_in, mid1_in = permute(far1, inward, "sum1_far_in"), permute(mid1, inward, "sum1_mid_in")
        near1, commit1, mid0_in, near0_in, far0_in, skip0_in = barrier(
            (near1, commit1, mid0_in, near0_in, far0_in, skip0_in)
        )
        mid0_on = permute(add(mid0, mid0_in), middle, "sum0_mid_on")
        second = [own1, near1, mid1, far1, commit1]
        results = [first, second]
    else:
        results = []
        for part in range(parts):
            slots = [(held[part],)]
            for _ in range(nz - 1):
                slots.append((permute(slots[-1][0], ring, f"gather{part}"),))
            results.append(run(part, slots))

    packed = jnp.concatenate([r[-1] for r in results], axis=1)
    packed = jnp.concatenate([packed[0], swap(packed[1], "swap_commit")], axis=0)
    sent = jnp.dot(pick, packed, preferred_element_type=jnp.float32).astype(jnp.bfloat16)
    if line:
        far1_on = permute(add(far1, far1_in), middle, "sum1_far_on")
        mid1, sent = barrier((add(mid1, mid1_in), sent))
    got = lax.all_to_all(sent, "dp", split_axis=0, concat_axis=0, tiled=True)
    if line:
        mid1_on = permute(mid1, middle, "sum1_mid_on")
        near1 = add(near1, jnp.where(is_end, 0, far1_on))
        near1_in = permute(near1, ends, "sum1_near")
        wide = lambda value: value.astype(jnp.float32)
        total0 = own0 + wide(near0_in) + jnp.where(is_end, wide(far0_in) + wide(skip0_in), wide(mid0_on))
        total1 = own1 + wide(near1_in) + jnp.where(is_end, 0, wide(mid1_on))
        totals = [total0, total1]
    else:
        totals = []
        for terms in results:
            flow = terms[1]
            for k in range(2, nz):
                flow = add(terms[k], permute(flow, ring, "sum"))
            totals.append(terms[0] + permute(flow, ring, "sum").astype(jnp.float32))
    mixed = [
        total.astype(jnp.bfloat16).reshape(size, steps, width) for total, size in zip(totals, sizes)
    ]
    mixed = jnp.concatenate(mixed, axis=0)

    placed = jnp.dot(put, got, preferred_element_type=jnp.float32)
    edge = 3 * tail_len * local
    new_tails = placed[:, :edge].astype(jnp.bfloat16).reshape(rows, 3, tail_len, local)
    new_tails = jnp.transpose(new_tails, (0, 2, 1, 3))
    new_states = placed[:, edge:edge + local] + placed[:, edge + local:]
    return (mixed, new_tails, new_states)


def solution(mesh):
    return jax.shard_map(
        functools.partial(per_device, mesh.shape["tensor"], mesh.shape["dp"]),
        mesh=mesh,
        in_specs=(
            P("dp", None, "tensor"),
            P(),
            P(None, None, "tensor"),
            P(None, None, "tensor"),
            P("tensor"),
            P("tensor", None),
            P("dp", None, None, "tensor"),
            P("dp", "tensor"),
            P("dp"),
            P("dp"),
        ),
        out_specs=(
            P(("dp", "tensor"), None, None),
            P("dp", None, None, "tensor"),
            P("dp", "tensor"),
        ),
        check_vma=False,
    )
```

time: 348 us -> 178 us (0.51)
  waiting for transfers between devices: 175 us -> 69.6 us
  local copies, waits for them, and re-layouts: 71.6 us -> 10.6 us
  Pallas kernels: 0 us -> 38.1 us
  other arithmetic: 46.8 us -> 10.2 us
  starting transfers between devices: 11.4 us -> 45.5 us
  matrix products: 26.9 us -> 1.88 us
  between operations: 14.3 us -> 1.27 us
    reduce_scatter x1 -> x0, waiting for transfers between devices: 105 us -> none  [per_device(): lax.psum_scatter(jnp.dot(gated.reshape(share * lax.axis_size('tensor') *...]
    all_gather x1 -> x0, waiting for transfers between devices: 68.6 us -> none  [per_device(): full = lax.all_gather(drafted, 'tensor', axis=2, tiled=True)]
    ppermute x0 -> x27, waiting for transfers between devices: none -> 64.9 us  [permute(): return lax.ppermute(value, 'tensor', links)]
    pallas_call x0 -> x2, Pallas kernels: none -> 38.1 us  [run_chunk(): pl.pallas_call(functools.partial(chunk_kernel, nz, choices, tail_len, tap...]
    ppermute x0 -> x27, starting transfers between devices: none -> 37.7 us  [permute(): return lax.ppermute(value, 'tensor', links)]
    dot_general x2, matrix products: 26.9 us -> 1.88 us  [the longest x1 1.46 us: per_device(): jnp.dot(pick, packed, preferred_element_type=jnp.float32)]
    unnamed x26 -> x47, local copies, waits for them, and re-layouts: 21.3 us -> 1.48 us
    reshape x1 -> x8, local copies, waits for them, and re-layouts: 18.2 us -> 1.84 us  [the longest x1 1.45 us: per_device(): placed[:, :edge].astype(jnp.bfloat16).reshape(rows, 3, tail_len, local)]
  transfers between devices with their start and end apart: 5 -> 29, of which waited for: 3 -> 10; matrix products, arithmetic and copies ran while one was open for 19% -> 9% of each run, Pallas kernels for 0% -> 22%
where the time goes in v1:
time: 178 us; the launch traced here: 177 us
  waiting for transfers between devices  69.6 us (39%)
  starting transfers between devices  45.5 us (26%)
  Pallas kernels  38.1 us (21%)
  local copies, waits for them, and re-layouts  10.6 us (6%)
  other arithmetic  10.2 us (6%)
  matrix products  1.88 us (1%)
    ppermute x27, waiting for transfers between devices, permute(): return lax.ppermute(value, 'tensor', links)  64.9 us
    pallas_call x2, Pallas kernels, run_chunk(): pl.pallas_call(functools.partial(chunk_kernel, nz, choices, tail_len, tap...  38.1 us
    ppermute x27, starting transfers between devices, permute(): return lax.ppermute(value, 'tensor', links)  37.7 us
    all_to_all x1, waiting for transfers between devices, per_device(): lax.all_to_all(slot_out.reshape(n_dp, sends), 'dp', split_axis=0, concat_...  4.63 us
    all_to_all x1, starting transfers between devices, per_device(): lax.all_to_all(slot_out.reshape(n_dp, sends), 'dp', split_axis=0, concat_...  3.88 us
    all_to_all x1, starting transfers between devices, per_device(): got = lax.all_to_all(sent, 'dp', split_axis=0, concat_axis=0, tiled=True)  3.85 us
  transfers between devices with their start and end apart: 29, of which 10 were waited for; matrix products, arithmetic and copies ran while one was open for 9% of the time, Pallas kernels for 22%

profile of v1, /device:TPU:0, one launch (start us, length us, event | category | flops | bytes accessed | tf_op | source)
XLA Modules:
  0.0 177.0 jit_solution(11956952361490563627)
XLA Ops:
  0.7 1.3 dynamic-slice_bitcast_fusion.1
  2.5 1.5 collective-permute-done
  6.1 1.1 collective-permute-done.5
  8.0 0.6 stack.39.meta
  8.6 2.7 %collective-permute-start.1 = (bf16[2,256,512]{2,1,0:T(8,128)(2,1)S(1)}, bf16[2,256,512]{2,1,0:T(8,128)(2,1)}, u32[]{:S(2)}, u32[]{:S(2)}) collective-permute-start(bf16[2,256,512]{2,1,0:T(8,128)(2,1)S(1)} %get-tuple-element.60.refs_0_), channel_id=1, source_target_pairs={{0,2},{1,3},{2,0},{3,1},{4,6},{5,7},{6,4},{7,5},{8,10},{9,11},{10,... | collective-permute-start | bytes 1572872 | tf_op jit(solution)/shard_map/gather0_e1/ppermute | solution.py:210
  11.3 1.5 collective-permute-start.2
  12.9 0.7 maximum_bitcast_fusion.3.refs_14_
  13.6 0.7 maximum_bitcast_fusion.2.refs_14_
  14.3 0.6 slice.110.refs_12_
  14.9 0.8 maximum_bitcast_fusion.1.refs_13_
  15.8 0.8 maximum_bitcast_fusion.refs_13_
  16.5 7.3 %collective-permute-done.1.refs_1_ = bf16[2,256,512]{2,1,0:T(8,128)(2,1)} collective-permute-done((bf16[2,256,512]{2,1,0:T(8,128)(2,1)S(1)}, bf16[2,256,512]{2,1,0:T(8,128)(2,1)}, u32[]{:S(2)}, u32[]{:S(2)}) %collective-permute-start.1) | collective-permute-done | bytes 524320 | tf_op jit(solution)/shard_map/gather0_e1/ppermute | solution.py:210
  24.5 0.7 collective-permute-start.3
  25.2 1.3 collective-permute-start.4
  26.9 0.6 all_to_all.14
  27.5 3.9 %all-to-all-start = ((s32[4,1,32]{2,1,0:T(1,128)}), s32[4,1,32]{2,1,0:T(1,128)S(1)}, u32[]{:S(2)}, u32[]{:S(2)}) async-start(s32[4,1,32]{2,1,0:T(1,128)} %bitcast.38), calls=%async_computation | async-start | bytes 4096 | tf_op jit(solution)/shard_map/all_to_all | solution.py:302
  31.4 4.6 %all-to-all-done = s32[4,1,32]{2,1,0:T(1,128)S(1)} async-done(((s32[4,1,32]{2,1,0:T(1,128)}), s32[4,1,32]{2,1,0:T(1,128)S(1)}, u32[]{:S(2)}, u32[]{:S(2)}) %all-to-all-start) | async-done | bytes 544 | tf_op jit(solution)/shard_map/all_to_all | solution.py:302
  37.2 8.1 %collective-permute-done.4.refs_3_ = bf16[2,256,512]{2,1,0:T(8,128)(2,1)S(1)} collective-permute-done((bf16[2,256,512]{2,1,0:T(8,128)(2,1)}, bf16[2,256,512]{2,1,0:T(8,128)(2,1)S(1)}, u32[]{:S(2)}, u32[]{:S(2)}) %collective-permute-start.4) | collective-permute-done | bytes 524320 | tf_op jit(solution)/shard_map/gather0_e2/ppermute | solution.py:210
  45.4 1.3 collective-permute-start.8
  46.8 0.7 copy.27.refs_15_
  47.4 0.7 copy.28.refs_15_
  48.1 11.3 %collective-permute-done.8.refs_5_ = bf16[2,256,512]{2,1,0:T(8,128)(2,1)S(1)} collective-permute-done((bf16[2,256,512]{2,1,0:T(8,128)(2,1)S(1)}, bf16[2,256,512]{2,1,0:T(8,128)(2,1)S(1)}, u32[]{:S(2)}, u32[]{:S(2)}) %collective-permute-start.8) | collective-permute-done | bytes 524320 | tf_op jit(solution)/shard_map/gather0_e3/ppermute | solution.py:210
  59.4 0.8 copy-done.22
  60.2 1.0 collective-permute-start.12
  61.3 1.8 %collective-permute-start.14 = (bf16[2,256,512]{2,1,0:T(8,128)(2,1)S(1)}, bf16[2,256,512]{2,1,0:T(8,128)(2,1)S(1)}, u32[]{:S(2)}, u32[]{:S(2)}) collective-permute-start(bf16[2,256,512]{2,1,0:T(8,128)(2,1)S(1)} %get-tuple-element.86.refs_0_), channel_id=1, source_target_pairs={{0,6},{1,7},{6,0},{7,1},{2,3},{3,2},{4,5},{5,4},{8,14},{9,15},{14,... | collective-permute-start | bytes 1572872 | tf_op jit(solution)/shard_map/gather1_across/ppermute | solution.py:210
  63.1 1.4 collective-permute-start.15
  64.6 1.3 collective-permute-start.13
  65.9 19.0 %shard_map.121 = (f32[64,4096]{1,0:T(8,128)}, bf16[64,4096]{1,0:T(8,128)(2,1)}, bf16[64,4096]{1,0:T(8,128)(2,1)}, bf16[64,4096]{1,0:T(8,128)(2,1)}, bf16[2,32,4096]{2,1,0:T(8,128)(2,1)}) custom-call(s32[6]{0:T(128)} %stack.39.meta, bf16[2,256,512]{2,1,0:T(8,128)(2,1)} %copy-done.8, bf16[2,256,512]{2,1,0:T(8,128)(2,1)} %collective-permute-done.1.refs_1_, ...), custom_call_target="tpu_custom_call" | custom-call | flops 21474836480 | bytes 4194304 | tf_op jit(solution)/shard_map/pallas_call | solution.py:164
  85.0 8.9 %collective-permute-done.13.refs_3_ = bf16[2,256,512]{2,1,0:T(8,128)(2,1)S(1)} collective-permute-done((bf16[2,256,512]{2,1,0:T(8,128)(2,1)S(1)}, bf16[2,256,512]{2,1,0:T(8,128)(2,1)S(1)}, u32[]{:S(2)}, u32[]{:S(2)}) %collective-permute-start.13) | collective-permute-done | bytes 524320 | tf_op jit(solution)/shard_map/gather1_e2/ppermute | solution.py:210
  93.9 2.2 %collective-permute-start.18 = (bf16[64,4096]{1,0:T(8,128)(2,1)}, bf16[64,4096]{1,0:T(8,128)(2,1)}, u32[]{:S(2)}, u32[]{:S(2)}) collective-permute-start(bf16[64,4096]{1,0:T(8,128)(2,1)} %get-tuple-element.102), channel_id=1, source_target_pairs={{0,6},{1,7},{6,0},{7,1},{2,3},{3,2},{4,5},{5,4},{8,14},{9,15},{14,... | collective-permute-start | bytes 1572872 | tf_op jit(solution)/shard_map/sum0_across/ppermute | solution.py:210
  96.2 1.3 collective-permute-start.19
  97.5 5.8 %collective-permute-start.16 = (bf16[64,4096]{1,0:T(8,128)(2,1)}, bf16[64,4096]{1,0:T(8,128)(2,1)S(1)}, u32[]{:S(2)}, u32[]{:S(2)}) collective-permute-start(bf16[64,4096]{1,0:T(8,128)(2,1)} %get-tuple-element.100), channel_id=1, source_target_pairs={{0,2},{1,3},{6,4},{7,5},{8,10},{9,11},{14,12},{15,13},{16,18},{17,... | collective-permute-start | bytes 1572872 | tf_op jit(solution)/shard_map/sum0_mid_in/ppermute | solution.py:210
  103.4 19.0 %shard_map.122 = (f32[64,4096]{1,0:T(8,128)}, bf16[64,4096]{1,0:T(8,128)(2,1)}, bf16[64,4096]{1,0:T(8,128)(2,1)}, bf16[64,4096]{1,0:T(8,128)(2,1)}, bf16[2,32,4096]{2,1,0:T(8,128)(2,1)}) custom-call(s32[6]{0:T(128)} %stack.39.meta, bf16[2,256,512]{2,1,0:T(8,128)(2,1)} %copy-done.7, bf16[2,256,512]{2,1,0:T(8,128)(2,1)} %copy-done.18, ...), custom_call_target="tpu_custom_call" | custom-call | flops 21474836480 | bytes 4194304 | tf_op jit(solution)/shard_map/pallas_call | solution.py:164
  122.4 3.3 %collective-permute-start.24 = (bf16[64,4096]{1,0:T(8,128)(2,1)}, bf16[64,4096]{1,0:T(8,128)(2,1)S(1)}, u32[]{:S(2)}, u32[]{:S(2)}) collective-permute-start(bf16[64,4096]{1,0:T(8,128)(2,1)} %get-tuple-element.110), channel_id=1, source_target_pairs={{0,2},{1,3},{6,4},{7,5},{8,10},{9,11},{14,12},{15,13},{16,18},{17,... | collective-permute-start | bytes 1572872 | tf_op jit(solution)/shard_map/sum1_mid_in/ppermute | solution.py:210
  125.8 1.5 collective-permute-start.21
  127.3 4.1 %collective-permute-done.17 = bf16[64,4096]{1,0:T(8,128)(2,1)} collective-permute-done((bf16[64,4096]{1,0:T(8,128)(2,1)}, bf16[64,4096]{1,0:T(8,128)(2,1)}, u32[]{:S(2)}, u32[]{:S(2)}) %collective-permute-start.17) | collective-permute-done | bytes 524320 | tf_op jit(solution)/shard_map/sum0_near/ppermute | solution.py:210
  131.4 1.1 constant_dynamic-update-slice_fusion
  133.3 16.7 %collective-permute-done.21 = bf16[64,4096]{1,0:T(8,128)(2,1)S(1)} collective-permute-done((bf16[64,4096]{1,0:T(8,128)(2,1)}, bf16[64,4096]{1,0:T(8,128)(2,1)S(1)}, u32[]{:S(2)}, u32[]{:S(2)}) %collective-permute-start.21) | collective-permute-done | bytes 524320 | tf_op jit(solution)/shard_map/sum1_far_in/ppermute | solution.py:210
  150.1 0.9 add_convert_fusion.3
  151.1 1.5 convolution_convert_fusion
  152.6 3.8 %all-to-all-start.1 = ((bf16[4,32,4096]{2,1,0:T(8,128)(2,1)}), bf16[4,32,4096]{2,1,0:T(8,128)(2,1)S(1)}, u32[]{:S(2)}, u32[]{:S(2)}) async-start(bf16[4,32,4096]{2,1,0:T(8,128)(2,1)} %bitcast.45), calls=%async_computation.1 | async-start | bytes 2097152 | tf_op jit(solution)/shard_map/all_to_all | solution.py:372
  156.5 1.2 add_convert_fusion.2
  157.7 7.7 %collective-permute-start.23 = (bf16[64,4096]{1,0:T(8,128)(2,1)S(1)}, bf16[64,4096]{1,0:T(8,128)(2,1)S(1)}, u32[]{:S(2)}, u32[]{:S(2)}) collective-permute-start(bf16[64,4096]{1,0:T(8,128)(2,1)S(1)} %add_convert_fusion.2), channel_id=1, source_target_pairs={{0,2},{1,3},{2,0},{3,1},{4,6},{5,7},{6,4},{7,5},{8,10},{9,11},{10,... | collective-permute-start | bytes 1572872 | tf_op jit(solution)/shard_map/sum1_near/ppermute | solution.py:210
  165.4 1.8 %fusion.3 = bf16[8,8,4096]{2,1,0:T(8,128)(2,1)S(1)} fusion(bf16[64,4096]{1,0:T(8,128)(2,1)} %collective-permute-done.20, bf16[64,4096]{1,0:T(8,128)(2,1)} %collective-permute-done.19, bf16[64,4096]{1,0:T(8,128)(2,1)} %collective-permute-done.18, f32[64,4096]{1,0:T(8,128)S(1)} %copy-done.1, bf16[64,4096]{1,0:T(8,128)(2,1)} %collective-permute-done.17, pred[]{:T(512)S(6)} %or.3), kind=kLoop, calls=%fused_computation.12 | loop fusion | flops 2359296 | bytes 3670017 | tf_op jit(solution)/shard_map/reshape | solution.py:389
  167.2 5.8 %collective-permute-done.23 = bf16[64,4096]{1,0:T(8,128)(2,1)S(1)} collective-permute-done((bf16[64,4096]{1,0:T(8,128)(2,1)S(1)}, bf16[64,4096]{1,0:T(8,128)(2,1)S(1)}, u32[]{:S(2)}, u32[]{:S(2)}) %collective-permute-start.23) | collective-permute-done | bytes 524320 | tf_op jit(solution)/shard_map/sum1_near/ppermute | solution.py:210
  173.2 1.1 pad_maximum_fusion
  174.8 0.7 slice_add_fusion
  175.6 1.4 reshape.498
  (121 shorter events, 7.6 us)
Async XLA Ops:
  2.0 2.1 %collective-permute-start = (bf16[4,16,8,512]{3,2,1,0:T(8,128)(2,1)S(1)}, bf16[4,16,8,512]{3,2,1,0:T(8,128)(2,1)S(1)}, u32[]{:S(2)}, u32[]{:S(2)}) collective-permute-start(bf16[4,16,8,512]{3,2,1,0:T(8,128)(2,1)S(1)} %get-tuple-element.122), channel_id=1, source_target_pairs={{0,1},{1,0},{2,3},{3,2},{4,5},{5,4},{6,7},{7,6},{8,9},{9,8},{10,11... | collective-permute-start | bytes 1572872 | tf_op jit(solution)/shard_map/swap_tokens/ppermute | solution.py:210
  2.5 1.8 copy-start.2
  4.2 8.7 %copy-start.8 = (bf16[2,256,512]{2,1,0:T(8,128)(2,1)}, bf16[2,256,512]{2,1,0:T(8,128)(2,1)S(1)}, u32[]{:S(2)}) copy-start(bf16[2,256,512]{2,1,0:T(8,128)(2,1)S(1)} %get-tuple-element.60.refs_0_) | copy-start | bytes 1572868
  4.2 58.9 %copy-start.7 = (bf16[2,256,512]{2,1,0:T(8,128)(2,1)}, bf16[2,256,512]{2,1,0:T(8,128)(2,1)S(1)}, u32[]{:S(2)}) copy-start(bf16[2,256,512]{2,1,0:T(8,128)(2,1)S(1)} %get-tuple-element.86.refs_0_) | copy-start | bytes 1572868
  4.2 3.4 %copy-start.13 = (s32[128]{0:T(128)S(1)}, s32[128]{0:T(128)}, u32[]{:S(2)}) copy-start(s32[128]{0:T(128)} %param.18) | copy-start | bytes 1540
  4.4 2.7 %collective-permute-start.6 = (bf16[6,4,16,512]{3,2,1,0:T(8,128)(2,1)S(1)}, bf16[6,4,16,512]{3,2,1,0:T(8,128)(2,1)S(1)}, u32[]{:S(2)}, u32[]{:S(2)}) collective-permute-start(bf16[6,4,16,512]{3,2,1,0:T(8,128)(2,1)S(1)} %get-tuple-element.124), channel_id=1, source_target_pairs={{0,1},{1,0},{2,3},{3,2},{4,5},{5,4},{6,7},{7,6},{8,9},{9,8},{10,11... | collective-permute-start | bytes 1179656 | tf_op jit(solution)/shard_map/swap_tails/ppermute | solution.py:210
  5.4 1.7 collective-permute-start.7
  5.9 1.3 collective-permute-start.5
  7.2 58.7 %collective-permute-start.10 = (bf16[3,4096,512]{2,1,0:T(8,128)(2,1)}, bf16[3,4096,512]{2,1,0:T(8,128)(2,1)}, u32[]{:S(2)}, u32[]{:S(2)}) collective-permute-start(bf16[3,4096,512]{2,1,0:T(8,128)(2,1)} %bitcast.93), channel_id=1, source_target_pairs={{0,1},{1,0},{2,3},{3,2},{4,5},{5,4},{6,7},{7,6},{8,9},{9,8},{10,11... | collective-permute-start | bytes 37748744 | tf_op jit(solution)/shard_map/swap_w_in/ppermute | solution.py:210
  7.3 57.3 %collective-permute-start.11 = (bf16[512,4096]{1,0:T(8,128)(2,1)}, bf16[512,4096]{1,0:T(8,128)(2,1)}, u32[]{:S(2)}, u32[]{:S(2)}) collective-permute-start(bf16[512,4096]{1,0:T(8,128)(2,1)} %refs_8_.1), channel_id=1, source_target_pairs={{0,1},{1,0},{2,3},{3,2},{4,5},{5,4},{6,7},{7,6},{8,9},{9,8},{10,11... | collective-permute-start | bytes 12582920 | tf_op jit(solution)/shard_map/swap_w_out/ppermute | solution.py:210
  8.6 15.3 %collective-permute-start.1 = (bf16[2,256,512]{2,1,0:T(8,128)(2,1)S(1)}, bf16[2,256,512]{2,1,0:T(8,128)(2,1)}, u32[]{:S(2)}, u32[]{:S(2)}) collective-permute-start(bf16[2,256,512]{2,1,0:T(8,128)(2,1)S(1)} %get-tuple-element.60.refs_0_), channel_id=1, source_target_pairs={{0,2},{1,3},{2,0},{3,1},{4,6},{5,7},{6,4},{7,5},{8,10},{9,11},{10,... | collective-permute-start | bytes 1572872 | tf_op jit(solution)/shard_map/gather0_e1/ppermute | solution.py:210
  11.3 12.5 %collective-permute-start.2 = (bf16[2,256,512]{2,1,0:T(8,128)(2,1)S(1)}, bf16[2,256,512]{2,1,0:T(8,128)(2,1)}, u32[]{:S(2)}, u32[]{:S(2)}) collective-permute-start(bf16[2,256,512]{2,1,0:T(8,128)(2,1)S(1)} %get-tuple-element.60.refs_0_), channel_id=1, source_target_pairs={{2,4},{3,5},{4,2},{5,3},{10,12},{11,13},{12,10},{13,11},{18,20},{1... | collective-permute-start | bytes 1572872 | tf_op jit(solution)/shard_map/gather0_m1/ppermute | solution.py:210
  12.8 11.1 %copy-start.14 = (s32[128]{0:T(128)S(1)}, s32[128]{0:T(128)}, u32[]{:S(2)}) copy-start(s32[128]{0:T(128)} %param.19) | copy-start | bytes 1540
  14.3 51.6 %copy-start.10 = (f32[10,2,512]{2,0,1:T(8,128)}, f32[10,2,512]{2,0,1:T(8,128)S(1)}, u32[]{:S(2)}) copy-start(f32[10,2,512]{2,0,1:T(8,128)S(1)} %copy.30) | copy-start | bytes 122884
  24.5 12.8 %collective-permute-start.3 = (bf16[2,256,512]{2,1,0:T(8,128)(2,1)}, bf16[2,256,512]{2,1,0:T(8,128)(2,1)S(1)}, u32[]{:S(2)}, u32[]{:S(2)}) collective-permute-start(bf16[2,256,512]{2,1,0:T(8,128)(2,1)} %collective-permute-done.1.refs_1_), channel_id=1, source_target_pairs={{2,4},{3,5},{4,2},{5,3},{10,12},{11,13},{12,10},{13,11},{18,20},{1... | collective-permute-start | bytes 1572872 | tf_op jit(solution)/shard_map/gather0_m2/ppermute | solution.py:210
  25.2 20.2 %collective-permute-start.4 = (bf16[2,256,512]{2,1,0:T(8,128)(2,1)}, bf16[2,256,512]{2,1,0:T(8,128)(2,1)S(1)}, u32[]{:S(2)}, u32[]{:S(2)}) collective-permute-start(bf16[2,256,512]{2,1,0:T(8,128)(2,1)} %collective-permute-done.2.refs_2_), channel_id=1, source_target_pairs={{2,0},{3,1},{4,6},{5,7},{10,8},{11,9},{12,14},{13,15},{18,16},{19,... | collective-permute-start | bytes 1572872 | tf_op jit(solution)/shard_map/gather0_e2/ppermute | solution.py:210
  27.5 8.5 %all-to-all-start = ((s32[4,1,32]{2,1,0:T(1,128)}), s32[4,1,32]{2,1,0:T(1,128)S(1)}, u32[]{:S(2)}, u32[]{:S(2)}) async-start(s32[4,1,32]{2,1,0:T(1,128)} %bitcast.38), calls=%async_computation | async-start | bytes 4096 | tf_op jit(solution)/shard_map/all_to_all | solution.py:302
  37.2 28.7 %copy-start.15 = (bf16[2,256,512]{2,1,0:T(8,128)(2,1)}, bf16[2,256,512]{2,1,0:T(8,128)(2,1)S(1)}, u32[]{:S(2)}) copy-start(bf16[2,256,512]{2,1,0:T(8,128)(2,1)S(1)} %collective-permute-done.3.refs_4_) | copy-start | bytes 1572868
  45.4 20.5 %copy-start.16 = (bf16[2,256,512]{2,1,0:T(8,128)(2,1)}, bf16[2,256,512]{2,1,0:T(8,128)(2,1)S(1)}, u32[]{:S(2)}) copy-start(bf16[2,256,512]{2,1,0:T(8,128)(2,1)S(1)} %collective-permute-done.4.refs_3_) | copy-start | bytes 1572868
  45.4 14.0 %collective-permute-start.8 = (bf16[2,256,512]{2,1,0:T(8,128)(2,1)S(1)}, bf16[2,256,512]{2,1,0:T(8,128)(2,1)S(1)}, u32[]{:S(2)}, u32[]{:S(2)}) collective-permute-start(bf16[2,256,512]{2,1,0:T(8,128)(2,1)S(1)} %collective-permute-done.3.refs_4_), channel_id=1, source_target_pairs={{2,0},{3,1},{4,6},{5,7},{10,8},{11,9},{12,14},{13,15},{18,16},{19,... | collective-permute-start | bytes 1572872 | tf_op jit(solution)/shard_map/gather0_e3/ppermute | solution.py:210
  46.7 12.7 %collective-permute-start.9 = (bf16[2,256,512]{2,1,0:T(8,128)(2,1)S(1)}, bf16[2,256,512]{2,1,0:T(8,128)(2,1)S(1)}, u32[]{:S(2)}, u32[]{:S(2)}) collective-permute-start(bf16[2,256,512]{2,1,0:T(8,128)(2,1)S(1)} %get-tuple-element.86.refs_0_), channel_id=1, source_target_pairs={{2,4},{3,5},{4,2},{5,3},{0,1},{1,0},{6,7},{7,6},{10,12},{11,13},{1... | collective-permute-start | bytes 1572872 | tf_op jit(solution)/shard_map/gather1_m1/ppermute | solution.py:210
  60.2 24.7 %copy-start.17 = (bf16[2,256,512]{2,1,0:T(8,128)(2,1)}, bf16[2,256,512]{2,1,0:T(8,128)(2,1)S(1)}, u32[]{:S(2)}) copy-start(bf16[2,256,512]{2,1,0:T(8,128)(2,1)S(1)} %collective-permute-done.9.refs_2_) | copy-start | bytes 1572868
  60.2 24.7 %collective-permute-start.12 = (bf16[2,256,512]{2,1,0:T(8,128)(2,1)S(1)}, bf16[2,256,512]{2,1,0:T(8,128)(2,1)S(1)}, u32[]{:S(2)}, u32[]{:S(2)}) collective-permute-start(bf16[2,256,512]{2,1,0:T(8,128)(2,1)S(1)} %get-tuple-element.86.refs_0_), channel_id=1, source_target_pairs={{0,2},{1,3},{2,0},{3,1},{4,6},{5,7},{6,4},{7,5},{8,10},{9,11},{10,... | collective-permute-start | bytes 1572872 | tf_op jit(solution)/shard_map/gather1_e1/ppermute | solution.py:210
  61.3 32.6 %collective-permute-start.14 = (bf16[2,256,512]{2,1,0:T(8,128)(2,1)S(1)}, bf16[2,256,512]{2,1,0:T(8,128)(2,1)S(1)}, u32[]{:S(2)}, u32[]{:S(2)}) collective-permute-start(bf16[2,256,512]{2,1,0:T(8,128)(2,1)S(1)} %get-tuple-element.86.refs_0_), channel_id=1, source_target_pairs={{0,6},{1,7},{6,0},{7,1},{2,3},{3,2},{4,5},{5,4},{8,14},{9,15},{14,... | collective-permute-start | bytes 1572872 | tf_op jit(solution)/shard_map/gather1_across/ppermute | solution.py:210
  63.1 30.8 %collective-permute-start.15 = (bf16[2,256,512]{2,1,0:T(8,128)(2,1)S(1)}, bf16[2,256,512]{2,1,0:T(8,128)(2,1)S(1)}, u32[]{:S(2)}, u32[]{:S(2)}) collective-permute-start(bf16[2,256,512]{2,1,0:T(8,128)(2,1)S(1)} %get-tuple-element.86.refs_0_), channel_id=1, source_target_pairs={{0,4},{1,5},{6,2},{7,3},{8,12},{9,13},{14,10},{15,11},{16,20},{17,... | collective-permute-start | bytes 1572872 | tf_op jit(solution)/shard_map/gather1_skip/ppermute | solution.py:210
  64.6 29.3 %collective-permute-start.13 = (bf16[2,256,512]{2,1,0:T(8,128)(2,1)S(1)}, bf16[2,256,512]{2,1,0:T(8,128)(2,1)S(1)}, u32[]{:S(2)}, u32[]{:S(2)}) collective-permute-start(bf16[2,256,512]{2,1,0:T(8,128)(2,1)S(1)} %collective-permute-done.9.refs_2_), channel_id=1, source_target_pairs={{2,0},{3,1},{4,6},{5,7},{10,8},{11,9},{12,14},{13,15},{18,16},{19,... | collective-permute-start | bytes 1572872 | tf_op jit(solution)/shard_map/gather1_e2/ppermute | solution.py:210
  85.0 18.3 %copy-start.18 = (bf16[2,256,512]{2,1,0:T(8,128)(2,1)}, bf16[2,256,512]{2,1,0:T(8,128)(2,1)S(1)}, u32[]{:S(2)}) copy-start(bf16[2,256,512]{2,1,0:T(8,128)(2,1)S(1)} %collective-permute-done.12.refs_1_) | copy-start | bytes 1572868
  93.9 9.4 %copy-start.21 = (bf16[2,256,512]{2,1,0:T(8,128)(2,1)}, bf16[2,256,512]{2,1,0:T(8,128)(2,1)S(1)}, u32[]{:S(2)}) copy-start(bf16[2,256,512]{2,1,0:T(8,128)(2,1)S(1)} %collective-permute-done.13.refs_3_) | copy-start | bytes 1572868
  93.9 9.4 %copy-start.19 = (bf16[2,256,512]{2,1,0:T(8,128)(2,1)}, bf16[2,256,512]{2,1,0:T(8,128)(2,1)S(1)}, u32[]{:S(2)}) copy-start(bf16[2,256,512]{2,1,0:T(8,128)(2,1)S(1)} %collective-permute-done.14.refs_5_) | copy-start | bytes 1572868
  93.9 9.4 %copy-start.20 = (bf16[2,256,512]{2,1,0:T(8,128)(2,1)}, bf16[2,256,512]{2,1,0:T(8,128)(2,1)S(1)}, u32[]{:S(2)}) copy-start(bf16[2,256,512]{2,1,0:T(8,128)(2,1)S(1)} %collective-permute-done.15.refs_4_) | copy-start | bytes 1572868
  93.9 31.8 %copy-start.6 = (bf16[2,32,4096]{2,1,0:T(8,128)(2,1)S(1)}, bf16[2,32,4096]{2,1,0:T(8,128)(2,1)}, u32[]{:S(2)}) copy-start(bf16[2,32,4096]{2,1,0:T(8,128)(2,1)} %get-tuple-element.112) | copy-start | bytes 1572868
  93.9 37.4 %collective-permute-start.18 = (bf16[64,4096]{1,0:T(8,128)(2,1)}, bf16[64,4096]{1,0:T(8,128)(2,1)}, u32[]{:S(2)}, u32[]{:S(2)}) collective-permute-start(bf16[64,4096]{1,0:T(8,128)(2,1)} %get-tuple-element.102), channel_id=1, source_target_pairs={{0,6},{1,7},{6,0},{7,1},{2,3},{3,2},{4,5},{5,4},{8,14},{9,15},{14,... | collective-permute-start | bytes 1572872 | tf_op jit(solution)/shard_map/sum0_across/ppermute | solution.py:210
  96.2 35.2 %collective-permute-start.19 = (bf16[64,4096]{1,0:T(8,128)(2,1)}, bf16[64,4096]{1,0:T(8,128)(2,1)}, u32[]{:S(2)}, u32[]{:S(2)}) collective-permute-start(bf16[64,4096]{1,0:T(8,128)(2,1)} %get-tuple-element.102), channel_id=1, source_target_pairs={{4,0},{5,1},{2,6},{3,7},{12,8},{13,9},{10,14},{11,15},{20,16},{21,... | collective-permute-start | bytes 1572872 | tf_op jit(solution)/shard_map/sum0_skip/ppermute | solution.py:210
  97.5 28.3 %collective-permute-start.16 = (bf16[64,4096]{1,0:T(8,128)(2,1)}, bf16[64,4096]{1,0:T(8,128)(2,1)S(1)}, u32[]{:S(2)}, u32[]{:S(2)}) collective-permute-start(bf16[64,4096]{1,0:T(8,128)(2,1)} %get-tuple-element.100), channel_id=1, source_target_pairs={{0,2},{1,3},{6,4},{7,5},{8,10},{9,11},{14,12},{15,13},{16,18},{17,... | collective-permute-start | bytes 1572872 | tf_op jit(solution)/shard_map/sum0_mid_in/ppermute | solution.py:210
  103.2 28.2 %collective-permute-start.17 = (bf16[64,4096]{1,0:T(8,128)(2,1)}, bf16[64,4096]{1,0:T(8,128)(2,1)}, u32[]{:S(2)}, u32[]{:S(2)}) collective-permute-start(bf16[64,4096]{1,0:T(8,128)(2,1)} %get-tuple-element.101), channel_id=1, source_target_pairs={{0,2},{1,3},{2,0},{3,1},{4,6},{5,7},{6,4},{7,5},{8,10},{9,11},{10,... | collective-permute-start | bytes 1572872 | tf_op jit(solution)/shard_map/sum0_near/ppermute | solution.py:210
  122.4 28.6 %collective-permute-start.24 = (bf16[64,4096]{1,0:T(8,128)(2,1)}, bf16[64,4096]{1,0:T(8,128)(2,1)S(1)}, u32[]{:S(2)}, u32[]{:S(2)}) collective-permute-start(bf16[64,4096]{1,0:T(8,128)(2,1)} %get-tuple-element.110), channel_id=1, source_target_pairs={{0,2},{1,3},{6,4},{7,5},{8,10},{9,11},{14,12},{15,13},{16,18},{17,... | collective-permute-start | bytes 1572872 | tf_op jit(solution)/shard_map/sum1_mid_in/ppermute | solution.py:210
  125.7 6.9 %copy-start.3 = (bf16[64,4096]{1,0:T(8,128)(2,1)S(1)}, bf16[64,4096]{1,0:T(8,128)(2,1)}, u32[]{:S(2)}) copy-start(bf16[64,4096]{1,0:T(8,128)(2,1)} %get-tuple-element.100) | copy-start | bytes 1572868
  125.8 24.3 %collective-permute-start.21 = (bf16[64,4096]{1,0:T(8,128)(2,1)}, bf16[64,4096]{1,0:T(8,128)(2,1)S(1)}, u32[]{:S(2)}, u32[]{:S(2)}) collective-permute-start(bf16[64,4096]{1,0:T(8,128)(2,1)} %get-tuple-element.109), channel_id=1, source_target_pairs={{0,2},{1,3},{6,4},{7,5},{8,10},{9,11},{14,12},{15,13},{16,18},{17,... | collective-permute-start | bytes 1572872 | tf_op jit(solution)/shard_map/sum1_far_in/ppermute | solution.py:210
  132.5 17.6 %copy-start.5 = (bf16[64,4096]{1,0:T(8,128)(2,1)S(1)}, bf16[64,4096]{1,0:T(8,128)(2,1)}, u32[]{:S(2)}) copy-start(bf16[64,4096]{1,0:T(8,128)(2,1)} %get-tuple-element.109) | copy-start | bytes 1572868
  132.6 18.4 %copy-start.4 = (bf16[64,4096]{1,0:T(8,128)(2,1)S(1)}, bf16[64,4096]{1,0:T(8,128)(2,1)}, u32[]{:S(2)}) copy-start(bf16[64,4096]{1,0:T(8,128)(2,1)} %get-tuple-element.110) | copy-start | bytes 1572868
  132.6 18.6 %collective-permute-start.25 = (bf16[64,4096]{1,0:T(8,128)(2,1)S(1)}, bf16[64,4096]{1,0:T(8,128)(2,1)S(1)}, u32[]{:S(2)}, u32[]{:S(2)}) collective-permute-start(bf16[64,4096]{1,0:T(8,128)(2,1)S(1)} %get-tuple-element.120), channel_id=1, source_target_pairs={{0,1},{1,0},{2,3},{3,2},{4,5},{5,4},{6,7},{7,6},{8,9},{9,8},{10,11... | collective-permute-start | bytes 1572872 | tf_op jit(solution)/shard_map/swap_commit/ppermute | solution.py:210
  132.8 32.6 %collective-permute-start.20 = (bf16[64,4096]{1,0:T(8,128)(2,1)S(1)}, bf16[64,4096]{1,0:T(8,128)(2,1)}, u32[]{:S(2)}, u32[]{:S(2)}) collective-permute-start(bf16[64,4096]{1,0:T(8,128)(2,1)S(1)} %add_convert_fusion.5), channel_id=1, source_target_pairs={{2,4},{3,5},{4,2},{5,3},{0,1},{1,0},{6,7},{7,6},{10,12},{11,13},{1... | collective-permute-start | bytes 1572872 | tf_op jit(solution)/shard_map/sum0_mid_on/ppermute | solution.py:210
  151.0 5.5 %collective-permute-start.22 = (bf16[64,4096]{1,0:T(8,128)(2,1)}, bf16[64,4096]{1,0:T(8,128)(2,1)}, u32[]{:S(2)}, u32[]{:S(2)}) collective-permute-start(bf16[64,4096]{1,0:T(8,128)(2,1)} %add_convert_fusion.3), channel_id=1, source_target_pairs={{2,4},{3,5},{4,2},{5,3},{0,1},{1,0},{6,7},{7,6},{10,12},{11,13},{1... | collective-permute-start | bytes 1572872 | tf_op jit(solution)/shard_map/sum1_far_on/ppermute | solution.py:210
  152.6 12.8 %copy-start.1 = (f32[64,4096]{1,0:T(8,128)S(1)}, f32[64,4096]{1,0:T(8,128)}, u32[]{:S(2)}) copy-start(f32[64,4096]{1,0:T(8,128)} %get-tuple-element.85) | copy-start | bytes 3145732
  152.6 21.7 %all-to-all-start.1 = ((bf16[4,32,4096]{2,1,0:T(8,128)(2,1)}), bf16[4,32,4096]{2,1,0:T(8,128)(2,1)S(1)}, u32[]{:S(2)}, u32[]{:S(2)}) async-start(bf16[4,32,4096]{2,1,0:T(8,128)(2,1)} %bitcast.45), calls=%async_computation.1 | async-start | bytes 2097152 | tf_op jit(solution)/shard_map/all_to_all | solution.py:372
  157.7 15.4 %copy-start = (f32[64,4096]{1,0:T(8,128)S(1)}, f32[64,4096]{1,0:T(8,128)}, u32[]{:S(2)}) copy-start(f32[64,4096]{1,0:T(8,128)} %get-tuple-element.107) | copy-start | bytes 3145732
  157.7 15.3 %collective-permute-start.23 = (bf16[64,4096]{1,0:T(8,128)(2,1)S(1)}, bf16[64,4096]{1,0:T(8,128)(2,1)S(1)}, u32[]{:S(2)}, u32[]{:S(2)}) collective-permute-start(bf16[64,4096]{1,0:T(8,128)(2,1)S(1)} %add_convert_fusion.2), channel_id=1, source_target_pairs={{0,2},{1,3},{2,0},{3,1},{4,6},{5,7},{6,4},{7,5},{8,10},{9,11},{10,... | collective-permute-start | bytes 1572872 | tf_op jit(solution)/shard_map/sum1_near/ppermute | solution.py:210
  165.4 7.6 %collective-permute-start.26 = (bf16[64,4096]{1,0:T(8,128)(2,1)S(1)}, bf16[64,4096]{1,0:T(8,128)(2,1)S(1)}, u32[]{:S(2)}, u32[]{:S(2)}) collective-permute-start(bf16[64,4096]{1,0:T(8,128)(2,1)S(1)} %add_convert_fusion.1), channel_id=1, source_target_pairs={{2,4},{3,5},{4,2},{5,3},{0,1},{1,0},{6,7},{7,6},{10,12},{11,13},{1... | collective-permute-start | bytes 1572872 | tf_op jit(solution)/shard_map/sum1_mid_on/ppermute | solution.py:210
  (4 other events, 4.4 us)

commit v2 on v1

--- a/solution.py
+++ b/solution.py
@@ -248,20 +248,11 @@
     states_sib = swap(other(states_core), "swap_states")
     states_here = mine(states_core)
 
-    w_in, w_out, small_sib, tails_sib, states_sib = lax.optimization_barrier(
-        (w_in, w_out, small_sib, tails_sib, states_sib)
-    )
-    w_own = jnp.transpose(w_in, (1, 0, 2))
-    w_sib = swap(w_own, "swap_w_in")
-    o_sib = swap(w_out, "swap_w_out")
-
     def blocked(own, sib):
         both = jnp.concatenate([own, sib], axis=-1)
         cut = both.reshape(*both.shape[:-1], 2 * local // block, block)
         return jnp.moveaxis(cut, -2, 0)
 
-    small_all = blocked(small, small_sib)
-    taps_all, decay_all = small_all[:, :-1], small_all[:, -1:]
     accepted_here = mine(accepted.reshape(nz, 2, share))
 
     line = nz == 4
@@ -285,24 +276,33 @@
             [array[:, cut].reshape(-1) for cut in cuts]
         )
 
+    def commit_order(owner_map):
+        owner_core = owner_map.reshape(nz, 2, share)
+        owner = jnp.concatenate([ordered(mine(owner_core)), ordered(other(owner_core))])
+        sends = rows // n_dp
+        target, slot = owner // rows, owner % rows
+        same = target[:, None] == target[None, :]
+        index = jnp.arange(rows, dtype=jnp.int32)
+        rank = jnp.sum(jnp.where(same & (index[None, :] < index[:, None]), 1, 0), axis=1)
+        place = target * sends + rank
+        pick = place[None, :] == index[:, None]
+        slot_out = jnp.sum(jnp.where(pick, slot[None, :], 0), axis=1)
+        slot_in = lax.all_to_all(slot_out.reshape(n_dp, sends), "dp", split_axis=0, concat_axis=0, tiled=True)
+        put = (slot_in.reshape(rows)[None, :] == index[:, None]).astype(jnp.bfloat16)
+        pick = pick.astype(jnp.bfloat16)
+        return pick, put
+
     if line:
         x0, x1 = held
-        e1, m1 = permute(x0, ends, "gather0_e1"), permute(x0, between, "gather0_m1")
-        e1, m1, owner_map = lax.optimization_barrier((e1, m1, owner_map))
-    owner_core = owner_map.reshape(nz, 2, share)
-    owner = jnp.concatenate([ordered(mine(owner_core)), ordered(other(owner_core))])
-    sends = rows // n_dp
-    target, slot = owner // rows, owner % rows
-    same = target[:, None] == target[None, :]
-    index = jnp.arange(rows, dtype=jnp.int32)
-    rank = jnp.sum(jnp.where(same & (index[None, :] < index[:, None]), 1, 0), axis=1)
-    place = target * sends + rank
-    pick = place[None, :] == index[:, None]
-    slot_out = jnp.sum(jnp.where(pick, slot[None, :], 0), axis=1)
-    slot_in = lax.all_to_all(slot_out.reshape(n_dp, sends), "dp", split_axis=0, concat_axis=0, tiled=True)
-    put = (slot_in.reshape(rows)[None, :] == index[:, None]).astype(jnp.bfloat16)
-    pick = pick.astype(jnp.bfloat16)
-
+        e1, m1 = permute(x0, ends, "gather0_e1"), permute(x0, middle, "gather0_m1")
+        e1, m1, owner_map, w_in, w_out, small_sib, tails_sib, states_sib = lax.optimization_barrier(
+            (e1, m1, owner_map, w_in, w_out, small_sib, tails_sib, states_sib)
+        )
+    w_own = jnp.transpose(w_in, (1, 0, 2))
+    w_sib = swap(w_own, "swap_w_in")
+    o_sib = swap(w_out, "swap_w_out")
+    small_all = blocked(small, small_sib)
+    taps_all, decay_all = small_all[:, :-1], small_all[:, -1:]
     gain = norm_gain[None]
     sides = []
     for cut, size in zip(cuts, sizes):
@@ -332,30 +332,32 @@
     if line:
         e2 = permute(m1, outward, "gather0_e2")
         m2 = permute(e1, between, "gather0_m2")
-        m2, e2, x1, sides, taps_all, decay_all, meta, pick, put = barrier(
-            (m2, e2, x1, sides, taps_all, decay_all, meta, pick, put)
+        m2, e2, x1, sides, taps_all, decay_all, meta, owner_map = barrier(
+            (m2, e2, x1, sides, taps_all, decay_all, meta, owner_map)
         )
+        pick, put = commit_order(owner_map)
         e3 = permute(m2, outward, "gather0_e3")
         g1 = permute(x1, middle, "gather1_m1")
-        e3, g1, x1 = barrier((e3, g1, x1))
+        e3, g1, x1, pick, put = barrier((e3, g1, x1, pick, put))
         f1 = permute(x1, ends, "gather1_e1")
         g2, f3 = permute(x1, skip_in, "gather1_skip"), permute(x1, across, "gather1_across")
         f2 = permute(g1, outward, "gather1_e2")
         first = run(0, [(x0,), (e1,), (m1, e2), (m2, e3)])
         own0, near0, mid0, far0, commit0 = first
-        near0, mid0, far0, f1, f2, f3, g2 = barrier((near0, mid0, far0, f1, f2, f3, g2))
+        mid0, far0, f1, f2, f3, g2 = barrier((mid0, far0, f1, f2, f3, g2))
         mid0_in = permute(mid0, inward, "sum0_mid_in")
-        near0_in = permute(near0, ends, "sum0_near")
         far0_in, skip0_in = permute(far0, across, "sum0_across"), permute(far0, skip_out, "sum0_skip")
         own1, near1, mid1, far1, commit1 = run(1, [(x1,), (f1,), (g1, f2), (g2, f3)])
-        far1_in, mid1_in = permute(far1, inward, "sum1_far_in"), permute(mid1, inward, "sum1_mid_in")
-        near1, commit1, mid0_in, near0_in, far0_in, skip0_in = barrier(
-            (near1, commit1, mid0_in, near0_in, far0_in, skip0_in)
-        )
+        far1_in = permute(far1, inward, "sum1_far_in")
+        near1, commit1, mid0_in, far0_in, skip0_in = barrier((near1, commit1, mid0_in, far0_in, skip0_in))
         mid0_on = permute(add(mid0, mid0_in), middle, "sum0_mid_on")
+        near0, mid1, far1_in, mid0_on = barrier((near0, mid1, far1_in, mid0_on))
+        mid1_in = permute(mid1, inward, "sum1_mid_in")
+        near0_in = permute(near0, ends, "sum0_near")
         second = [own1, near1, mid1, far1, commit1]
         results = [first, second]
     else:
+        pick, put = commit_order(owner_map)
         results = []
         for part in range(parts):
             slots = [(held[part],)]

time: 178 us -> 168 us (0.944)
  starting transfers between devices: 45.5 us -> 39.7 us
  waiting for transfers between devices: 69.6 us -> 67.3 us
    ppermute x27, starting transfers between devices: 37.7 us -> 32.1 us  [permute(): return lax.ppermute(value, 'tensor', links)]
  transfers between devices with their start and end apart: 29 -> 29, of which waited for: 10 -> 12; matrix products, arithmetic and copies ran while one was open for 9% -> 9% of each run, Pallas kernels for 22% -> 23%
where the time goes in v2:
time: 168 us
  waiting for transfers between devices  67.3 us (40%)
  starting transfers between devices  39.7 us (24%)
  Pallas kernels  38.1 us (23%)
  local copies, waits for them, and re-layouts  10.1 us (6%)
  other arithmetic  9.45 us (6%)
  matrix products  1.86 us (1%)
    ppermute x27, waiting for transfers between devices, permute(): return lax.ppermute(value, 'tensor', links)  64 us
    pallas_call x2, Pallas kernels, run_chunk(): pl.pallas_call(functools.partial(chunk_kernel, nz, choices, tail_len, tap...  38.1 us
    ppermute x27, starting transfers between devices, permute(): return lax.ppermute(value, 'tensor', links)  32.1 us
    all_to_all x1, starting transfers between devices, per_device(): got = lax.all_to_all(sent, 'dp', split_axis=0, concat_axis=0, tiled=True)  3.86 us
    all_to_all x1, starting transfers between devices, commit_order(): lax.all_to_all(slot_out.reshape(n_dp, sends), 'dp', split_axis=0, concat_...  3.72 us
  transfers between devices with their start and end apart: 29, of which 12 were waited for; matrix products, arithmetic and copies ran while one was open for 9% of the time, Pallas kernels for 23%

profile of v2, /device:TPU:0, one launch (start us, length us, event | category | flops | bytes accessed | tf_op | source)
XLA Modules:
  0.0 167.7 jit_solution(6545517667855846132)
XLA Ops:
  0.7 1.3 dynamic-slice_bitcast_fusion.1
  2.5 1.5 collective-permute-done
  4.2 3.0 %collective-permute-start.1 = (bf16[2,256,512]{2,1,0:T(8,128)(2,1)S(1)}, bf16[2,256,512]{2,1,0:T(8,128)(2,1)S(1)}, u32[]{:S(2)}, u32[]{:S(2)}) collective-permute-start(bf16[2,256,512]{2,1,0:T(8,128)(2,1)S(1)} %get-tuple-element.63.refs_0_), channel_id=1, source_target_pairs={{0,2},{1,3},{2,0},{3,1},{4,6},{5,7},{6,4},{7,5},{8,10},{9,11},{10,... | collective-permute-start | bytes 1572872 | tf_op jit(solution)/shard_map/gather0_e1/ppermute | solution.py:210
  7.4 0.6 collective-permute-start.4
  8.7 1.2 collective-permute-done.3
  10.0 9.5 %collective-permute-done.1.refs_1_ = bf16[2,256,512]{2,1,0:T(8,128)(2,1)S(1)} collective-permute-done((bf16[2,256,512]{2,1,0:T(8,128)(2,1)S(1)}, bf16[2,256,512]{2,1,0:T(8,128)(2,1)S(1)}, u32[]{:S(2)}, u32[]{:S(2)}) %collective-permute-start.1) | collective-permute-done | bytes 524320 | tf_op jit(solution)/shard_map/gather0_e1/ppermute | solution.py:210
  20.3 0.7 stack.39.meta
  21.1 1.5 collective-permute-start.6
  22.5 1.3 collective-permute-start.7
  23.8 0.7 maximum_bitcast_fusion.3.refs_14_
  24.5 0.7 maximum_bitcast_fusion.2.refs_14_
  25.2 0.6 slice.110.refs_12_
  25.9 0.8 maximum_bitcast_fusion.1.refs_13_
  26.7 0.8 maximum_bitcast_fusion.refs_13_
  27.5 13.5 %collective-permute-done.7.refs_3_ = bf16[2,256,512]{2,1,0:T(8,128)(2,1)S(1)} collective-permute-done((bf16[2,256,512]{2,1,0:T(8,128)(2,1)}, bf16[2,256,512]{2,1,0:T(8,128)(2,1)S(1)}, u32[]{:S(2)}, u32[]{:S(2)}) %collective-permute-start.7) | collective-permute-done | bytes 524320 | tf_op jit(solution)/shard_map/gather0_e2/ppermute | solution.py:210
  41.6 1.3 collective-permute-start.8
  43.4 0.7 all_to_all.14
  44.0 3.7 %all-to-all-start = ((s32[4,1,32]{2,1,0:T(1,128)}), s32[4,1,32]{2,1,0:T(1,128)S(1)}, u32[]{:S(2)}, u32[]{:S(2)}) async-start(s32[4,1,32]{2,1,0:T(1,128)} %bitcast.38), calls=%async_computation | async-start | bytes 4096 | tf_op jit(solution)/shard_map/all_to_all | solution.py:290
  47.8 0.7 copy.27.refs_15_
  48.4 0.7 copy.28.refs_15_
  49.1 3.3 %all-to-all-done = s32[4,1,32]{2,1,0:T(1,128)S(1)} async-done(((s32[4,1,32]{2,1,0:T(1,128)}), s32[4,1,32]{2,1,0:T(1,128)S(1)}, u32[]{:S(2)}, u32[]{:S(2)}) %all-to-all-start) | async-done | bytes 544 | tf_op jit(solution)/shard_map/all_to_all | solution.py:290
  52.9 0.6 reduce.3
  53.6 3.0 %collective-permute-done.8.refs_5_ = bf16[2,256,512]{2,1,0:T(8,128)(2,1)S(1)} collective-permute-done((bf16[2,256,512]{2,1,0:T(8,128)(2,1)}, bf16[2,256,512]{2,1,0:T(8,128)(2,1)S(1)}, u32[]{:S(2)}, u32[]{:S(2)}) %collective-permute-start.8) | collective-permute-done | bytes 524320 | tf_op jit(solution)/shard_map/gather0_e3/ppermute | solution.py:210
  56.7 1.6 collective-permute-start.12
  58.3 1.4 collective-permute-start.14
  59.7 1.3 collective-permute-start.15
  61.0 1.3 collective-permute-start.13
  62.4 19.1 %shard_map.121 = (f32[64,4096]{1,0:T(8,128)}, bf16[64,4096]{1,0:T(8,128)(2,1)}, bf16[64,4096]{1,0:T(8,128)(2,1)}, bf16[64,4096]{1,0:T(8,128)(2,1)}, bf16[2,32,4096]{2,1,0:T(8,128)(2,1)}) custom-call(s32[6]{0:T(128)} %stack.39.meta, bf16[2,256,512]{2,1,0:T(8,128)(2,1)} %copy-done.9, bf16[2,256,512]{2,1,0:T(8,128)(2,1)} %copy-done.19, ...), custom_call_target="tpu_custom_call" | custom-call | flops 21474836480 | bytes 4194304 | tf_op jit(solution)/shard_map/pallas_call | solution.py:164
  81.9 9.4 %collective-permute-done.13.refs_3_ = bf16[2,256,512]{2,1,0:T(8,128)(2,1)S(1)} collective-permute-done((bf16[2,256,512]{2,1,0:T(8,128)(2,1)S(1)}, bf16[2,256,512]{2,1,0:T(8,128)(2,1)S(1)}, u32[]{:S(2)}, u32[]{:S(2)}) %collective-permute-start.13) | collective-permute-done | bytes 524320 | tf_op jit(solution)/shard_map/gather1_e2/ppermute | solution.py:210
  91.3 0.8 copy-done.26
  92.5 1.4 collective-permute-start.18
  93.9 1.3 collective-permute-start.19
  95.2 5.7 %collective-permute-start.17 = (bf16[64,4096]{1,0:T(8,128)(2,1)}, bf16[64,4096]{1,0:T(8,128)(2,1)S(1)}, u32[]{:S(2)}, u32[]{:S(2)}) collective-permute-start(bf16[64,4096]{1,0:T(8,128)(2,1)} %get-tuple-element.104), channel_id=1, source_target_pairs={{0,2},{1,3},{6,4},{7,5},{8,10},{9,11},{14,12},{15,13},{16,18},{17,... | collective-permute-start | bytes 1572872 | tf_op jit(solution)/shard_map/sum0_mid_in/ppermute | solution.py:210
  101.0 19.0 %shard_map.122 = (f32[64,4096]{1,0:T(8,128)}, bf16[64,4096]{1,0:T(8,128)(2,1)}, bf16[64,4096]{1,0:T(8,128)(2,1)}, bf16[64,4096]{1,0:T(8,128)(2,1)}, bf16[2,32,4096]{2,1,0:T(8,128)(2,1)}) custom-call(s32[6]{0:T(128)} %stack.39.meta, bf16[2,256,512]{2,1,0:T(8,128)(2,1)} %copy-done.8, bf16[2,256,512]{2,1,0:T(8,128)(2,1)} %copy-done.23, ...), custom_call_target="tpu_custom_call" | custom-call | flops 21474836480 | bytes 4194304 | tf_op jit(solution)/shard_map/pallas_call | solution.py:164
  120.0 1.5 collective-permute-start.16
  122.5 7.3 %collective-permute-done.16 = bf16[64,4096]{1,0:T(8,128)(2,1)S(1)} collective-permute-done((bf16[64,4096]{1,0:T(8,128)(2,1)}, bf16[64,4096]{1,0:T(8,128)(2,1)S(1)}, u32[]{:S(2)}, u32[]{:S(2)}) %collective-permute-start.16) | collective-permute-done | bytes 524320 | tf_op jit(solution)/shard_map/sum1_far_in/ppermute | solution.py:210
  129.8 4.3 %collective-permute-start.24 = (bf16[64,4096]{1,0:T(8,128)(2,1)S(1)}, bf16[64,4096]{1,0:T(8,128)(2,1)S(1)}, u32[]{:S(2)}, u32[]{:S(2)}) collective-permute-start(bf16[64,4096]{1,0:T(8,128)(2,1)S(1)} %copy-done.3), channel_id=1, source_target_pairs={{0,2},{1,3},{6,4},{7,5},{8,10},{9,11},{14,12},{15,13},{16,18},{17,... | collective-permute-start | bytes 1572872 | tf_op jit(solution)/shard_map/sum1_mid_in/ppermute | solution.py:210
  134.4 1.4 convolution_convert_fusion
  135.9 10.6 %collective-permute-done.24 = bf16[64,4096]{1,0:T(8,128)(2,1)S(1)} collective-permute-done((bf16[64,4096]{1,0:T(8,128)(2,1)S(1)}, bf16[64,4096]{1,0:T(8,128)(2,1)S(1)}, u32[]{:S(2)}, u32[]{:S(2)}) %collective-permute-start.24) | collective-permute-done | bytes 524320 | tf_op jit(solution)/shard_map/sum1_mid_in/ppermute | solution.py:210
  146.6 3.9 %all-to-all-start.1 = ((bf16[4,32,4096]{2,1,0:T(8,128)(2,1)}), bf16[4,32,4096]{2,1,0:T(8,128)(2,1)S(1)}, u32[]{:S(2)}, u32[]{:S(2)}) async-start(bf16[4,32,4096]{2,1,0:T(8,128)(2,1)} %bitcast.45), calls=%async_computation.1 | async-start | bytes 2097152 | tf_op jit(solution)/shard_map/all_to_all | solution.py:374
  150.5 1.2 add_convert_fusion.2
  151.7 2.7 %collective-permute-start.23 = (bf16[64,4096]{1,0:T(8,128)(2,1)S(1)}, bf16[64,4096]{1,0:T(8,128)(2,1)S(1)}, u32[]{:S(2)}, u32[]{:S(2)}) collective-permute-start(bf16[64,4096]{1,0:T(8,128)(2,1)S(1)} %add_convert_fusion.2), channel_id=1, source_target_pairs={{0,2},{1,3},{2,0},{3,1},{4,6},{5,7},{6,4},{7,5},{8,10},{9,11},{10,... | collective-permute-start | bytes 1572872 | tf_op jit(solution)/shard_map/sum1_near/ppermute | solution.py:210
  154.4 3.4 %collective-permute-done.21 = bf16[64,4096]{1,0:T(8,128)(2,1)} collective-permute-done((bf16[64,4096]{1,0:T(8,128)(2,1)}, bf16[64,4096]{1,0:T(8,128)(2,1)}, u32[]{:S(2)}, u32[]{:S(2)}) %collective-permute-start.21) | collective-permute-done | bytes 524320 | tf_op jit(solution)/shard_map/sum0_near/ppermute | solution.py:210
  157.8 1.8 %fusion.3 = bf16[8,8,4096]{2,1,0:T(8,128)(2,1)S(1)} fusion(bf16[64,4096]{1,0:T(8,128)(2,1)} %copy-done.12, bf16[64,4096]{1,0:T(8,128)(2,1)} %copy-done.11, bf16[64,4096]{1,0:T(8,128)(2,1)} %copy-done.10, f32[64,4096]{1,0:T(8,128)S(1)} %copy-done.1, bf16[64,4096]{1,0:T(8,128)(2,1)} %collective-permute-done.21, pred[]{:T(512)S(6)} %or.3), kind=kLoop, calls=%fused_computation.12 | loop fusion | flops 2359296 | bytes 3670017 | tf_op jit(solution)/shard_map/reshape | solution.py:391
  159.6 4.1 %collective-permute-done.23 = bf16[64,4096]{1,0:T(8,128)(2,1)S(1)} collective-permute-done((bf16[64,4096]{1,0:T(8,128)(2,1)S(1)}, bf16[64,4096]{1,0:T(8,128)(2,1)S(1)}, u32[]{:S(2)}, u32[]{:S(2)}) %collective-permute-start.23) | collective-permute-done | bytes 524320 | tf_op jit(solution)/shard_map/sum1_near/ppermute | solution.py:210
  163.9 1.1 pad_maximum_fusion
  165.5 0.7 slice_add_fusion
  166.2 1.4 reshape.498
  (129 shorter events, 7.2 us)
Async XLA Ops:
  2.0 2.1 %collective-permute-start = (bf16[4,16,8,512]{3,2,1,0:T(8,128)(2,1)S(1)}, bf16[4,16,8,512]{3,2,1,0:T(8,128)(2,1)S(1)}, u32[]{:S(2)}, u32[]{:S(2)}) collective-permute-start(bf16[4,16,8,512]{3,2,1,0:T(8,128)(2,1)S(1)} %get-tuple-element.128), channel_id=1, source_target_pairs={{0,1},{1,0},{2,3},{3,2},{4,5},{5,4},{6,7},{7,6},{8,9},{9,8},{10,11... | collective-permute-start | bytes 1572872 | tf_op jit(solution)/shard_map/swap_tokens/ppermute | solution.py:210
  2.5 4.8 %copy-start.2 = (bf16[128,2,3,512]{3,1,2,0:T(2,128)(2,1)S(1)}, bf16[128,2,3,512]{3,1,2,0:T(2,128)(2,1)}, u32[]{:S(2)}) copy-start(bf16[128,2,3,512]{3,1,2,0:T(2,128)(2,1)} %param.16) | copy-start | bytes 2359300
  4.2 16.9 %copy-start.9 = (bf16[2,256,512]{2,1,0:T(8,128)(2,1)}, bf16[2,256,512]{2,1,0:T(8,128)(2,1)S(1)}, u32[]{:S(2)}) copy-start(bf16[2,256,512]{2,1,0:T(8,128)(2,1)S(1)} %get-tuple-element.63.refs_0_) | copy-start | bytes 1572868
  4.2 55.5 %copy-start.8 = (bf16[2,256,512]{2,1,0:T(8,128)(2,1)}, bf16[2,256,512]{2,1,0:T(8,128)(2,1)S(1)}, u32[]{:S(2)}) copy-start(bf16[2,256,512]{2,1,0:T(8,128)(2,1)S(1)} %get-tuple-element.91.refs_0_) | copy-start | bytes 1572868
  4.2 3.9 %copy-start.16 = (f32[512]{0:T(512)S(1)}, f32[512]{0:T(512)}, u32[]{:S(2)}) copy-start(f32[512]{0:T(512)} %param.14) | copy-start | bytes 6148
  4.2 15.8 %copy-start.17 = (s32[128]{0:T(128)S(1)}, s32[128]{0:T(128)}, u32[]{:S(2)}) copy-start(s32[128]{0:T(128)} %param.18) | copy-start | bytes 1540
  4.2 15.2 %collective-permute-start.1 = (bf16[2,256,512]{2,1,0:T(8,128)(2,1)S(1)}, bf16[2,256,512]{2,1,0:T(8,128)(2,1)S(1)}, u32[]{:S(2)}, u32[]{:S(2)}) collective-permute-start(bf16[2,256,512]{2,1,0:T(8,128)(2,1)S(1)} %get-tuple-element.63.refs_0_), channel_id=1, source_target_pairs={{0,2},{1,3},{2,0},{3,1},{4,6},{5,7},{6,4},{7,5},{8,10},{9,11},{10,... | collective-permute-start | bytes 1572872 | tf_op jit(solution)/shard_map/gather0_e1/ppermute | solution.py:210
  7.2 12.2 %collective-permute-start.2 = (bf16[2,256,512]{2,1,0:T(8,128)(2,1)S(1)}, bf16[2,256,512]{2,1,0:T(8,128)(2,1)}, u32[]{:S(2)}, u32[]{:S(2)}) collective-permute-start(bf16[2,256,512]{2,1,0:T(8,128)(2,1)S(1)} %get-tuple-element.63.refs_0_), channel_id=1, source_target_pairs={{2,4},{3,5},{4,2},{5,3},{0,1},{1,0},{6,7},{7,6},{10,12},{11,13},{1... | collective-permute-start | bytes 1572872 | tf_op jit(solution)/shard_map/gather0_m1/ppermute | solution.py:210
  7.4 2.5 %collective-permute-start.4 = (bf16[6,4,16,512]{3,2,1,0:T(8,128)(2,1)S(1)}, bf16[6,4,16,512]{3,2,1,0:T(8,128)(2,1)S(1)}, u32[]{:S(2)}, u32[]{:S(2)}) collective-permute-start(bf16[6,4,16,512]{3,2,1,0:T(8,128)(2,1)S(1)} %get-tuple-element.130), channel_id=1, source_target_pairs={{0,1},{1,0},{2,3},{3,2},{4,5},{5,4},{6,7},{7,6},{8,9},{9,8},{10,11... | collective-permute-start | bytes 1179656 | tf_op jit(solution)/shard_map/swap_tails/ppermute | solution.py:210
  8.0 1.9 %collective-permute-start.5 = (f32[4,16,512]{2,1,0:T(8,128)S(1)}, f32[4,16,512]{2,1,0:T(8,128)S(1)}, u32[]{:S(2)}, u32[]{:S(2)}) collective-permute-start(f32[4,16,512]{2,1,0:T(8,128)S(1)} %get-tuple-element.140), channel_id=1, source_target_pairs={{0,1},{1,0},{2,3},{3,2},{4,5},{5,4},{6,7},{7,6},{8,9},{9,8},{10,11... | collective-permute-start | bytes 393224 | tf_op jit(solution)/shard_map/swap_states/ppermute | solution.py:210
  8.2 1.8 %collective-permute-start.3 = (f32[10,512]{1,0:T(8,128)S(1)}, f32[10,512]{1,0:T(8,128)S(1)}, u32[]{:S(2)}, u32[]{:S(2)}) collective-permute-start(f32[10,512]{1,0:T(8,128)S(1)} %pad_maximum_fusion.4), channel_id=1, source_target_pairs={{0,1},{1,0},{2,3},{3,2},{4,5},{5,4},{6,7},{7,6},{8,9},{9,8},{10,11... | collective-permute-start | bytes 61448 | tf_op jit(solution)/shard_map/swap_taps/ppermute | solution.py:210
  19.5 8.0 %copy-start.19 = (bf16[2,256,512]{2,1,0:T(8,128)(2,1)}, bf16[2,256,512]{2,1,0:T(8,128)(2,1)S(1)}, u32[]{:S(2)}) copy-start(bf16[2,256,512]{2,1,0:T(8,128)(2,1)S(1)} %collective-permute-done.1.refs_1_) | copy-start | bytes 1572868
  19.5 42.8 %collective-permute-start.10 = (bf16[3,4096,512]{2,1,0:T(8,128)(2,1)}, bf16[3,4096,512]{2,1,0:T(8,128)(2,1)}, u32[]{:S(2)}, u32[]{:S(2)}) collective-permute-start(bf16[3,4096,512]{2,1,0:T(8,128)(2,1)} %bitcast.93), channel_id=1, source_target_pairs={{0,1},{1,0},{2,3},{3,2},{4,5},{5,4},{6,7},{7,6},{8,9},{9,8},{10,11... | collective-permute-start | bytes 37748744 | tf_op jit(solution)/shard_map/swap_w_in/ppermute | solution.py:210
  19.5 41.5 %collective-permute-start.11 = (bf16[512,4096]{1,0:T(8,128)(2,1)}, bf16[512,4096]{1,0:T(8,128)(2,1)}, u32[]{:S(2)}, u32[]{:S(2)}) collective-permute-start(bf16[512,4096]{1,0:T(8,128)(2,1)} %refs_8_.1), channel_id=1, source_target_pairs={{0,1},{1,0},{2,3},{3,2},{4,5},{5,4},{6,7},{7,6},{8,9},{9,8},{10,11... | collective-permute-start | bytes 12582920 | tf_op jit(solution)/shard_map/swap_w_out/ppermute | solution.py:210
  21.0 20.0 %copy-start.18 = (s32[128]{0:T(128)S(1)}, s32[128]{0:T(128)}, u32[]{:S(2)}) copy-start(s32[128]{0:T(128)} %param.19) | copy-start | bytes 1540
  21.1 6.4 %collective-permute-start.6 = (bf16[2,256,512]{2,1,0:T(8,128)(2,1)S(1)}, bf16[2,256,512]{2,1,0:T(8,128)(2,1)}, u32[]{:S(2)}, u32[]{:S(2)}) collective-permute-start(bf16[2,256,512]{2,1,0:T(8,128)(2,1)S(1)} %collective-permute-done.1.refs_1_), channel_id=1, source_target_pairs={{2,4},{3,5},{4,2},{5,3},{10,12},{11,13},{12,10},{13,11},{18,20},{1... | collective-permute-start | bytes 1572872 | tf_op jit(solution)/shard_map/gather0_m2/ppermute | solution.py:210
  22.5 18.5 %collective-permute-start.7 = (bf16[2,256,512]{2,1,0:T(8,128)(2,1)}, bf16[2,256,512]{2,1,0:T(8,128)(2,1)S(1)}, u32[]{:S(2)}, u32[]{:S(2)}) collective-permute-start(bf16[2,256,512]{2,1,0:T(8,128)(2,1)} %collective-permute-done.2.refs_2_), channel_id=1, source_target_pairs={{2,0},{3,1},{4,6},{5,7},{10,8},{11,9},{12,14},{13,15},{18,16},{19,... | collective-permute-start | bytes 1572872 | tf_op jit(solution)/shard_map/gather0_e2/ppermute | solution.py:210
  25.2 37.1 %copy-start.14 = (f32[10,2,512]{2,0,1:T(8,128)}, f32[10,2,512]{2,0,1:T(8,128)S(1)}, u32[]{:S(2)}) copy-start(f32[10,2,512]{2,0,1:T(8,128)S(1)} %copy.30) | copy-start | bytes 122884
  41.0 21.3 %copy-start.20 = (bf16[2,256,512]{2,1,0:T(8,128)(2,1)}, bf16[2,256,512]{2,1,0:T(8,128)(2,1)S(1)}, u32[]{:S(2)}) copy-start(bf16[2,256,512]{2,1,0:T(8,128)(2,1)S(1)} %collective-permute-done.7.refs_3_) | copy-start | bytes 1572868
  41.6 15.1 %collective-permute-start.8 = (bf16[2,256,512]{2,1,0:T(8,128)(2,1)}, bf16[2,256,512]{2,1,0:T(8,128)(2,1)S(1)}, u32[]{:S(2)}, u32[]{:S(2)}) collective-permute-start(bf16[2,256,512]{2,1,0:T(8,128)(2,1)} %collective-permute-done.6.refs_4_), channel_id=1, source_target_pairs={{2,0},{3,1},{4,6},{5,7},{10,8},{11,9},{12,14},{13,15},{18,16},{19,... | collective-permute-start | bytes 1572872 | tf_op jit(solution)/shard_map/gather0_e3/ppermute | solution.py:210
  42.9 13.8 %collective-permute-start.9 = (bf16[2,256,512]{2,1,0:T(8,128)(2,1)S(1)}, bf16[2,256,512]{2,1,0:T(8,128)(2,1)S(1)}, u32[]{:S(2)}, u32[]{:S(2)}) collective-permute-start(bf16[2,256,512]{2,1,0:T(8,128)(2,1)S(1)} %get-tuple-element.91.refs_0_), channel_id=1, source_target_pairs={{2,4},{3,5},{4,2},{5,3},{0,1},{1,0},{6,7},{7,6},{10,12},{11,13},{1... | collective-permute-start | bytes 1572872 | tf_op jit(solution)/shard_map/gather1_m1/ppermute | solution.py:210
  44.0 8.4 %all-to-all-start = ((s32[4,1,32]{2,1,0:T(1,128)}), s32[4,1,32]{2,1,0:T(1,128)S(1)}, u32[]{:S(2)}, u32[]{:S(2)}) async-start(s32[4,1,32]{2,1,0:T(1,128)} %bitcast.38), calls=%async_computation | async-start | bytes 4096 | tf_op jit(solution)/shard_map/all_to_all | solution.py:290
  56.7 5.7 %copy-start.22 = (bf16[2,256,512]{2,1,0:T(8,128)(2,1)}, bf16[2,256,512]{2,1,0:T(8,128)(2,1)S(1)}, u32[]{:S(2)}) copy-start(bf16[2,256,512]{2,1,0:T(8,128)(2,1)S(1)} %collective-permute-done.8.refs_5_) | copy-start | bytes 1572868
  56.7 24.8 %copy-start.21 = (bf16[2,256,512]{2,1,0:T(8,128)(2,1)}, bf16[2,256,512]{2,1,0:T(8,128)(2,1)S(1)}, u32[]{:S(2)}) copy-start(bf16[2,256,512]{2,1,0:T(8,128)(2,1)S(1)} %collective-permute-done.9.refs_2_) | copy-start | bytes 1572868
  56.7 25.2 %collective-permute-start.12 = (bf16[2,256,512]{2,1,0:T(8,128)(2,1)S(1)}, bf16[2,256,512]{2,1,0:T(8,128)(2,1)S(1)}, u32[]{:S(2)}, u32[]{:S(2)}) collective-permute-start(bf16[2,256,512]{2,1,0:T(8,128)(2,1)S(1)} %get-tuple-element.91.refs_0_), channel_id=1, source_target_pairs={{0,2},{1,3},{2,0},{3,1},{4,6},{5,7},{6,4},{7,5},{8,10},{9,11},{10,... | collective-permute-start | bytes 1572872 | tf_op jit(solution)/shard_map/gather1_e1/ppermute | solution.py:210
  58.3 32.9 %collective-permute-start.14 = (bf16[2,256,512]{2,1,0:T(8,128)(2,1)S(1)}, bf16[2,256,512]{2,1,0:T(8,128)(2,1)S(1)}, u32[]{:S(2)}, u32[]{:S(2)}) collective-permute-start(bf16[2,256,512]{2,1,0:T(8,128)(2,1)S(1)} %get-tuple-element.91.refs_0_), channel_id=1, source_target_pairs={{0,6},{1,7},{6,0},{7,1},{2,3},{3,2},{4,5},{5,4},{8,14},{9,15},{14,... | collective-permute-start | bytes 1572872 | tf_op jit(solution)/shard_map/gather1_across/ppermute | solution.py:210
  59.7 31.6 %collective-permute-start.15 = (bf16[2,256,512]{2,1,0:T(8,128)(2,1)S(1)}, bf16[2,256,512]{2,1,0:T(8,128)(2,1)S(1)}, u32[]{:S(2)}, u32[]{:S(2)}) collective-permute-start(bf16[2,256,512]{2,1,0:T(8,128)(2,1)S(1)} %get-tuple-element.91.refs_0_), channel_id=1, source_target_pairs={{0,4},{1,5},{6,2},{7,3},{8,12},{9,13},{14,10},{15,11},{16,20},{17,... | collective-permute-start | bytes 1572872 | tf_op jit(solution)/shard_map/gather1_skip/ppermute | solution.py:210
  61.0 30.2 %collective-permute-start.13 = (bf16[2,256,512]{2,1,0:T(8,128)(2,1)S(1)}, bf16[2,256,512]{2,1,0:T(8,128)(2,1)S(1)}, u32[]{:S(2)}, u32[]{:S(2)}) collective-permute-start(bf16[2,256,512]{2,1,0:T(8,128)(2,1)S(1)} %collective-permute-done.9.refs_2_), channel_id=1, source_target_pairs={{2,0},{3,1},{4,6},{5,7},{10,8},{11,9},{12,14},{13,15},{18,16},{19,... | collective-permute-start | bytes 1572872 | tf_op jit(solution)/shard_map/gather1_e2/ppermute | solution.py:210
  81.9 19.1 %copy-start.23 = (bf16[2,256,512]{2,1,0:T(8,128)(2,1)}, bf16[2,256,512]{2,1,0:T(8,128)(2,1)S(1)}, u32[]{:S(2)}) copy-start(bf16[2,256,512]{2,1,0:T(8,128)(2,1)S(1)} %collective-permute-done.12.refs_1_) | copy-start | bytes 1572868
  92.5 28.9 %copy-start.6 = (bf16[2,32,4096]{2,1,0:T(8,128)(2,1)S(1)}, bf16[2,32,4096]{2,1,0:T(8,128)(2,1)}, u32[]{:S(2)}) copy-start(bf16[2,32,4096]{2,1,0:T(8,128)(2,1)} %get-tuple-element.118) | copy-start | bytes 1572868
  92.5 29.0 %copy-start.4 = (bf16[64,4096]{1,0:T(8,128)(2,1)S(1)}, bf16[64,4096]{1,0:T(8,128)(2,1)}, u32[]{:S(2)}) copy-start(bf16[64,4096]{1,0:T(8,128)(2,1)} %get-tuple-element.104) | copy-start | bytes 1572868
  92.5 29.0 %collective-permute-start.18 = (bf16[64,4096]{1,0:T(8,128)(2,1)}, bf16[64,4096]{1,0:T(8,128)(2,1)S(1)}, u32[]{:S(2)}, u32[]{:S(2)}) collective-permute-start(bf16[64,4096]{1,0:T(8,128)(2,1)} %get-tuple-element.107), channel_id=1, source_target_pairs={{0,6},{1,7},{6,0},{7,1},{2,3},{3,2},{4,5},{5,4},{8,14},{9,15},{14,... | collective-permute-start | bytes 1572872 | tf_op jit(solution)/shard_map/sum0_across/ppermute | solution.py:210
  93.9 27.6 %collective-permute-start.19 = (bf16[64,4096]{1,0:T(8,128)(2,1)}, bf16[64,4096]{1,0:T(8,128)(2,1)S(1)}, u32[]{:S(2)}, u32[]{:S(2)}) collective-permute-start(bf16[64,4096]{1,0:T(8,128)(2,1)} %get-tuple-element.107), channel_id=1, source_target_pairs={{4,0},{5,1},{2,6},{3,7},{12,8},{13,9},{10,14},{11,15},{20,16},{21,... | collective-permute-start | bytes 1572872 | tf_op jit(solution)/shard_map/sum0_skip/ppermute | solution.py:210
  95.2 26.3 %collective-permute-start.17 = (bf16[64,4096]{1,0:T(8,128)(2,1)}, bf16[64,4096]{1,0:T(8,128)(2,1)S(1)}, u32[]{:S(2)}, u32[]{:S(2)}) collective-permute-start(bf16[64,4096]{1,0:T(8,128)(2,1)} %get-tuple-element.104), channel_id=1, source_target_pairs={{0,2},{1,3},{6,4},{7,5},{8,10},{9,11},{14,12},{15,13},{16,18},{17,... | collective-permute-start | bytes 1572872 | tf_op jit(solution)/shard_map/sum0_mid_in/ppermute | solution.py:210
  120.0 9.8 %collective-permute-start.16 = (bf16[64,4096]{1,0:T(8,128)(2,1)}, bf16[64,4096]{1,0:T(8,128)(2,1)S(1)}, u32[]{:S(2)}, u32[]{:S(2)}) collective-permute-start(bf16[64,4096]{1,0:T(8,128)(2,1)} %get-tuple-element.103), channel_id=1, source_target_pairs={{0,2},{1,3},{6,4},{7,5},{8,10},{9,11},{14,12},{15,13},{16,18},{17,... | collective-permute-start | bytes 1572872 | tf_op jit(solution)/shard_map/sum1_far_in/ppermute | solution.py:210
  121.5 8.3 %copy-start.3 = (bf16[64,4096]{1,0:T(8,128)(2,1)S(1)}, bf16[64,4096]{1,0:T(8,128)(2,1)}, u32[]{:S(2)}) copy-start(bf16[64,4096]{1,0:T(8,128)(2,1)} %get-tuple-element.116) | copy-start | bytes 1572868
  121.5 12.6 %copy-start.5 = (bf16[64,4096]{1,0:T(8,128)(2,1)S(1)}, bf16[64,4096]{1,0:T(8,128)(2,1)}, u32[]{:S(2)}) copy-start(bf16[64,4096]{1,0:T(8,128)(2,1)} %get-tuple-element.103) | copy-start | bytes 1572868
  121.7 8.1 %collective-permute-start.20 = (bf16[64,4096]{1,0:T(8,128)(2,1)S(1)}, bf16[64,4096]{1,0:T(8,128)(2,1)S(1)}, u32[]{:S(2)}, u32[]{:S(2)}) collective-permute-start(bf16[64,4096]{1,0:T(8,128)(2,1)S(1)} %add_convert_fusion.5), channel_id=1, source_target_pairs={{2,4},{3,5},{4,2},{5,3},{0,1},{1,0},{6,7},{7,6},{10,12},{11,13},{1... | collective-permute-start | bytes 1572872 | tf_op jit(solution)/shard_map/sum0_mid_on/ppermute | solution.py:210
  122.5 11.9 %collective-permute-start.25 = (bf16[64,4096]{1,0:T(8,128)(2,1)S(1)}, bf16[64,4096]{1,0:T(8,128)(2,1)S(1)}, u32[]{:S(2)}, u32[]{:S(2)}) collective-permute-start(bf16[64,4096]{1,0:T(8,128)(2,1)S(1)} %get-tuple-element.126), channel_id=1, source_target_pairs={{0,1},{1,0},{2,3},{3,2},{4,5},{5,4},{6,7},{7,6},{8,9},{9,8},{10,11... | collective-permute-start | bytes 1572872 | tf_op jit(solution)/shard_map/swap_commit/ppermute | solution.py:210
  129.8 16.8 %copy-start.12 = (bf16[64,4096]{1,0:T(8,128)(2,1)}, bf16[64,4096]{1,0:T(8,128)(2,1)S(1)}, u32[]{:S(2)}) copy-start(bf16[64,4096]{1,0:T(8,128)(2,1)S(1)} %collective-permute-done.20) | copy-start | bytes 1572868
  129.8 16.7 %collective-permute-start.24 = (bf16[64,4096]{1,0:T(8,128)(2,1)S(1)}, bf16[64,4096]{1,0:T(8,128)(2,1)S(1)}, u32[]{:S(2)}, u32[]{:S(2)}) collective-permute-start(bf16[64,4096]{1,0:T(8,128)(2,1)S(1)} %copy-done.3), channel_id=1, source_target_pairs={{0,2},{1,3},{6,4},{7,5},{8,10},{9,11},{14,12},{15,13},{16,18},{17,... | collective-permute-start | bytes 1572872 | tf_op jit(solution)/shard_map/sum1_mid_in/ppermute | solution.py:210
  134.1 23.7 %collective-permute-start.21 = (bf16[64,4096]{1,0:T(8,128)(2,1)}, bf16[64,4096]{1,0:T(8,128)(2,1)}, u32[]{:S(2)}, u32[]{:S(2)}) collective-permute-start(bf16[64,4096]{1,0:T(8,128)(2,1)} %get-tuple-element.109), channel_id=1, source_target_pairs={{0,2},{1,3},{2,0},{3,1},{4,6},{5,7},{6,4},{7,5},{8,10},{9,11},{10,... | collective-permute-start | bytes 1572872 | tf_op jit(solution)/shard_map/sum0_near/ppermute | solution.py:210
  134.3 16.1 %collective-permute-start.22 = (bf16[64,4096]{1,0:T(8,128)(2,1)S(1)}, bf16[64,4096]{1,0:T(8,128)(2,1)}, u32[]{:S(2)}, u32[]{:S(2)}) collective-permute-start(bf16[64,4096]{1,0:T(8,128)(2,1)S(1)} %add_convert_fusion.3), channel_id=1, source_target_pairs={{2,4},{3,5},{4,2},{5,3},{0,1},{1,0},{6,7},{7,6},{10,12},{11,13},{1... | collective-permute-start | bytes 1572872 | tf_op jit(solution)/shard_map/sum1_far_on/ppermute | solution.py:210
  146.6 11.2 %copy-start.1 = (f32[64,4096]{1,0:T(8,128)S(1)}, f32[64,4096]{1,0:T(8,128)}, u32[]{:S(2)}) copy-start(f32[64,4096]{1,0:T(8,128)} %get-tuple-element.89) | copy-start | bytes 3145732
  146.6 18.4 %all-to-all-start.1 = ((bf16[4,32,4096]{2,1,0:T(8,128)(2,1)}), bf16[4,32,4096]{2,1,0:T(8,128)(2,1)S(1)}, u32[]{:S(2)}, u32[]{:S(2)}) async-start(bf16[4,32,4096]{2,1,0:T(8,128)(2,1)} %bitcast.45), calls=%async_computation.1 | async-start | bytes 2097152 | tf_op jit(solution)/shard_map/all_to_all | solution.py:374
  151.7 12.1 %copy-start = (f32[64,4096]{1,0:T(8,128)S(1)}, f32[64,4096]{1,0:T(8,128)}, u32[]{:S(2)}) copy-start(f32[64,4096]{1,0:T(8,128)} %get-tuple-element.113) | copy-start | bytes 3145732
  151.7 12.0 %collective-permute-start.23 = (bf16[64,4096]{1,0:T(8,128)(2,1)S(1)}, bf16[64,4096]{1,0:T(8,128)(2,1)S(1)}, u32[]{:S(2)}, u32[]{:S(2)}) collective-permute-start(bf16[64,4096]{1,0:T(8,128)(2,1)S(1)} %add_convert_fusion.2), channel_id=1, source_target_pairs={{0,2},{1,3},{2,0},{3,1},{4,6},{5,7},{6,4},{7,5},{8,10},{9,11},{10,... | collective-permute-start | bytes 1572872 | tf_op jit(solution)/shard_map/sum1_near/ppermute | solution.py:210
  154.4 9.3 %collective-permute-start.26 = (bf16[64,4096]{1,0:T(8,128)(2,1)S(1)}, bf16[64,4096]{1,0:T(8,128)(2,1)S(1)}, u32[]{:S(2)}, u32[]{:S(2)}) collective-permute-start(bf16[64,4096]{1,0:T(8,128)(2,1)S(1)} %add_convert_fusion.1), channel_id=1, source_target_pairs={{2,4},{3,5},{4,2},{5,3},{0,1},{1,0},{6,7},{7,6},{10,12},{11,13},{1... | collective-permute-start | bytes 1572872 | tf_op jit(solution)/shard_map/sum1_mid_on/ppermute | solution.py:210
  (8 other events, 14.2 us)

commit v3 on v2

--- a/solution.py
+++ b/solution.py
@@ -19,9 +19,8 @@
     pieces = [refs[sum(choices[:k]):sum(choices[:k + 1])] for k in range(nz)]
     (w_own, w_sib, o_own, o_sib, gain, taps, decay, tails, states, accepted) = refs[n_in:n_in + 10]
     outs = refs[n_in + 10:]
-    terms = outs[:nz]
-    commit = outs[nz]
-    xs, ns, wbuf, wob, br, gf, gs, pf, xsem, wsem, osem = outs[nz + 1:]
+    terms_out, commit_out = outs[:nz], outs[nz]
+    xs, ns, wbuf, wob, br, gf, gs, pf, own, rest, commit, xsem, wsem, osem, tsem, csem = outs[nz + 1:]
     is_end, core = meta[0], meta[1]
     tokens = rows * steps
     unit = share_rows * steps
@@ -129,10 +128,12 @@
         for lane in range(block // 128):
             gs[block_index, :, pl.ds(lane * 128, 128)] = gf[lane].astype(jnp.bfloat16)
 
+    commit_copy = pltpu.make_async_copy(commit, commit_out, csem)
+    commit_copy.start()
     for number in range(12, 16):
         take(number)
     gated = jnp.concatenate([gs[b] for b in range(2)], axis=1)
-    wide_out = 512
+    wide_out, sent = 512, []
     for at in range(0, width, wide_out):
         columns = pl.ds(at, wide_out)
         pf[...] = jnp.dot(gated, wob[:, columns], preferred_element_type=jnp.float32)
@@ -140,9 +141,20 @@
             picked = pl.ds(pl.multiple_of(meta[2 + slot] * unit, 16), unit)
             value = pf[picked, :]
             if slot == 0:
-                terms[slot][:, columns] = value + xs[picked, columns].astype(jnp.float32)
+                own[:, columns] = value + xs[picked, columns].astype(jnp.float32)
             else:
-                terms[slot][:, columns] = value.astype(jnp.bfloat16)
+                rest[slot - 1, :, columns] = value.astype(jnp.bfloat16)
+        if (at + wide_out) % (width // 2) == 0:
+            part = at // (width // 2)
+            half = pl.ds(part * (width // 2), width // 2)
+            for slot in range(nz):
+                src = own if slot == 0 else rest.at[slot - 1]
+                copy = pltpu.make_async_copy(src.at[:, half], terms_out[slot].at[:, half], tsem.at[part, slot])
+                copy.start()
+                sent.append(copy)
+    for copy in sent:
+        copy.wait()
+    commit_copy.wait()
 
 
 def run_chunk(nz, meta, slots, w_own, w_sib, o_own, o_sib, gain, taps, decay, tails, states, accepted, steps, share_rows, taps_n, tail_len):
@@ -167,7 +179,7 @@
         ),
         out_shape=out_shape,
         in_specs=[pl.BlockSpec(memory_space=pltpu.SMEM)] + [anywhere] * (len(pieces) + 4) + [vmem] * 6,
-        out_specs=[vmem] * len(out_shape),
+        out_specs=[anywhere] * len(out_shape),
         scratch_shapes=[
             pltpu.VMEM((tokens, width), jnp.bfloat16),
             pltpu.VMEM((tokens, width), jnp.bfloat16),
@@ -177,9 +189,14 @@
             pltpu.VMEM((block // 128, tokens, 128), jnp.float32),
             pltpu.VMEM((blocks, tokens, block), jnp.bfloat16),
             pltpu.VMEM((tokens, 512), jnp.float32),
+            pltpu.VMEM((unit, width), jnp.float32),
+            pltpu.VMEM((nz - 1, unit, width), jnp.bfloat16),
+            pltpu.VMEM(out_shape[-1].shape, jnp.bfloat16),
             pltpu.SemaphoreType.DMA((nz, 2)),
             pltpu.SemaphoreType.DMA((12,)),
             pltpu.SemaphoreType.DMA((4,)),
+            pltpu.SemaphoreType.DMA((2, nz)),
+            pltpu.SemaphoreType.DMA,
         ],
         compiler_params=pltpu.CompilerParams(vmem_limit_bytes=58 * 1024 * 1024),
         cost_estimate=pl.CostEstimate(
@@ -332,13 +349,13 @@
     if line:
         e2 = permute(m1, outward, "gather0_e2")
         m2 = permute(e1, between, "gather0_m2")
-        m2, e2, x1, sides, taps_all, decay_all, meta, owner_map = barrier(
-            (m2, e2, x1, sides, taps_all, decay_all, meta, owner_map)
+        m2, x1, sides, taps_all, decay_all, meta, owner_map = barrier(
+            (m2, x1, sides, taps_all, decay_all, meta, owner_map)
         )
         pick, put = commit_order(owner_map)
         e3 = permute(m2, outward, "gather0_e3")
         g1 = permute(x1, middle, "gather1_m1")
-        e3, g1, x1, pick, put = barrier((e3, g1, x1, pick, put))
+        e2, e3, g1, x1, pick, put = barrier((e2, e3, g1, x1, pick, put))
         f1 = permute(x1, ends, "gather1_e1")
         g2, f3 = permute(x1, skip_in, "gather1_skip"), permute(x1, across, "gather1_across")
         f2 = permute(g1, outward, "gather1_e2")

time: 168 us -> 167 us (level)
  transfers between devices with their start and end apart: 29 -> 29, of which waited for: 12 -> 11; matrix products, arithmetic and copies ran while one was open for 9% -> 9% of each run, Pallas kernels for 23% -> 22%
where the time goes in v3:
time: 167 us
  waiting for transfers between devices  66.2 us (40%)
  starting transfers between devices  40.6 us (24%)
  Pallas kernels  37 us (22%)
  local copies, waits for them, and re-layouts  10.1 us (6%)
  other arithmetic  9.46 us (6%)
  matrix products  1.86 us (1%)
    ppermute x27, waiting for transfers between devices, permute(): return lax.ppermute(value, 'tensor', links)  62.9 us
    pallas_call x2, Pallas kernels, run_chunk(): pl.pallas_call(functools.partial(chunk_kernel, nz, choices, tail_len, tap...  37 us
    ppermute x27, starting transfers between devices, permute(): return lax.ppermute(value, 'tensor', links)  32.9 us
    all_to_all x1, starting transfers between devices, commit_order(): lax.all_to_all(slot_out.reshape(n_dp, sends), 'dp', split_axis=0, concat_...  3.88 us
    all_to_all x1, starting transfers between devices, per_device(): got = lax.all_to_all(sent, 'dp', split_axis=0, concat_axis=0, tiled=True)  3.86 us
  transfers between devices with their start and end apart: 29, of which 11 were waited for; matrix products, arithmetic and copies ran while one was open for 9% of the time, Pallas kernels for 22%

profile of v3, /device:TPU:0, one launch (start us, length us, event | category | flops | bytes accessed | tf_op | source)
XLA Modules:
  0.0 166.5 jit_solution(16336867559326235863)
XLA Ops:
  0.7 1.3 dynamic-slice_bitcast_fusion.1
  2.5 1.5 collective-permute-done
  4.2 3.0 %collective-permute-start.1 = (bf16[2,256,512]{2,1,0:T(8,128)(2,1)S(1)}, bf16[2,256,512]{2,1,0:T(8,128)(2,1)S(1)}, u32[]{:S(2)}, u32[]{:S(2)}) collective-permute-start(bf16[2,256,512]{2,1,0:T(8,128)(2,1)S(1)} %get-tuple-element.63.refs_0_), channel_id=1, source_target_pairs={{0,2},{1,3},{2,0},{3,1},{4,6},{5,7},{6,4},{7,5},{8,10},{9,11},{10,... | collective-permute-start | bytes 1572872 | tf_op jit(solution)/shard_map/gather0_e1/ppermute | solution.py:227
  7.4 0.6 collective-permute-start.4
  8.7 1.2 collective-permute-done.3
  10.0 9.5 %collective-permute-done.1.refs_1_ = bf16[2,256,512]{2,1,0:T(8,128)(2,1)S(1)} collective-permute-done((bf16[2,256,512]{2,1,0:T(8,128)(2,1)S(1)}, bf16[2,256,512]{2,1,0:T(8,128)(2,1)S(1)}, u32[]{:S(2)}, u32[]{:S(2)}) %collective-permute-start.1) | collective-permute-done | bytes 524320 | tf_op jit(solution)/shard_map/gather0_e1/ppermute | solution.py:227
  20.3 0.7 stack.39.meta
  21.2 0.6 slice.110.refs_12_
  21.8 0.7 collective-permute-start.6
  22.5 1.3 collective-permute-start.7
  23.8 0.7 maximum_bitcast_fusion.3.refs_14_
  24.5 0.7 maximum_bitcast_fusion.2.refs_14_
  25.1 0.8 maximum_bitcast_fusion.1.refs_13_
  26.0 0.8 maximum_bitcast_fusion.refs_13_
  27.3 1.3 collective-permute-start.8
  29.2 0.7 all_to_all.14
  29.8 3.9 %all-to-all-start = ((s32[4,1,32]{2,1,0:T(1,128)}), s32[4,1,32]{2,1,0:T(1,128)S(1)}, u32[]{:S(2)}, u32[]{:S(2)}) async-start(s32[4,1,32]{2,1,0:T(1,128)} %bitcast.38), calls=%async_computation | async-start | bytes 4096 | tf_op jit(solution)/shard_map/all_to_all | solution.py:307
  33.7 0.7 copy.27.refs_15_
  34.4 0.7 copy.28.refs_15_
  35.1 3.3 %all-to-all-done = s32[4,1,32]{2,1,0:T(1,128)S(1)} async-done(((s32[4,1,32]{2,1,0:T(1,128)}), s32[4,1,32]{2,1,0:T(1,128)S(1)}, u32[]{:S(2)}, u32[]{:S(2)}) %all-to-all-start) | async-done | bytes 544 | tf_op jit(solution)/shard_map/all_to_all | solution.py:307
  38.9 0.6 reduce.3
  39.6 2.2 %collective-permute-done.7.refs_3_ = bf16[2,256,512]{2,1,0:T(8,128)(2,1)} collective-permute-done((bf16[2,256,512]{2,1,0:T(8,128)(2,1)}, bf16[2,256,512]{2,1,0:T(8,128)(2,1)}, u32[]{:S(2)}, u32[]{:S(2)}) %collective-permute-start.7) | collective-permute-done | bytes 524320 | tf_op jit(solution)/shard_map/gather0_e2/ppermute | solution.py:227
  41.8 11.8 %collective-permute-done.8.refs_5_ = bf16[2,256,512]{2,1,0:T(8,128)(2,1)S(1)} collective-permute-done((bf16[2,256,512]{2,1,0:T(8,128)(2,1)S(1)}, bf16[2,256,512]{2,1,0:T(8,128)(2,1)S(1)}, u32[]{:S(2)}, u32[]{:S(2)}) %collective-permute-start.8) | collective-permute-done | bytes 524320 | tf_op jit(solution)/shard_map/gather0_e3/ppermute | solution.py:227
  53.6 1.9 %collective-permute-start.12 = (bf16[2,256,512]{2,1,0:T(8,128)(2,1)S(1)}, bf16[2,256,512]{2,1,0:T(8,128)(2,1)S(1)}, u32[]{:S(2)}, u32[]{:S(2)}) collective-permute-start(bf16[2,256,512]{2,1,0:T(8,128)(2,1)S(1)} %get-tuple-element.91.refs_0_), channel_id=1, source_target_pairs={{0,2},{1,3},{2,0},{3,1},{4,6},{5,7},{6,4},{7,5},{8,10},{9,11},{10,... | collective-permute-start | bytes 1572872 | tf_op jit(solution)/shard_map/gather1_e1/ppermute | solution.py:227
  55.4 2.6 %collective-permute-start.14 = (bf16[2,256,512]{2,1,0:T(8,128)(2,1)S(1)}, bf16[2,256,512]{2,1,0:T(8,128)(2,1)S(1)}, u32[]{:S(2)}, u32[]{:S(2)}) collective-permute-start(bf16[2,256,512]{2,1,0:T(8,128)(2,1)S(1)} %get-tuple-element.91.refs_0_), channel_id=1, source_target_pairs={{0,6},{1,7},{6,0},{7,1},{2,3},{3,2},{4,5},{5,4},{8,14},{9,15},{14,... | collective-permute-start | bytes 1572872 | tf_op jit(solution)/shard_map/gather1_across/ppermute | solution.py:227
  58.1 1.3 collective-permute-start.15
  59.4 1.3 collective-permute-start.13
  60.7 18.5 %shard_map.121 = (f32[64,4096]{1,0:T(8,128)}, bf16[64,4096]{1,0:T(8,128)(2,1)}, bf16[64,4096]{1,0:T(8,128)(2,1)}, bf16[64,4096]{1,0:T(8,128)(2,1)}, bf16[2,32,4096]{2,1,0:T(8,128)(2,1)}) custom-call(s32[6]{0:T(128)} %stack.39.meta, bf16[2,256,512]{2,1,0:T(8,128)(2,1)} %copy-done.9, bf16[2,256,512]{2,1,0:T(8,128)(2,1)} %copy-done.19, ...), custom_call_target="tpu_custom_call" | custom-call | flops 21474836480 | bytes 4194304 | tf_op jit(solution)/shard_map/pallas_call | solution.py:176
  79.3 9.2 %collective-permute-done.13.refs_3_ = bf16[2,256,512]{2,1,0:T(8,128)(2,1)S(1)} collective-permute-done((bf16[2,256,512]{2,1,0:T(8,128)(2,1)S(1)}, bf16[2,256,512]{2,1,0:T(8,128)(2,1)S(1)}, u32[]{:S(2)}, u32[]{:S(2)}) %collective-permute-start.13) | collective-permute-done | bytes 524320 | tf_op jit(solution)/shard_map/gather1_e2/ppermute | solution.py:227
  88.5 0.8 copy-done.26
  89.7 2.6 %collective-permute-start.18 = (bf16[64,4096]{1,0:T(8,128)(2,1)}, bf16[64,4096]{1,0:T(8,128)(2,1)S(1)}, u32[]{:S(2)}, u32[]{:S(2)}) collective-permute-start(bf16[64,4096]{1,0:T(8,128)(2,1)} %get-tuple-element.107), channel_id=1, source_target_pairs={{0,6},{1,7},{6,0},{7,1},{2,3},{3,2},{4,5},{5,4},{8,14},{9,15},{14,... | collective-permute-start | bytes 1572872 | tf_op jit(solution)/shard_map/sum0_across/ppermute | solution.py:227
  92.3 1.3 collective-permute-start.19
  93.6 4.5 %collective-permute-start.17 = (bf16[64,4096]{1,0:T(8,128)(2,1)}, bf16[64,4096]{1,0:T(8,128)(2,1)S(1)}, u32[]{:S(2)}, u32[]{:S(2)}) collective-permute-start(bf16[64,4096]{1,0:T(8,128)(2,1)} %get-tuple-element.104), channel_id=1, source_target_pairs={{0,2},{1,3},{6,4},{7,5},{8,10},{9,11},{14,12},{15,13},{16,18},{17,... | collective-permute-start | bytes 1572872 | tf_op jit(solution)/shard_map/sum0_mid_in/ppermute | solution.py:227
  98.2 18.5 %shard_map.122 = (f32[64,4096]{1,0:T(8,128)}, bf16[64,4096]{1,0:T(8,128)(2,1)}, bf16[64,4096]{1,0:T(8,128)(2,1)}, bf16[64,4096]{1,0:T(8,128)(2,1)}, bf16[2,32,4096]{2,1,0:T(8,128)(2,1)}) custom-call(s32[6]{0:T(128)} %stack.39.meta, bf16[2,256,512]{2,1,0:T(8,128)(2,1)} %copy-done.8, bf16[2,256,512]{2,1,0:T(8,128)(2,1)} %copy-done.23, ...), custom_call_target="tpu_custom_call" | custom-call | flops 21474836480 | bytes 4194304 | tf_op jit(solution)/shard_map/pallas_call | solution.py:176
  116.7 1.5 collective-permute-start.16
  119.2 8.4 %collective-permute-done.16 = bf16[64,4096]{1,0:T(8,128)(2,1)S(1)} collective-permute-done((bf16[64,4096]{1,0:T(8,128)(2,1)}, bf16[64,4096]{1,0:T(8,128)(2,1)S(1)}, u32[]{:S(2)}, u32[]{:S(2)}) %collective-permute-start.16) | collective-permute-done | bytes 524320 | tf_op jit(solution)/shard_map/sum1_far_in/ppermute | solution.py:227
  127.6 4.3 %collective-permute-start.24 = (bf16[64,4096]{1,0:T(8,128)(2,1)S(1)}, bf16[64,4096]{1,0:T(8,128)(2,1)S(1)}, u32[]{:S(2)}, u32[]{:S(2)}) collective-permute-start(bf16[64,4096]{1,0:T(8,128)(2,1)S(1)} %copy-done.3), channel_id=1, source_target_pairs={{0,2},{1,3},{6,4},{7,5},{8,10},{9,11},{14,12},{15,13},{16,18},{17,... | collective-permute-start | bytes 1572872 | tf_op jit(solution)/shard_map/sum1_mid_in/ppermute | solution.py:227
  132.2 1.4 convolution_convert_fusion
  133.6 10.6 %collective-permute-done.24 = bf16[64,4096]{1,0:T(8,128)(2,1)S(1)} collective-permute-done((bf16[64,4096]{1,0:T(8,128)(2,1)S(1)}, bf16[64,4096]{1,0:T(8,128)(2,1)S(1)}, u32[]{:S(2)}, u32[]{:S(2)}) %collective-permute-start.24) | collective-permute-done | bytes 524320 | tf_op jit(solution)/shard_map/sum1_mid_in/ppermute | solution.py:227
  144.4 3.9 %all-to-all-start.1 = ((bf16[4,32,4096]{2,1,0:T(8,128)(2,1)}), bf16[4,32,4096]{2,1,0:T(8,128)(2,1)S(1)}, u32[]{:S(2)}, u32[]{:S(2)}) async-start(bf16[4,32,4096]{2,1,0:T(8,128)(2,1)} %bitcast.45), calls=%async_computation.1 | async-start | bytes 2097152 | tf_op jit(solution)/shard_map/all_to_all | solution.py:391
  148.2 1.2 add_convert_fusion.2
  149.4 2.7 %collective-permute-start.23 = (bf16[64,4096]{1,0:T(8,128)(2,1)S(1)}, bf16[64,4096]{1,0:T(8,128)(2,1)S(1)}, u32[]{:S(2)}, u32[]{:S(2)}) collective-permute-start(bf16[64,4096]{1,0:T(8,128)(2,1)S(1)} %add_convert_fusion.2), channel_id=1, source_target_pairs={{0,2},{1,3},{2,0},{3,1},{4,6},{5,7},{6,4},{7,5},{8,10},{9,11},{10,... | collective-permute-start | bytes 1572872 | tf_op jit(solution)/shard_map/sum1_near/ppermute | solution.py:227
  152.1 3.4 %collective-permute-done.21 = bf16[64,4096]{1,0:T(8,128)(2,1)} collective-permute-done((bf16[64,4096]{1,0:T(8,128)(2,1)}, bf16[64,4096]{1,0:T(8,128)(2,1)}, u32[]{:S(2)}, u32[]{:S(2)}) %collective-permute-start.21) | collective-permute-done | bytes 524320 | tf_op jit(solution)/shard_map/sum0_near/ppermute | solution.py:227
  155.6 1.8 %fusion.3 = bf16[8,8,4096]{2,1,0:T(8,128)(2,1)S(1)} fusion(bf16[64,4096]{1,0:T(8,128)(2,1)} %copy-done.12, bf16[64,4096]{1,0:T(8,128)(2,1)} %copy-done.11, bf16[64,4096]{1,0:T(8,128)(2,1)} %copy-done.10, f32[64,4096]{1,0:T(8,128)S(1)} %copy-done.1, bf16[64,4096]{1,0:T(8,128)(2,1)} %collective-permute-done.21, pred[]{:T(512)S(6)} %or.3), kind=kLoop, calls=%fused_computation.12 | loop fusion | flops 2359296 | bytes 3670017 | tf_op jit(solution)/shard_map/reshape | solution.py:408
  157.4 5.2 %collective-permute-done.23 = bf16[64,4096]{1,0:T(8,128)(2,1)S(1)} collective-permute-done((bf16[64,4096]{1,0:T(8,128)(2,1)S(1)}, bf16[64,4096]{1,0:T(8,128)(2,1)S(1)}, u32[]{:S(2)}, u32[]{:S(2)}) %collective-permute-start.23) | collective-permute-done | bytes 524320 | tf_op jit(solution)/shard_map/sum1_near/ppermute | solution.py:227
  162.7 1.1 pad_maximum_fusion
  164.3 0.7 slice_add_fusion
  165.1 1.4 reshape.498
  (129 shorter events, 6.9 us)
Async XLA Ops:
  2.0 2.1 %collective-permute-start = (bf16[4,16,8,512]{3,2,1,0:T(8,128)(2,1)S(1)}, bf16[4,16,8,512]{3,2,1,0:T(8,128)(2,1)S(1)}, u32[]{:S(2)}, u32[]{:S(2)}) collective-permute-start(bf16[4,16,8,512]{3,2,1,0:T(8,128)(2,1)S(1)} %get-tuple-element.128), channel_id=1, source_target_pairs={{0,1},{1,0},{2,3},{3,2},{4,5},{5,4},{6,7},{7,6},{8,9},{9,8},{10,11... | collective-permute-start | bytes 1572872 | tf_op jit(solution)/shard_map/swap_tokens/ppermute | solution.py:227
  2.5 4.8 %copy-start.2 = (bf16[128,2,3,512]{3,1,2,0:T(2,128)(2,1)S(1)}, bf16[128,2,3,512]{3,1,2,0:T(2,128)(2,1)}, u32[]{:S(2)}) copy-start(bf16[128,2,3,512]{3,1,2,0:T(2,128)(2,1)} %param.16) | copy-start | bytes 2359300
  4.2 16.9 %copy-start.9 = (bf16[2,256,512]{2,1,0:T(8,128)(2,1)}, bf16[2,256,512]{2,1,0:T(8,128)(2,1)S(1)}, u32[]{:S(2)}) copy-start(bf16[2,256,512]{2,1,0:T(8,128)(2,1)S(1)} %get-tuple-element.63.refs_0_) | copy-start | bytes 1572868
  4.2 53.9 %copy-start.8 = (bf16[2,256,512]{2,1,0:T(8,128)(2,1)}, bf16[2,256,512]{2,1,0:T(8,128)(2,1)S(1)}, u32[]{:S(2)}) copy-start(bf16[2,256,512]{2,1,0:T(8,128)(2,1)S(1)} %get-tuple-element.91.refs_0_) | copy-start | bytes 1572868
  4.2 3.9 %copy-start.16 = (f32[512]{0:T(512)S(1)}, f32[512]{0:T(512)}, u32[]{:S(2)}) copy-start(f32[512]{0:T(512)} %param.14) | copy-start | bytes 6148
  4.2 15.8 %copy-start.17 = (s32[128]{0:T(128)S(1)}, s32[128]{0:T(128)}, u32[]{:S(2)}) copy-start(s32[128]{0:T(128)} %param.18) | copy-start | bytes 1540
  4.2 15.2 %collective-permute-start.1 = (bf16[2,256,512]{2,1,0:T(8,128)(2,1)S(1)}, bf16[2,256,512]{2,1,0:T(8,128)(2,1)S(1)}, u32[]{:S(2)}, u32[]{:S(2)}) collective-permute-start(bf16[2,256,512]{2,1,0:T(8,128)(2,1)S(1)} %get-tuple-element.63.refs_0_), channel_id=1, source_target_pairs={{0,2},{1,3},{2,0},{3,1},{4,6},{5,7},{6,4},{7,5},{8,10},{9,11},{10,... | collective-permute-start | bytes 1572872 | tf_op jit(solution)/shard_map/gather0_e1/ppermute | solution.py:227
  7.2 12.2 %collective-permute-start.2 = (bf16[2,256,512]{2,1,0:T(8,128)(2,1)S(1)}, bf16[2,256,512]{2,1,0:T(8,128)(2,1)}, u32[]{:S(2)}, u32[]{:S(2)}) collective-permute-start(bf16[2,256,512]{2,1,0:T(8,128)(2,1)S(1)} %get-tuple-element.63.refs_0_), channel_id=1, source_target_pairs={{2,4},{3,5},{4,2},{5,3},{0,1},{1,0},{6,7},{7,6},{10,12},{11,13},{1... | collective-permute-start | bytes 1572872 | tf_op jit(solution)/shard_map/gather0_m1/ppermute | solution.py:227
  7.4 2.5 %collective-permute-start.4 = (bf16[6,4,16,512]{3,2,1,0:T(8,128)(2,1)S(1)}, bf16[6,4,16,512]{3,2,1,0:T(8,128)(2,1)S(1)}, u32[]{:S(2)}, u32[]{:S(2)}) collective-permute-start(bf16[6,4,16,512]{3,2,1,0:T(8,128)(2,1)S(1)} %get-tuple-element.130), channel_id=1, source_target_pairs={{0,1},{1,0},{2,3},{3,2},{4,5},{5,4},{6,7},{7,6},{8,9},{9,8},{10,11... | collective-permute-start | bytes 1179656 | tf_op jit(solution)/shard_map/swap_tails/ppermute | solution.py:227
  8.0 1.9 %collective-permute-start.5 = (f32[4,16,512]{2,1,0:T(8,128)S(1)}, f32[4,16,512]{2,1,0:T(8,128)S(1)}, u32[]{:S(2)}, u32[]{:S(2)}) collective-permute-start(f32[4,16,512]{2,1,0:T(8,128)S(1)} %get-tuple-element.140), channel_id=1, source_target_pairs={{0,1},{1,0},{2,3},{3,2},{4,5},{5,4},{6,7},{7,6},{8,9},{9,8},{10,11... | collective-permute-start | bytes 393224 | tf_op jit(solution)/shard_map/swap_states/ppermute | solution.py:227
  8.2 1.8 %collective-permute-start.3 = (f32[10,512]{1,0:T(8,128)S(1)}, f32[10,512]{1,0:T(8,128)S(1)}, u32[]{:S(2)}, u32[]{:S(2)}) collective-permute-start(f32[10,512]{1,0:T(8,128)S(1)} %pad_maximum_fusion.4), channel_id=1, source_target_pairs={{0,1},{1,0},{2,3},{3,2},{4,5},{5,4},{6,7},{7,6},{8,9},{9,8},{10,11... | collective-permute-start | bytes 61448 | tf_op jit(solution)/shard_map/swap_taps/ppermute | solution.py:227
  19.5 7.3 %copy-start.19 = (bf16[2,256,512]{2,1,0:T(8,128)(2,1)}, bf16[2,256,512]{2,1,0:T(8,128)(2,1)S(1)}, u32[]{:S(2)}) copy-start(bf16[2,256,512]{2,1,0:T(8,128)(2,1)S(1)} %collective-permute-done.1.refs_1_) | copy-start | bytes 1572868
  19.5 41.2 %collective-permute-start.10 = (bf16[3,4096,512]{2,1,0:T(8,128)(2,1)}, bf16[3,4096,512]{2,1,0:T(8,128)(2,1)}, u32[]{:S(2)}, u32[]{:S(2)}) collective-permute-start(bf16[3,4096,512]{2,1,0:T(8,128)(2,1)} %bitcast.93), channel_id=1, source_target_pairs={{0,1},{1,0},{2,3},{3,2},{4,5},{5,4},{6,7},{7,6},{8,9},{9,8},{10,11... | collective-permute-start | bytes 37748744 | tf_op jit(solution)/shard_map/swap_w_in/ppermute | solution.py:227
  19.5 39.9 %collective-permute-start.11 = (bf16[512,4096]{1,0:T(8,128)(2,1)}, bf16[512,4096]{1,0:T(8,128)(2,1)}, u32[]{:S(2)}, u32[]{:S(2)}) collective-permute-start(bf16[512,4096]{1,0:T(8,128)(2,1)} %refs_8_.1), channel_id=1, source_target_pairs={{0,1},{1,0},{2,3},{3,2},{4,5},{5,4},{6,7},{7,6},{8,9},{9,8},{10,11... | collective-permute-start | bytes 12582920 | tf_op jit(solution)/shard_map/swap_w_out/ppermute | solution.py:227
  21.0 5.7 %copy-start.18 = (s32[128]{0:T(128)S(1)}, s32[128]{0:T(128)}, u32[]{:S(2)}) copy-start(s32[128]{0:T(128)} %param.19) | copy-start | bytes 1540
  21.2 39.5 %copy-start.14 = (f32[10,2,512]{2,0,1:T(8,128)}, f32[10,2,512]{2,0,1:T(8,128)S(1)}, u32[]{:S(2)}) copy-start(f32[10,2,512]{2,0,1:T(8,128)S(1)} %copy.30) | copy-start | bytes 122884
  21.8 5.0 %collective-permute-start.6 = (bf16[2,256,512]{2,1,0:T(8,128)(2,1)S(1)}, bf16[2,256,512]{2,1,0:T(8,128)(2,1)S(1)}, u32[]{:S(2)}, u32[]{:S(2)}) collective-permute-start(bf16[2,256,512]{2,1,0:T(8,128)(2,1)S(1)} %collective-permute-done.1.refs_1_), channel_id=1, source_target_pairs={{2,4},{3,5},{4,2},{5,3},{10,12},{11,13},{12,10},{13,11},{18,20},{1... | collective-permute-start | bytes 1572872 | tf_op jit(solution)/shard_map/gather0_m2/ppermute | solution.py:227
  22.5 19.3 %collective-permute-start.7 = (bf16[2,256,512]{2,1,0:T(8,128)(2,1)}, bf16[2,256,512]{2,1,0:T(8,128)(2,1)}, u32[]{:S(2)}, u32[]{:S(2)}) collective-permute-start(bf16[2,256,512]{2,1,0:T(8,128)(2,1)} %collective-permute-done.2.refs_2_), channel_id=1, source_target_pairs={{2,0},{3,1},{4,6},{5,7},{10,8},{11,9},{12,14},{13,15},{18,16},{19,... | collective-permute-start | bytes 1572872 | tf_op jit(solution)/shard_map/gather0_e2/ppermute | solution.py:227
  26.8 34.0 %copy-start.20 = (bf16[2,256,512]{2,1,0:T(8,128)(2,1)}, bf16[2,256,512]{2,1,0:T(8,128)(2,1)S(1)}, u32[]{:S(2)}) copy-start(bf16[2,256,512]{2,1,0:T(8,128)(2,1)S(1)} %collective-permute-done.6.refs_4_) | copy-start | bytes 1572868
  27.3 26.2 %collective-permute-start.8 = (bf16[2,256,512]{2,1,0:T(8,128)(2,1)S(1)}, bf16[2,256,512]{2,1,0:T(8,128)(2,1)S(1)}, u32[]{:S(2)}, u32[]{:S(2)}) collective-permute-start(bf16[2,256,512]{2,1,0:T(8,128)(2,1)S(1)} %collective-permute-done.6.refs_4_), channel_id=1, source_target_pairs={{2,0},{3,1},{4,6},{5,7},{10,8},{11,9},{12,14},{13,15},{18,16},{19,... | collective-permute-start | bytes 1572872 | tf_op jit(solution)/shard_map/gather0_e3/ppermute | solution.py:227
  28.6 25.0 %collective-permute-start.9 = (bf16[2,256,512]{2,1,0:T(8,128)(2,1)S(1)}, bf16[2,256,512]{2,1,0:T(8,128)(2,1)S(1)}, u32[]{:S(2)}, u32[]{:S(2)}) collective-permute-start(bf16[2,256,512]{2,1,0:T(8,128)(2,1)S(1)} %get-tuple-element.91.refs_0_), channel_id=1, source_target_pairs={{2,4},{3,5},{4,2},{5,3},{0,1},{1,0},{6,7},{7,6},{10,12},{11,13},{1... | collective-permute-start | bytes 1572872 | tf_op jit(solution)/shard_map/gather1_m1/ppermute | solution.py:227
  29.8 8.5 %all-to-all-start = ((s32[4,1,32]{2,1,0:T(1,128)}), s32[4,1,32]{2,1,0:T(1,128)S(1)}, u32[]{:S(2)}, u32[]{:S(2)}) async-start(s32[4,1,32]{2,1,0:T(1,128)} %bitcast.38), calls=%async_computation | async-start | bytes 4096 | tf_op jit(solution)/shard_map/all_to_all | solution.py:307
  53.6 7.1 %copy-start.22 = (bf16[2,256,512]{2,1,0:T(8,128)(2,1)}, bf16[2,256,512]{2,1,0:T(8,128)(2,1)S(1)}, u32[]{:S(2)}) copy-start(bf16[2,256,512]{2,1,0:T(8,128)(2,1)S(1)} %collective-permute-done.8.refs_5_) | copy-start | bytes 1572868
  53.6 25.7 %copy-start.21 = (bf16[2,256,512]{2,1,0:T(8,128)(2,1)}, bf16[2,256,512]{2,1,0:T(8,128)(2,1)S(1)}, u32[]{:S(2)}) copy-start(bf16[2,256,512]{2,1,0:T(8,128)(2,1)S(1)} %collective-permute-done.9.refs_2_) | copy-start | bytes 1572868
  53.6 25.7 %collective-permute-start.12 = (bf16[2,256,512]{2,1,0:T(8,128)(2,1)S(1)}, bf16[2,256,512]{2,1,0:T(8,128)(2,1)S(1)}, u32[]{:S(2)}, u32[]{:S(2)}) collective-permute-start(bf16[2,256,512]{2,1,0:T(8,128)(2,1)S(1)} %get-tuple-element.91.refs_0_), channel_id=1, source_target_pairs={{0,2},{1,3},{2,0},{3,1},{4,6},{5,7},{6,4},{7,5},{8,10},{9,11},{10,... | collective-permute-start | bytes 1572872 | tf_op jit(solution)/shard_map/gather1_e1/ppermute | solution.py:227
  55.4 33.0 %collective-permute-start.14 = (bf16[2,256,512]{2,1,0:T(8,128)(2,1)S(1)}, bf16[2,256,512]{2,1,0:T(8,128)(2,1)S(1)}, u32[]{:S(2)}, u32[]{:S(2)}) collective-permute-start(bf16[2,256,512]{2,1,0:T(8,128)(2,1)S(1)} %get-tuple-element.91.refs_0_), channel_id=1, source_target_pairs={{0,6},{1,7},{6,0},{7,1},{2,3},{3,2},{4,5},{5,4},{8,14},{9,15},{14,... | collective-permute-start | bytes 1572872 | tf_op jit(solution)/shard_map/gather1_across/ppermute | solution.py:227
  58.1 30.4 %collective-permute-start.15 = (bf16[2,256,512]{2,1,0:T(8,128)(2,1)S(1)}, bf16[2,256,512]{2,1,0:T(8,128)(2,1)S(1)}, u32[]{:S(2)}, u32[]{:S(2)}) collective-permute-start(bf16[2,256,512]{2,1,0:T(8,128)(2,1)S(1)} %get-tuple-element.91.refs_0_), channel_id=1, source_target_pairs={{0,4},{1,5},{6,2},{7,3},{8,12},{9,13},{14,10},{15,11},{16,20},{17,... | collective-permute-start | bytes 1572872 | tf_op jit(solution)/shard_map/gather1_skip/ppermute | solution.py:227
  59.4 29.1 %collective-permute-start.13 = (bf16[2,256,512]{2,1,0:T(8,128)(2,1)S(1)}, bf16[2,256,512]{2,1,0:T(8,128)(2,1)S(1)}, u32[]{:S(2)}, u32[]{:S(2)}) collective-permute-start(bf16[2,256,512]{2,1,0:T(8,128)(2,1)S(1)} %collective-permute-done.9.refs_2_), channel_id=1, source_target_pairs={{2,0},{3,1},{4,6},{5,7},{10,8},{11,9},{12,14},{13,15},{18,16},{19,... | collective-permute-start | bytes 1572872 | tf_op jit(solution)/shard_map/gather1_e2/ppermute | solution.py:227
  79.3 18.9 %copy-start.23 = (bf16[2,256,512]{2,1,0:T(8,128)(2,1)}, bf16[2,256,512]{2,1,0:T(8,128)(2,1)S(1)}, u32[]{:S(2)}) copy-start(bf16[2,256,512]{2,1,0:T(8,128)(2,1)S(1)} %collective-permute-done.12.refs_1_) | copy-start | bytes 1572868
  89.7 28.4 %copy-start.6 = (bf16[2,32,4096]{2,1,0:T(8,128)(2,1)S(1)}, bf16[2,32,4096]{2,1,0:T(8,128)(2,1)}, u32[]{:S(2)}) copy-start(bf16[2,32,4096]{2,1,0:T(8,128)(2,1)} %get-tuple-element.118) | copy-start | bytes 1572868
  89.7 28.5 %copy-start.4 = (bf16[64,4096]{1,0:T(8,128)(2,1)S(1)}, bf16[64,4096]{1,0:T(8,128)(2,1)}, u32[]{:S(2)}) copy-start(bf16[64,4096]{1,0:T(8,128)(2,1)} %get-tuple-element.104) | copy-start | bytes 1572868
  89.7 28.5 %collective-permute-start.18 = (bf16[64,4096]{1,0:T(8,128)(2,1)}, bf16[64,4096]{1,0:T(8,128)(2,1)S(1)}, u32[]{:S(2)}, u32[]{:S(2)}) collective-permute-start(bf16[64,4096]{1,0:T(8,128)(2,1)} %get-tuple-element.107), channel_id=1, source_target_pairs={{0,6},{1,7},{6,0},{7,1},{2,3},{3,2},{4,5},{5,4},{8,14},{9,15},{14,... | collective-permute-start | bytes 1572872 | tf_op jit(solution)/shard_map/sum0_across/ppermute | solution.py:227
  92.3 25.9 %collective-permute-start.19 = (bf16[64,4096]{1,0:T(8,128)(2,1)}, bf16[64,4096]{1,0:T(8,128)(2,1)S(1)}, u32[]{:S(2)}, u32[]{:S(2)}) collective-permute-start(bf16[64,4096]{1,0:T(8,128)(2,1)} %get-tuple-element.107), channel_id=1, source_target_pairs={{4,0},{5,1},{2,6},{3,7},{12,8},{13,9},{10,14},{11,15},{20,16},{21,... | collective-permute-start | bytes 1572872 | tf_op jit(solution)/shard_map/sum0_skip/ppermute | solution.py:227
  93.6 24.6 %collective-permute-start.17 = (bf16[64,4096]{1,0:T(8,128)(2,1)}, bf16[64,4096]{1,0:T(8,128)(2,1)S(1)}, u32[]{:S(2)}, u32[]{:S(2)}) collective-permute-start(bf16[64,4096]{1,0:T(8,128)(2,1)} %get-tuple-element.104), channel_id=1, source_target_pairs={{0,2},{1,3},{6,4},{7,5},{8,10},{9,11},{14,12},{15,13},{16,18},{17,... | collective-permute-start | bytes 1572872 | tf_op jit(solution)/shard_map/sum0_mid_in/ppermute | solution.py:227
  116.7 10.9 %collective-permute-start.16 = (bf16[64,4096]{1,0:T(8,128)(2,1)}, bf16[64,4096]{1,0:T(8,128)(2,1)S(1)}, u32[]{:S(2)}, u32[]{:S(2)}) collective-permute-start(bf16[64,4096]{1,0:T(8,128)(2,1)} %get-tuple-element.103), channel_id=1, source_target_pairs={{0,2},{1,3},{6,4},{7,5},{8,10},{9,11},{14,12},{15,13},{16,18},{17,... | collective-permute-start | bytes 1572872 | tf_op jit(solution)/shard_map/sum1_far_in/ppermute | solution.py:227
  118.2 9.3 %copy-start.3 = (bf16[64,4096]{1,0:T(8,128)(2,1)S(1)}, bf16[64,4096]{1,0:T(8,128)(2,1)}, u32[]{:S(2)}) copy-start(bf16[64,4096]{1,0:T(8,128)(2,1)} %get-tuple-element.116) | copy-start | bytes 1572868
  118.3 13.7 %copy-start.5 = (bf16[64,4096]{1,0:T(8,128)(2,1)S(1)}, bf16[64,4096]{1,0:T(8,128)(2,1)}, u32[]{:S(2)}) copy-start(bf16[64,4096]{1,0:T(8,128)(2,1)} %get-tuple-element.103) | copy-start | bytes 1572868
  118.4 9.2 %collective-permute-start.20 = (bf16[64,4096]{1,0:T(8,128)(2,1)S(1)}, bf16[64,4096]{1,0:T(8,128)(2,1)S(1)}, u32[]{:S(2)}, u32[]{:S(2)}) collective-permute-start(bf16[64,4096]{1,0:T(8,128)(2,1)S(1)} %add_convert_fusion.5), channel_id=1, source_target_pairs={{2,4},{3,5},{4,2},{5,3},{0,1},{1,0},{6,7},{7,6},{10,12},{11,13},{1... | collective-permute-start | bytes 1572872 | tf_op jit(solution)/shard_map/sum0_mid_on/ppermute | solution.py:227
  119.2 13.0 %collective-permute-start.25 = (bf16[64,4096]{1,0:T(8,128)(2,1)S(1)}, bf16[64,4096]{1,0:T(8,128)(2,1)S(1)}, u32[]{:S(2)}, u32[]{:S(2)}) collective-permute-start(bf16[64,4096]{1,0:T(8,128)(2,1)S(1)} %get-tuple-element.126), channel_id=1, source_target_pairs={{0,1},{1,0},{2,3},{3,2},{4,5},{5,4},{6,7},{7,6},{8,9},{9,8},{10,11... | collective-permute-start | bytes 1572872 | tf_op jit(solution)/shard_map/swap_commit/ppermute | solution.py:227
  127.6 16.8 %copy-start.12 = (bf16[64,4096]{1,0:T(8,128)(2,1)}, bf16[64,4096]{1,0:T(8,128)(2,1)S(1)}, u32[]{:S(2)}) copy-start(bf16[64,4096]{1,0:T(8,128)(2,1)S(1)} %collective-permute-done.20) | copy-start | bytes 1572868
  127.6 16.7 %collective-permute-start.24 = (bf16[64,4096]{1,0:T(8,128)(2,1)S(1)}, bf16[64,4096]{1,0:T(8,128)(2,1)S(1)}, u32[]{:S(2)}, u32[]{:S(2)}) collective-permute-start(bf16[64,4096]{1,0:T(8,128)(2,1)S(1)} %copy-done.3), channel_id=1, source_target_pairs={{0,2},{1,3},{6,4},{7,5},{8,10},{9,11},{14,12},{15,13},{16,18},{17,... | collective-permute-start | bytes 1572872 | tf_op jit(solution)/shard_map/sum1_mid_in/ppermute | solution.py:227
  131.9 23.7 %collective-permute-start.21 = (bf16[64,4096]{1,0:T(8,128)(2,1)}, bf16[64,4096]{1,0:T(8,128)(2,1)}, u32[]{:S(2)}, u32[]{:S(2)}) collective-permute-start(bf16[64,4096]{1,0:T(8,128)(2,1)} %get-tuple-element.109), channel_id=1, source_target_pairs={{0,2},{1,3},{2,0},{3,1},{4,6},{5,7},{6,4},{7,5},{8,10},{9,11},{10,... | collective-permute-start | bytes 1572872 | tf_op jit(solution)/shard_map/sum0_near/ppermute | solution.py:227
  132.1 16.1 %collective-permute-start.22 = (bf16[64,4096]{1,0:T(8,128)(2,1)S(1)}, bf16[64,4096]{1,0:T(8,128)(2,1)}, u32[]{:S(2)}, u32[]{:S(2)}) collective-permute-start(bf16[64,4096]{1,0:T(8,128)(2,1)S(1)} %add_convert_fusion.3), channel_id=1, source_target_pairs={{2,4},{3,5},{4,2},{5,3},{0,1},{1,0},{6,7},{7,6},{10,12},{11,13},{1... | collective-permute-start | bytes 1572872 | tf_op jit(solution)/shard_map/sum1_far_on/ppermute | solution.py:227
  144.4 11.2 %copy-start.1 = (f32[64,4096]{1,0:T(8,128)S(1)}, f32[64,4096]{1,0:T(8,128)}, u32[]{:S(2)}) copy-start(f32[64,4096]{1,0:T(8,128)} %get-tuple-element.89) | copy-start | bytes 3145732
  144.4 19.5 %all-to-all-start.1 = ((bf16[4,32,4096]{2,1,0:T(8,128)(2,1)}), bf16[4,32,4096]{2,1,0:T(8,128)(2,1)S(1)}, u32[]{:S(2)}, u32[]{:S(2)}) async-start(bf16[4,32,4096]{2,1,0:T(8,128)(2,1)} %bitcast.45), calls=%async_computation.1 | async-start | bytes 2097152 | tf_op jit(solution)/shard_map/all_to_all | solution.py:391
  149.4 13.1 %copy-start = (f32[64,4096]{1,0:T(8,128)S(1)}, f32[64,4096]{1,0:T(8,128)}, u32[]{:S(2)}) copy-start(f32[64,4096]{1,0:T(8,128)} %get-tuple-element.113) | copy-start | bytes 3145732
  149.4 13.1 %collective-permute-start.23 = (bf16[64,4096]{1,0:T(8,128)(2,1)S(1)}, bf16[64,4096]{1,0:T(8,128)(2,1)S(1)}, u32[]{:S(2)}, u32[]{:S(2)}) collective-permute-start(bf16[64,4096]{1,0:T(8,128)(2,1)S(1)} %add_convert_fusion.2), channel_id=1, source_target_pairs={{0,2},{1,3},{2,0},{3,1},{4,6},{5,7},{6,4},{7,5},{8,10},{9,11},{10,... | collective-permute-start | bytes 1572872 | tf_op jit(solution)/shard_map/sum1_near/ppermute | solution.py:227
  152.1 10.4 %collective-permute-start.26 = (bf16[64,4096]{1,0:T(8,128)(2,1)S(1)}, bf16[64,4096]{1,0:T(8,128)(2,1)S(1)}, u32[]{:S(2)}, u32[]{:S(2)}) collective-permute-start(bf16[64,4096]{1,0:T(8,128)(2,1)S(1)} %add_convert_fusion.1), channel_id=1, source_target_pairs={{2,4},{3,5},{4,2},{5,3},{0,1},{1,0},{6,7},{7,6},{10,12},{11,13},{1... | collective-permute-start | bytes 1572872 | tf_op jit(solution)/shard_map/sum1_mid_on/ppermute | solution.py:227
  (8 other events, 14.2 us)

commit v4 on v3

--- a/solution.py
+++ b/solution.py
@@ -404,10 +404,7 @@
             for k in range(2, nz):
                 flow = add(terms[k], permute(flow, ring, "sum"))
             totals.append(terms[0] + permute(flow, ring, "sum").astype(jnp.float32))
-    mixed = [
-        total.astype(jnp.bfloat16).reshape(size, steps, width) for total, size in zip(totals, sizes)
-    ]
-    mixed = jnp.concatenate(mixed, axis=0)
+    mixed = jnp.concatenate(totals, axis=0).astype(jnp.bfloat16).reshape(share, steps, width)
 
     placed = jnp.dot(put, got, preferred_element_type=jnp.float32)
     edge = 3 * tail_len * local

time: 167 us -> 167 us (level)
    another operation x0 -> x2, other arithmetic: none -> 2 us
    reshape x2 -> x0, other arithmetic: 2 us -> none  [per_device(): total.astype(jnp.bfloat16).reshape(size, steps, width)]
where the time goes in v4:
time: 167 us
  waiting for transfers between devices  66.2 us (40%)
  starting transfers between devices  40.6 us (24%)
  Pallas kernels  37 us (22%)
  local copies, waits for them, and re-layouts  10.1 us (6%)
  other arithmetic  9.47 us (6%)
  matrix products  1.86 us (1%)
    ppermute x27, waiting for transfers between devices, permute(): return lax.ppermute(value, 'tensor', links)  62.9 us
    pallas_call x2, Pallas kernels, run_chunk(): pl.pallas_call(functools.partial(chunk_kernel, nz, choices, tail_len, tap...  37 us
    ppermute x27, starting transfers between devices, permute(): return lax.ppermute(value, 'tensor', links)  32.9 us
    all_to_all x1, starting transfers between devices, commit_order(): lax.all_to_all(slot_out.reshape(n_dp, sends), 'dp', split_axis=0, concat_...  3.88 us
    all_to_all x1, starting transfers between devices, per_device(): got = lax.all_to_all(sent, 'dp', split_axis=0, concat_axis=0, tiled=True)  3.86 us
  transfers between devices with their start and end apart: 29, of which 11 were waited for; matrix products, arithmetic and copies ran while one was open for 9% of the time, Pallas kernels for 22%

profile of v4, /device:TPU:0, one launch (start us, length us, event | category | flops | bytes accessed | tf_op | source)
XLA Modules:
  0.0 166.5 jit_solution(17896655389354265806)
XLA Ops:
  0.7 1.3 dynamic-slice_bitcast_fusion.1
  2.5 1.5 collective-permute-done
  4.2 3.0 %collective-permute-start.1 = (bf16[2,256,512]{2,1,0:T(8,128)(2,1)S(1)}, bf16[2,256,512]{2,1,0:T(8,128)(2,1)S(1)}, u32[]{:S(2)}, u32[]{:S(2)}) collective-permute-start(bf16[2,256,512]{2,1,0:T(8,128)(2,1)S(1)} %get-tuple-element.63.refs_0_), channel_id=1, source_target_pairs={{0,2},{1,3},{2,0},{3,1},{4,6},{5,7},{6,4},{7,5},{8,10},{9,11},{10,... | collective-permute-start | bytes 1572872 | tf_op jit(solution)/shard_map/gather0_e1/ppermute | solution.py:227
  7.4 0.6 collective-permute-start.4
  8.7 1.2 collective-permute-done.3
  10.0 9.5 %collective-permute-done.1.refs_1_ = bf16[2,256,512]{2,1,0:T(8,128)(2,1)S(1)} collective-permute-done((bf16[2,256,512]{2,1,0:T(8,128)(2,1)S(1)}, bf16[2,256,512]{2,1,0:T(8,128)(2,1)S(1)}, u32[]{:S(2)}, u32[]{:S(2)}) %collective-permute-start.1) | collective-permute-done | bytes 524320 | tf_op jit(solution)/shard_map/gather0_e1/ppermute | solution.py:227
  20.3 0.7 stack.39.meta
  21.2 0.6 slice.110.refs_12_
  21.8 0.7 collective-permute-start.6
  22.5 1.3 collective-permute-start.7
  23.8 0.7 maximum_bitcast_fusion.4.refs_14_
  24.5 0.7 maximum_bitcast_fusion.3.refs_14_
  25.1 0.8 maximum_bitcast_fusion.2.refs_13_
  26.0 0.8 maximum_bitcast_fusion.1.refs_13_
  27.3 1.3 collective-permute-start.8
  29.2 0.7 all_to_all.14
  29.8 3.9 %all-to-all-start = ((s32[4,1,32]{2,1,0:T(1,128)}), s32[4,1,32]{2,1,0:T(1,128)S(1)}, u32[]{:S(2)}, u32[]{:S(2)}) async-start(s32[4,1,32]{2,1,0:T(1,128)} %bitcast.38), calls=%async_computation | async-start | bytes 4096 | tf_op jit(solution)/shard_map/all_to_all | solution.py:307
  33.7 0.7 copy.27.refs_15_
  34.4 0.7 copy.28.refs_15_
  35.1 3.3 %all-to-all-done = s32[4,1,32]{2,1,0:T(1,128)S(1)} async-done(((s32[4,1,32]{2,1,0:T(1,128)}), s32[4,1,32]{2,1,0:T(1,128)S(1)}, u32[]{:S(2)}, u32[]{:S(2)}) %all-to-all-start) | async-done | bytes 544 | tf_op jit(solution)/shard_map/all_to_all | solution.py:307
  38.9 0.6 reduce.3
  39.6 2.2 %collective-permute-done.7.refs_3_ = bf16[2,256,512]{2,1,0:T(8,128)(2,1)} collective-permute-done((bf16[2,256,512]{2,1,0:T(8,128)(2,1)}, bf16[2,256,512]{2,1,0:T(8,128)(2,1)}, u32[]{:S(2)}, u32[]{:S(2)}) %collective-permute-start.7) | collective-permute-done | bytes 524320 | tf_op jit(solution)/shard_map/gather0_e2/ppermute | solution.py:227
  41.8 11.8 %collective-permute-done.8.refs_5_ = bf16[2,256,512]{2,1,0:T(8,128)(2,1)S(1)} collective-permute-done((bf16[2,256,512]{2,1,0:T(8,128)(2,1)S(1)}, bf16[2,256,512]{2,1,0:T(8,128)(2,1)S(1)}, u32[]{:S(2)}, u32[]{:S(2)}) %collective-permute-start.8) | collective-permute-done | bytes 524320 | tf_op jit(solution)/shard_map/gather0_e3/ppermute | solution.py:227
  53.6 1.9 %collective-permute-start.12 = (bf16[2,256,512]{2,1,0:T(8,128)(2,1)S(1)}, bf16[2,256,512]{2,1,0:T(8,128)(2,1)S(1)}, u32[]{:S(2)}, u32[]{:S(2)}) collective-permute-start(bf16[2,256,512]{2,1,0:T(8,128)(2,1)S(1)} %get-tuple-element.91.refs_0_), channel_id=1, source_target_pairs={{0,2},{1,3},{2,0},{3,1},{4,6},{5,7},{6,4},{7,5},{8,10},{9,11},{10,... | collective-permute-start | bytes 1572872 | tf_op jit(solution)/shard_map/gather1_e1/ppermute | solution.py:227
  55.4 2.6 %collective-permute-start.14 = (bf16[2,256,512]{2,1,0:T(8,128)(2,1)S(1)}, bf16[2,256,512]{2,1,0:T(8,128)(2,1)S(1)}, u32[]{:S(2)}, u32[]{:S(2)}) collective-permute-start(bf16[2,256,512]{2,1,0:T(8,128)(2,1)S(1)} %get-tuple-element.91.refs_0_), channel_id=1, source_target_pairs={{0,6},{1,7},{6,0},{7,1},{2,3},{3,2},{4,5},{5,4},{8,14},{9,15},{14,... | collective-permute-start | bytes 1572872 | tf_op jit(solution)/shard_map/gather1_across/ppermute | solution.py:227
  58.1 1.3 collective-permute-start.15
  59.4 1.3 collective-permute-start.13
  60.7 18.5 %shard_map.121 = (f32[64,4096]{1,0:T(8,128)}, bf16[64,4096]{1,0:T(8,128)(2,1)}, bf16[64,4096]{1,0:T(8,128)(2,1)}, bf16[64,4096]{1,0:T(8,128)(2,1)}, bf16[2,32,4096]{2,1,0:T(8,128)(2,1)}) custom-call(s32[6]{0:T(128)} %stack.39.meta, bf16[2,256,512]{2,1,0:T(8,128)(2,1)} %copy-done.9, bf16[2,256,512]{2,1,0:T(8,128)(2,1)} %copy-done.19, ...), custom_call_target="tpu_custom_call" | custom-call | flops 21474836480 | bytes 4194304 | tf_op jit(solution)/shard_map/pallas_call | solution.py:176
  79.3 9.2 %collective-permute-done.13.refs_3_ = bf16[2,256,512]{2,1,0:T(8,128)(2,1)S(1)} collective-permute-done((bf16[2,256,512]{2,1,0:T(8,128)(2,1)S(1)}, bf16[2,256,512]{2,1,0:T(8,128)(2,1)S(1)}, u32[]{:S(2)}, u32[]{:S(2)}) %collective-permute-start.13) | collective-permute-done | bytes 524320 | tf_op jit(solution)/shard_map/gather1_e2/ppermute | solution.py:227
  88.5 0.8 copy-done.26
  89.7 2.6 %collective-permute-start.18 = (bf16[64,4096]{1,0:T(8,128)(2,1)}, bf16[64,4096]{1,0:T(8,128)(2,1)S(1)}, u32[]{:S(2)}, u32[]{:S(2)}) collective-permute-start(bf16[64,4096]{1,0:T(8,128)(2,1)} %get-tuple-element.107), channel_id=1, source_target_pairs={{0,6},{1,7},{6,0},{7,1},{2,3},{3,2},{4,5},{5,4},{8,14},{9,15},{14,... | collective-permute-start | bytes 1572872 | tf_op jit(solution)/shard_map/sum0_across/ppermute | solution.py:227
  92.3 1.3 collective-permute-start.19
  93.6 4.5 %collective-permute-start.17 = (bf16[64,4096]{1,0:T(8,128)(2,1)}, bf16[64,4096]{1,0:T(8,128)(2,1)S(1)}, u32[]{:S(2)}, u32[]{:S(2)}) collective-permute-start(bf16[64,4096]{1,0:T(8,128)(2,1)} %get-tuple-element.104), channel_id=1, source_target_pairs={{0,2},{1,3},{6,4},{7,5},{8,10},{9,11},{14,12},{15,13},{16,18},{17,... | collective-permute-start | bytes 1572872 | tf_op jit(solution)/shard_map/sum0_mid_in/ppermute | solution.py:227
  98.2 18.5 %shard_map.122 = (f32[64,4096]{1,0:T(8,128)}, bf16[64,4096]{1,0:T(8,128)(2,1)}, bf16[64,4096]{1,0:T(8,128)(2,1)}, bf16[64,4096]{1,0:T(8,128)(2,1)}, bf16[2,32,4096]{2,1,0:T(8,128)(2,1)}) custom-call(s32[6]{0:T(128)} %stack.39.meta, bf16[2,256,512]{2,1,0:T(8,128)(2,1)} %copy-done.8, bf16[2,256,512]{2,1,0:T(8,128)(2,1)} %copy-done.23, ...), custom_call_target="tpu_custom_call" | custom-call | flops 21474836480 | bytes 4194304 | tf_op jit(solution)/shard_map/pallas_call | solution.py:176
  116.7 1.5 collective-permute-start.16
  119.2 8.4 %collective-permute-done.16 = bf16[64,4096]{1,0:T(8,128)(2,1)S(1)} collective-permute-done((bf16[64,4096]{1,0:T(8,128)(2,1)}, bf16[64,4096]{1,0:T(8,128)(2,1)S(1)}, u32[]{:S(2)}, u32[]{:S(2)}) %collective-permute-start.16) | collective-permute-done | bytes 524320 | tf_op jit(solution)/shard_map/sum1_far_in/ppermute | solution.py:227
  127.6 4.3 %collective-permute-start.24 = (bf16[64,4096]{1,0:T(8,128)(2,1)S(1)}, bf16[64,4096]{1,0:T(8,128)(2,1)S(1)}, u32[]{:S(2)}, u32[]{:S(2)}) collective-permute-start(bf16[64,4096]{1,0:T(8,128)(2,1)S(1)} %copy-done.3), channel_id=1, source_target_pairs={{0,2},{1,3},{6,4},{7,5},{8,10},{9,11},{14,12},{15,13},{16,18},{17,... | collective-permute-start | bytes 1572872 | tf_op jit(solution)/shard_map/sum1_mid_in/ppermute | solution.py:227
  132.2 1.4 convolution_convert_fusion
  133.6 10.6 %collective-permute-done.24 = bf16[64,4096]{1,0:T(8,128)(2,1)S(1)} collective-permute-done((bf16[64,4096]{1,0:T(8,128)(2,1)S(1)}, bf16[64,4096]{1,0:T(8,128)(2,1)S(1)}, u32[]{:S(2)}, u32[]{:S(2)}) %collective-permute-start.24) | collective-permute-done | bytes 524320 | tf_op jit(solution)/shard_map/sum1_mid_in/ppermute | solution.py:227
  144.4 3.9 %all-to-all-start.1 = ((bf16[4,32,4096]{2,1,0:T(8,128)(2,1)}), bf16[4,32,4096]{2,1,0:T(8,128)(2,1)S(1)}, u32[]{:S(2)}, u32[]{:S(2)}) async-start(bf16[4,32,4096]{2,1,0:T(8,128)(2,1)} %bitcast.44), calls=%async_computation.1 | async-start | bytes 2097152 | tf_op jit(solution)/shard_map/all_to_all | solution.py:391
  148.2 1.2 add_convert_fusion.2
  149.4 2.7 %collective-permute-start.23 = (bf16[64,4096]{1,0:T(8,128)(2,1)S(1)}, bf16[64,4096]{1,0:T(8,128)(2,1)S(1)}, u32[]{:S(2)}, u32[]{:S(2)}) collective-permute-start(bf16[64,4096]{1,0:T(8,128)(2,1)S(1)} %add_convert_fusion.2), channel_id=1, source_target_pairs={{0,2},{1,3},{2,0},{3,1},{4,6},{5,7},{6,4},{7,5},{8,10},{9,11},{10,... | collective-permute-start | bytes 1572872 | tf_op jit(solution)/shard_map/sum1_near/ppermute | solution.py:227
  152.1 3.4 %collective-permute-done.21 = bf16[64,4096]{1,0:T(8,128)(2,1)} collective-permute-done((bf16[64,4096]{1,0:T(8,128)(2,1)}, bf16[64,4096]{1,0:T(8,128)(2,1)}, u32[]{:S(2)}, u32[]{:S(2)}) %collective-permute-start.21) | collective-permute-done | bytes 524320 | tf_op jit(solution)/shard_map/sum0_near/ppermute | solution.py:227
  155.6 1.8 %add_convert_fusion.4 = bf16[64,4096]{1,0:T(8,128)(2,1)S(1)} fusion(bf16[64,4096]{1,0:T(8,128)(2,1)} %copy-done.12, bf16[64,4096]{1,0:T(8,128)(2,1)} %copy-done.11, bf16[64,4096]{1,0:T(8,128)(2,1)} %copy-done.10, f32[64,4096]{1,0:T(8,128)S(1)} %copy-done.1, bf16[64,4096]{1,0:T(8,128)(2,1)} %collective-permute-done.21, pred[]{:T(512)S(6)} %or.3), kind=kLoop, calls=%fused_computation.10 | loop fusion | flops 2359296 | bytes 3670017 | tf_op jit(solution)/shard_map/convert.2
  157.4 5.2 %collective-permute-done.23 = bf16[64,4096]{1,0:T(8,128)(2,1)S(1)} collective-permute-done((bf16[64,4096]{1,0:T(8,128)(2,1)S(1)}, bf16[64,4096]{1,0:T(8,128)(2,1)S(1)}, u32[]{:S(2)}, u32[]{:S(2)}) %collective-permute-start.23) | collective-permute-done | bytes 524320 | tf_op jit(solution)/shard_map/sum1_near/ppermute | solution.py:227
  162.7 1.1 maximum_bitcast_fusion
  164.3 0.7 slice_add_fusion
  165.1 1.4 reshape.493
  (129 shorter events, 6.9 us)
Async XLA Ops:
  2.0 2.1 %collective-permute-start = (bf16[4,16,8,512]{3,2,1,0:T(8,128)(2,1)S(1)}, bf16[4,16,8,512]{3,2,1,0:T(8,128)(2,1)S(1)}, u32[]{:S(2)}, u32[]{:S(2)}) collective-permute-start(bf16[4,16,8,512]{3,2,1,0:T(8,128)(2,1)S(1)} %get-tuple-element.128), channel_id=1, source_target_pairs={{0,1},{1,0},{2,3},{3,2},{4,5},{5,4},{6,7},{7,6},{8,9},{9,8},{10,11... | collective-permute-start | bytes 1572872 | tf_op jit(solution)/shard_map/swap_tokens/ppermute | solution.py:227
  2.5 4.8 %copy-start.2 = (bf16[128,2,3,512]{3,1,2,0:T(2,128)(2,1)S(1)}, bf16[128,2,3,512]{3,1,2,0:T(2,128)(2,1)}, u32[]{:S(2)}) copy-start(bf16[128,2,3,512]{3,1,2,0:T(2,128)(2,1)} %param.16) | copy-start | bytes 2359300
  4.2 16.9 %copy-start.9 = (bf16[2,256,512]{2,1,0:T(8,128)(2,1)}, bf16[2,256,512]{2,1,0:T(8,128)(2,1)S(1)}, u32[]{:S(2)}) copy-start(bf16[2,256,512]{2,1,0:T(8,128)(2,1)S(1)} %get-tuple-element.63.refs_0_) | copy-start | bytes 1572868
  4.2 53.9 %copy-start.8 = (bf16[2,256,512]{2,1,0:T(8,128)(2,1)}, bf16[2,256,512]{2,1,0:T(8,128)(2,1)S(1)}, u32[]{:S(2)}) copy-start(bf16[2,256,512]{2,1,0:T(8,128)(2,1)S(1)} %get-tuple-element.91.refs_0_) | copy-start | bytes 1572868
  4.2 3.9 %copy-start.16 = (f32[512]{0:T(512)S(1)}, f32[512]{0:T(512)}, u32[]{:S(2)}) copy-start(f32[512]{0:T(512)} %param.14) | copy-start | bytes 6148
  4.2 15.8 %copy-start.17 = (s32[128]{0:T(128)S(1)}, s32[128]{0:T(128)}, u32[]{:S(2)}) copy-start(s32[128]{0:T(128)} %param.18) | copy-start | bytes 1540
  4.2 15.2 %collective-permute-start.1 = (bf16[2,256,512]{2,1,0:T(8,128)(2,1)S(1)}, bf16[2,256,512]{2,1,0:T(8,128)(2,1)S(1)}, u32[]{:S(2)}, u32[]{:S(2)}) collective-permute-start(bf16[2,256,512]{2,1,0:T(8,128)(2,1)S(1)} %get-tuple-element.63.refs_0_), channel_id=1, source_target_pairs={{0,2},{1,3},{2,0},{3,1},{4,6},{5,7},{6,4},{7,5},{8,10},{9,11},{10,... | collective-permute-start | bytes 1572872 | tf_op jit(solution)/shard_map/gather0_e1/ppermute | solution.py:227
  7.2 12.2 %collective-permute-start.2 = (bf16[2,256,512]{2,1,0:T(8,128)(2,1)S(1)}, bf16[2,256,512]{2,1,0:T(8,128)(2,1)}, u32[]{:S(2)}, u32[]{:S(2)}) collective-permute-start(bf16[2,256,512]{2,1,0:T(8,128)(2,1)S(1)} %get-tuple-element.63.refs_0_), channel_id=1, source_target_pairs={{2,4},{3,5},{4,2},{5,3},{0,1},{1,0},{6,7},{7,6},{10,12},{11,13},{1... | collective-permute-start | bytes 1572872 | tf_op jit(solution)/shard_map/gather0_m1/ppermute | solution.py:227
  7.4 2.5 %collective-permute-start.4 = (bf16[6,4,16,512]{3,2,1,0:T(8,128)(2,1)S(1)}, bf16[6,4,16,512]{3,2,1,0:T(8,128)(2,1)S(1)}, u32[]{:S(2)}, u32[]{:S(2)}) collective-permute-start(bf16[6,4,16,512]{3,2,1,0:T(8,128)(2,1)S(1)} %get-tuple-element.130), channel_id=1, source_target_pairs={{0,1},{1,0},{2,3},{3,2},{4,5},{5,4},{6,7},{7,6},{8,9},{9,8},{10,11... | collective-permute-start | bytes 1179656 | tf_op jit(solution)/shard_map/swap_tails/ppermute | solution.py:227
  8.0 1.9 %collective-permute-start.5 = (f32[4,16,512]{2,1,0:T(8,128)S(1)}, f32[4,16,512]{2,1,0:T(8,128)S(1)}, u32[]{:S(2)}, u32[]{:S(2)}) collective-permute-start(f32[4,16,512]{2,1,0:T(8,128)S(1)} %get-tuple-element.140), channel_id=1, source_target_pairs={{0,1},{1,0},{2,3},{3,2},{4,5},{5,4},{6,7},{7,6},{8,9},{9,8},{10,11... | collective-permute-start | bytes 393224 | tf_op jit(solution)/shard_map/swap_states/ppermute | solution.py:227
  8.2 1.8 %collective-permute-start.3 = (f32[10,512]{1,0:T(8,128)S(1)}, f32[10,512]{1,0:T(8,128)S(1)}, u32[]{:S(2)}, u32[]{:S(2)}) collective-permute-start(f32[10,512]{1,0:T(8,128)S(1)} %pad_maximum_fusion.3), channel_id=1, source_target_pairs={{0,1},{1,0},{2,3},{3,2},{4,5},{5,4},{6,7},{7,6},{8,9},{9,8},{10,11... | collective-permute-start | bytes 61448 | tf_op jit(solution)/shard_map/swap_taps/ppermute | solution.py:227
  19.5 7.3 %copy-start.19 = (bf16[2,256,512]{2,1,0:T(8,128)(2,1)}, bf16[2,256,512]{2,1,0:T(8,128)(2,1)S(1)}, u32[]{:S(2)}) copy-start(bf16[2,256,512]{2,1,0:T(8,128)(2,1)S(1)} %collective-permute-done.1.refs_1_) | copy-start | bytes 1572868
  19.5 41.2 %collective-permute-start.10 = (bf16[3,4096,512]{2,1,0:T(8,128)(2,1)}, bf16[3,4096,512]{2,1,0:T(8,128)(2,1)}, u32[]{:S(2)}, u32[]{:S(2)}) collective-permute-start(bf16[3,4096,512]{2,1,0:T(8,128)(2,1)} %bitcast.91), channel_id=1, source_target_pairs={{0,1},{1,0},{2,3},{3,2},{4,5},{5,4},{6,7},{7,6},{8,9},{9,8},{10,11... | collective-permute-start | bytes 37748744 | tf_op jit(solution)/shard_map/swap_w_in/ppermute | solution.py:227
  19.5 39.9 %collective-permute-start.11 = (bf16[512,4096]{1,0:T(8,128)(2,1)}, bf16[512,4096]{1,0:T(8,128)(2,1)}, u32[]{:S(2)}, u32[]{:S(2)}) collective-permute-start(bf16[512,4096]{1,0:T(8,128)(2,1)} %refs_8_.1), channel_id=1, source_target_pairs={{0,1},{1,0},{2,3},{3,2},{4,5},{5,4},{6,7},{7,6},{8,9},{9,8},{10,11... | collective-permute-start | bytes 12582920 | tf_op jit(solution)/shard_map/swap_w_out/ppermute | solution.py:227
  21.0 5.7 %copy-start.18 = (s32[128]{0:T(128)S(1)}, s32[128]{0:T(128)}, u32[]{:S(2)}) copy-start(s32[128]{0:T(128)} %param.19) | copy-start | bytes 1540
  21.2 39.5 %copy-start.14 = (f32[10,2,512]{2,0,1:T(8,128)}, f32[10,2,512]{2,0,1:T(8,128)S(1)}, u32[]{:S(2)}) copy-start(f32[10,2,512]{2,0,1:T(8,128)S(1)} %copy.30) | copy-start | bytes 122884
  21.8 5.0 %collective-permute-start.6 = (bf16[2,256,512]{2,1,0:T(8,128)(2,1)S(1)}, bf16[2,256,512]{2,1,0:T(8,128)(2,1)S(1)}, u32[]{:S(2)}, u32[]{:S(2)}) collective-permute-start(bf16[2,256,512]{2,1,0:T(8,128)(2,1)S(1)} %collective-permute-done.1.refs_1_), channel_id=1, source_target_pairs={{2,4},{3,5},{4,2},{5,3},{10,12},{11,13},{12,10},{13,11},{18,20},{1... | collective-permute-start | bytes 1572872 | tf_op jit(solution)/shard_map/gather0_m2/ppermute | solution.py:227
  22.5 19.3 %collective-permute-start.7 = (bf16[2,256,512]{2,1,0:T(8,128)(2,1)}, bf16[2,256,512]{2,1,0:T(8,128)(2,1)}, u32[]{:S(2)}, u32[]{:S(2)}) collective-permute-start(bf16[2,256,512]{2,1,0:T(8,128)(2,1)} %collective-permute-done.2.refs_2_), channel_id=1, source_target_pairs={{2,0},{3,1},{4,6},{5,7},{10,8},{11,9},{12,14},{13,15},{18,16},{19,... | collective-permute-start | bytes 1572872 | tf_op jit(solution)/shard_map/gather0_e2/ppermute | solution.py:227
  26.8 34.0 %copy-start.20 = (bf16[2,256,512]{2,1,0:T(8,128)(2,1)}, bf16[2,256,512]{2,1,0:T(8,128)(2,1)S(1)}, u32[]{:S(2)}) copy-start(bf16[2,256,512]{2,1,0:T(8,128)(2,1)S(1)} %collective-permute-done.6.refs_4_) | copy-start | bytes 1572868
  27.3 26.2 %collective-permute-start.8 = (bf16[2,256,512]{2,1,0:T(8,128)(2,1)S(1)}, bf16[2,256,512]{2,1,0:T(8,128)(2,1)S(1)}, u32[]{:S(2)}, u32[]{:S(2)}) collective-permute-start(bf16[2,256,512]{2,1,0:T(8,128)(2,1)S(1)} %collective-permute-done.6.refs_4_), channel_id=1, source_target_pairs={{2,0},{3,1},{4,6},{5,7},{10,8},{11,9},{12,14},{13,15},{18,16},{19,... | collective-permute-start | bytes 1572872 | tf_op jit(solution)/shard_map/gather0_e3/ppermute | solution.py:227
  28.6 25.0 %collective-permute-start.9 = (bf16[2,256,512]{2,1,0:T(8,128)(2,1)S(1)}, bf16[2,256,512]{2,1,0:T(8,128)(2,1)S(1)}, u32[]{:S(2)}, u32[]{:S(2)}) collective-permute-start(bf16[2,256,512]{2,1,0:T(8,128)(2,1)S(1)} %get-tuple-element.91.refs_0_), channel_id=1, source_target_pairs={{2,4},{3,5},{4,2},{5,3},{0,1},{1,0},{6,7},{7,6},{10,12},{11,13},{1... | collective-permute-start | bytes 1572872 | tf_op jit(solution)/shard_map/gather1_m1/ppermute | solution.py:227
  29.8 8.5 %all-to-all-start = ((s32[4,1,32]{2,1,0:T(1,128)}), s32[4,1,32]{2,1,0:T(1,128)S(1)}, u32[]{:S(2)}, u32[]{:S(2)}) async-start(s32[4,1,32]{2,1,0:T(1,128)} %bitcast.38), calls=%async_computation | async-start | bytes 4096 | tf_op jit(solution)/shard_map/all_to_all | solution.py:307
  53.6 7.1 %copy-start.22 = (bf16[2,256,512]{2,1,0:T(8,128)(2,1)}, bf16[2,256,512]{2,1,0:T(8,128)(2,1)S(1)}, u32[]{:S(2)}) copy-start(bf16[2,256,512]{2,1,0:T(8,128)(2,1)S(1)} %collective-permute-done.8.refs_5_) | copy-start | bytes 1572868
  53.6 25.7 %copy-start.21 = (bf16[2,256,512]{2,1,0:T(8,128)(2,1)}, bf16[2,256,512]{2,1,0:T(8,128)(2,1)S(1)}, u32[]{:S(2)}) copy-start(bf16[2,256,512]{2,1,0:T(8,128)(2,1)S(1)} %collective-permute-done.9.refs_2_) | copy-start | bytes 1572868
  53.6 25.7 %collective-permute-start.12 = (bf16[2,256,512]{2,1,0:T(8,128)(2,1)S(1)}, bf16[2,256,512]{2,1,0:T(8,128)(2,1)S(1)}, u32[]{:S(2)}, u32[]{:S(2)}) collective-permute-start(bf16[2,256,512]{2,1,0:T(8,128)(2,1)S(1)} %get-tuple-element.91.refs_0_), channel_id=1, source_target_pairs={{0,2},{1,3},{2,0},{3,1},{4,6},{5,7},{6,4},{7,5},{8,10},{9,11},{10,... | collective-permute-start | bytes 1572872 | tf_op jit(solution)/shard_map/gather1_e1/ppermute | solution.py:227
  55.4 33.0 %collective-permute-start.14 = (bf16[2,256,512]{2,1,0:T(8,128)(2,1)S(1)}, bf16[2,256,512]{2,1,0:T(8,128)(2,1)S(1)}, u32[]{:S(2)}, u32[]{:S(2)}) collective-permute-start(bf16[2,256,512]{2,1,0:T(8,128)(2,1)S(1)} %get-tuple-element.91.refs_0_), channel_id=1, source_target_pairs={{0,6},{1,7},{6,0},{7,1},{2,3},{3,2},{4,5},{5,4},{8,14},{9,15},{14,... | collective-permute-start | bytes 1572872 | tf_op jit(solution)/shard_map/gather1_across/ppermute | solution.py:227
  58.1 30.4 %collective-permute-start.15 = (bf16[2,256,512]{2,1,0:T(8,128)(2,1)S(1)}, bf16[2,256,512]{2,1,0:T(8,128)(2,1)S(1)}, u32[]{:S(2)}, u32[]{:S(2)}) collective-permute-start(bf16[2,256,512]{2,1,0:T(8,128)(2,1)S(1)} %get-tuple-element.91.refs_0_), channel_id=1, source_target_pairs={{0,4},{1,5},{6,2},{7,3},{8,12},{9,13},{14,10},{15,11},{16,20},{17,... | collective-permute-start | bytes 1572872 | tf_op jit(solution)/shard_map/gather1_skip/ppermute | solution.py:227
  59.4 29.1 %collective-permute-start.13 = (bf16[2,256,512]{2,1,0:T(8,128)(2,1)S(1)}, bf16[2,256,512]{2,1,0:T(8,128)(2,1)S(1)}, u32[]{:S(2)}, u32[]{:S(2)}) collective-permute-start(bf16[2,256,512]{2,1,0:T(8,128)(2,1)S(1)} %collective-permute-done.9.refs_2_), channel_id=1, source_target_pairs={{2,0},{3,1},{4,6},{5,7},{10,8},{11,9},{12,14},{13,15},{18,16},{19,... | collective-permute-start | bytes 1572872 | tf_op jit(solution)/shard_map/gather1_e2/ppermute | solution.py:227
  79.3 18.9 %copy-start.23 = (bf16[2,256,512]{2,1,0:T(8,128)(2,1)}, bf16[2,256,512]{2,1,0:T(8,128)(2,1)S(1)}, u32[]{:S(2)}) copy-start(bf16[2,256,512]{2,1,0:T(8,128)(2,1)S(1)} %collective-permute-done.12.refs_1_) | copy-start | bytes 1572868
  89.7 28.4 %copy-start.6 = (bf16[2,32,4096]{2,1,0:T(8,128)(2,1)S(1)}, bf16[2,32,4096]{2,1,0:T(8,128)(2,1)}, u32[]{:S(2)}) copy-start(bf16[2,32,4096]{2,1,0:T(8,128)(2,1)} %get-tuple-element.118) | copy-start | bytes 1572868
  89.7 28.5 %copy-start.4 = (bf16[64,4096]{1,0:T(8,128)(2,1)S(1)}, bf16[64,4096]{1,0:T(8,128)(2,1)}, u32[]{:S(2)}) copy-start(bf16[64,4096]{1,0:T(8,128)(2,1)} %get-tuple-element.104) | copy-start | bytes 1572868
  89.7 28.5 %collective-permute-start.18 = (bf16[64,4096]{1,0:T(8,128)(2,1)}, bf16[64,4096]{1,0:T(8,128)(2,1)S(1)}, u32[]{:S(2)}, u32[]{:S(2)}) collective-permute-start(bf16[64,4096]{1,0:T(8,128)(2,1)} %get-tuple-element.107), channel_id=1, source_target_pairs={{0,6},{1,7},{6,0},{7,1},{2,3},{3,2},{4,5},{5,4},{8,14},{9,15},{14,... | collective-permute-start | bytes 1572872 | tf_op jit(solution)/shard_map/sum0_across/ppermute | solution.py:227
  92.3 25.9 %collective-permute-start.19 = (bf16[64,4096]{1,0:T(8,128)(2,1)}, bf16[64,4096]{1,0:T(8,128)(2,1)S(1)}, u32[]{:S(2)}, u32[]{:S(2)}) collective-permute-start(bf16[64,4096]{1,0:T(8,128)(2,1)} %get-tuple-element.107), channel_id=1, source_target_pairs={{4,0},{5,1},{2,6},{3,7},{12,8},{13,9},{10,14},{11,15},{20,16},{21,... | collective-permute-start | bytes 1572872 | tf_op jit(solution)/shard_map/sum0_skip/ppermute | solution.py:227
  93.6 24.6 %collective-permute-start.17 = (bf16[64,4096]{1,0:T(8,128)(2,1)}, bf16[64,4096]{1,0:T(8,128)(2,1)S(1)}, u32[]{:S(2)}, u32[]{:S(2)}) collective-permute-start(bf16[64,4096]{1,0:T(8,128)(2,1)} %get-tuple-element.104), channel_id=1, source_target_pairs={{0,2},{1,3},{6,4},{7,5},{8,10},{9,11},{14,12},{15,13},{16,18},{17,... | collective-permute-start | bytes 1572872 | tf_op jit(solution)/shard_map/sum0_mid_in/ppermute | solution.py:227
  116.7 10.9 %collective-permute-start.16 = (bf16[64,4096]{1,0:T(8,128)(2,1)}, bf16[64,4096]{1,0:T(8,128)(2,1)S(1)}, u32[]{:S(2)}, u32[]{:S(2)}) collective-permute-start(bf16[64,4096]{1,0:T(8,128)(2,1)} %get-tuple-element.103), channel_id=1, source_target_pairs={{0,2},{1,3},{6,4},{7,5},{8,10},{9,11},{14,12},{15,13},{16,18},{17,... | collective-permute-start | bytes 1572872 | tf_op jit(solution)/shard_map/sum1_far_in/ppermute | solution.py:227
  118.2 9.3 %copy-start.3 = (bf16[64,4096]{1,0:T(8,128)(2,1)S(1)}, bf16[64,4096]{1,0:T(8,128)(2,1)}, u32[]{:S(2)}) copy-start(bf16[64,4096]{1,0:T(8,128)(2,1)} %get-tuple-element.116) | copy-start | bytes 1572868
  118.3 13.7 %copy-start.5 = (bf16[64,4096]{1,0:T(8,128)(2,1)S(1)}, bf16[64,4096]{1,0:T(8,128)(2,1)}, u32[]{:S(2)}) copy-start(bf16[64,4096]{1,0:T(8,128)(2,1)} %get-tuple-element.103) | copy-start | bytes 1572868
  118.4 9.2 %collective-permute-start.20 = (bf16[64,4096]{1,0:T(8,128)(2,1)S(1)}, bf16[64,4096]{1,0:T(8,128)(2,1)S(1)}, u32[]{:S(2)}, u32[]{:S(2)}) collective-permute-start(bf16[64,4096]{1,0:T(8,128)(2,1)S(1)} %add_convert_fusion.5), channel_id=1, source_target_pairs={{2,4},{3,5},{4,2},{5,3},{0,1},{1,0},{6,7},{7,6},{10,12},{11,13},{1... | collective-permute-start | bytes 1572872 | tf_op jit(solution)/shard_map/sum0_mid_on/ppermute | solution.py:227
  119.2 13.0 %collective-permute-start.25 = (bf16[64,4096]{1,0:T(8,128)(2,1)S(1)}, bf16[64,4096]{1,0:T(8,128)(2,1)S(1)}, u32[]{:S(2)}, u32[]{:S(2)}) collective-permute-start(bf16[64,4096]{1,0:T(8,128)(2,1)S(1)} %get-tuple-element.126), channel_id=1, source_target_pairs={{0,1},{1,0},{2,3},{3,2},{4,5},{5,4},{6,7},{7,6},{8,9},{9,8},{10,11... | collective-permute-start | bytes 1572872 | tf_op jit(solution)/shard_map/swap_commit/ppermute | solution.py:227
  127.6 16.8 %copy-start.12 = (bf16[64,4096]{1,0:T(8,128)(2,1)}, bf16[64,4096]{1,0:T(8,128)(2,1)S(1)}, u32[]{:S(2)}) copy-start(bf16[64,4096]{1,0:T(8,128)(2,1)S(1)} %collective-permute-done.20) | copy-start | bytes 1572868
  127.6 16.7 %collective-permute-start.24 = (bf16[64,4096]{1,0:T(8,128)(2,1)S(1)}, bf16[64,4096]{1,0:T(8,128)(2,1)S(1)}, u32[]{:S(2)}, u32[]{:S(2)}) collective-permute-start(bf16[64,4096]{1,0:T(8,128)(2,1)S(1)} %copy-done.3), channel_id=1, source_target_pairs={{0,2},{1,3},{6,4},{7,5},{8,10},{9,11},{14,12},{15,13},{16,18},{17,... | collective-permute-start | bytes 1572872 | tf_op jit(solution)/shard_map/sum1_mid_in/ppermute | solution.py:227
  131.9 23.7 %collective-permute-start.21 = (bf16[64,4096]{1,0:T(8,128)(2,1)}, bf16[64,4096]{1,0:T(8,128)(2,1)}, u32[]{:S(2)}, u32[]{:S(2)}) collective-permute-start(bf16[64,4096]{1,0:T(8,128)(2,1)} %get-tuple-element.109), channel_id=1, source_target_pairs={{0,2},{1,3},{2,0},{3,1},{4,6},{5,7},{6,4},{7,5},{8,10},{9,11},{10,... | collective-permute-start | bytes 1572872 | tf_op jit(solution)/shard_map/sum0_near/ppermute | solution.py:227
  132.1 16.1 %collective-permute-start.22 = (bf16[64,4096]{1,0:T(8,128)(2,1)S(1)}, bf16[64,4096]{1,0:T(8,128)(2,1)}, u32[]{:S(2)}, u32[]{:S(2)}) collective-permute-start(bf16[64,4096]{1,0:T(8,128)(2,1)S(1)} %add_convert_fusion.3), channel_id=1, source_target_pairs={{2,4},{3,5},{4,2},{5,3},{0,1},{1,0},{6,7},{7,6},{10,12},{11,13},{1... | collective-permute-start | bytes 1572872 | tf_op jit(solution)/shard_map/sum1_far_on/ppermute | solution.py:227
  144.4 11.2 %copy-start.1 = (f32[64,4096]{1,0:T(8,128)S(1)}, f32[64,4096]{1,0:T(8,128)}, u32[]{:S(2)}) copy-start(f32[64,4096]{1,0:T(8,128)} %get-tuple-element.89) | copy-start | bytes 3145732
  144.4 19.5 %all-to-all-start.1 = ((bf16[4,32,4096]{2,1,0:T(8,128)(2,1)}), bf16[4,32,4096]{2,1,0:T(8,128)(2,1)S(1)}, u32[]{:S(2)}, u32[]{:S(2)}) async-start(bf16[4,32,4096]{2,1,0:T(8,128)(2,1)} %bitcast.44), calls=%async_computation.1 | async-start | bytes 2097152 | tf_op jit(solution)/shard_map/all_to_all | solution.py:391
  149.4 13.1 %copy-start = (f32[64,4096]{1,0:T(8,128)S(1)}, f32[64,4096]{1,0:T(8,128)}, u32[]{:S(2)}) copy-start(f32[64,4096]{1,0:T(8,128)} %get-tuple-element.113) | copy-start | bytes 3145732
  149.4 13.1 %collective-permute-start.23 = (bf16[64,4096]{1,0:T(8,128)(2,1)S(1)}, bf16[64,4096]{1,0:T(8,128)(2,1)S(1)}, u32[]{:S(2)}, u32[]{:S(2)}) collective-permute-start(bf16[64,4096]{1,0:T(8,128)(2,1)S(1)} %add_convert_fusion.2), channel_id=1, source_target_pairs={{0,2},{1,3},{2,0},{3,1},{4,6},{5,7},{6,4},{7,5},{8,10},{9,11},{10,... | collective-permute-start | bytes 1572872 | tf_op jit(solution)/shard_map/sum1_near/ppermute | solution.py:227
  152.1 10.4 %collective-permute-start.26 = (bf16[64,4096]{1,0:T(8,128)(2,1)S(1)}, bf16[64,4096]{1,0:T(8,128)(2,1)S(1)}, u32[]{:S(2)}, u32[]{:S(2)}) collective-permute-start(bf16[64,4096]{1,0:T(8,128)(2,1)S(1)} %add_convert_fusion.1), channel_id=1, source_target_pairs={{2,4},{3,5},{4,2},{5,3},{0,1},{1,0},{6,7},{7,6},{10,12},{11,13},{1... | collective-permute-start | bytes 1572872 | tf_op jit(solution)/shard_map/sum1_mid_on/ppermute | solution.py:227
  (8 other events, 14.2 us)
